TPU v7x, 1024 devices: a whole 8x8x8 slice. The times are simulated.
1024 devices in a mesh: row: 32 (over y_lo, x), col: 32 (over y_hi, z, core).
Axes of the slice: x: 8, y: 8 (y_hi: 2, y_lo: 4; y = y_hi * 4 + y_lo), z: 8, core: 2. Of those that a mesh axis runs over, the one named last changes fastest.
Arguments:
- amplitudes: bfloat16 [12288, 32768], P(('row', 'col')), may hold values from -12 to 12
- integrals: bfloat16 [32768, 2048], P(('row', 'col')), may hold values from -0.03125 to 0.03125
- pair_list: int32 [12288, 2], P(('row', 'col')), may hold values from 0 to 199
- block_sizes: int32 [8], replicated, may hold values from 104 to 128, as said below
- occ_energy: float32 [200], replicated, may hold values from -2 to -0.4
- virt_energy: float32 [128], replicated, may hold values from 0.3 to 2
Outputs:
- update: float32 [12288, 2048], P(('row', 'col'))
Inputs may be any that keep to these rules, and one draw needn't show every extreme that they name: `block_sizes`: the entries sum to 1000; entries 0, 1 and 7 are below 128, and at least one other entry equals 128.
All inputs are finite; a program needn't handle non-finite values.
Results may differ from a plain program's by a relative error of at most 0.0003.
Values may be sent and summed in bfloat16 or wider, within the bound.
No kernel may reach another device: no remote copies, remote signals or barrier semaphores. Data moves between devices by JAX's collectives and lax.ppermute only.
A program may use at most 32 MiB of HBM per device.

v0:
```python
import jax
import jax.numpy as jnp
from jax import lax
from jax.sharding import PartitionSpec as P

NIRREP = 8
NV = 128


def make_adder(columns, incoming):
    return jnp.dot(columns, incoming, preferred_element_type=jnp.float32)


def table_lookup(indices, table, table_length):
    matches = indices[..., None] == jnp.arange(table_length, dtype=jnp.int32)
    return jnp.sum(jnp.where(matches, table, jnp.zeros((), table.dtype)), axis=-1)


def local(amplitudes, integrals, pair_list, block_sizes, occ_energy, virt_energy):
    row_count = lax.axis_size("row")
    column_count = lax.axis_size("col")
    pairs_local = amplitudes.shape[0]
    slab_rows = integrals.shape[0]
    out_width = integrals.shape[1]
    shard_index = lax.axis_index("row") * column_count + lax.axis_index("col")
    pair_index = shard_index * slab_rows + jnp.arange(slab_rows, dtype=jnp.int32)
    irrep_index = pair_index // (NV * NV)
    first_virt = pair_index // NV % NV
    second_virt = pair_index % NV
    size_here = table_lookup(irrep_index, block_sizes, NIRREP)
    live_rows = (first_virt < size_here) & (second_virt < size_here)
    masked_panel = jnp.where(live_rows[:, None], integrals, jnp.zeros((), jnp.bfloat16))
    blocked = amplitudes.reshape(pairs_local, row_count, column_count, slab_rows)
    exchanged = lax.all_to_all(blocked, "col", split_axis=2, concat_axis=0, tiled=True)
    columns = exchanged.reshape(exchanged.shape[0], row_count * slab_rows)
    partial_value = make_adder(columns, lax.all_gather(masked_panel, "row", axis=0, tiled=True))
    ladder = lax.psum_scatter(partial_value, "col", scatter_dimension=0, tiled=True)
    pair_energy = jnp.sum(table_lookup(pair_list, occ_energy, occ_energy.shape[0]), axis=1)
    out_index = jnp.arange(out_width, dtype=jnp.int32)
    outer_virt = out_index // NV
    inner_virt = out_index % NV
    outer_energy = table_lookup(outer_virt, virt_energy, NV)
    inner_energy = table_lookup(inner_virt, virt_energy, NV)
    denominator = pair_energy[:, None] - outer_energy[None, :] - inner_energy[None, :]
    live_column = inner_virt < block_sizes[NIRREP - 1]
    return jnp.where(live_column[None, :], ladder / denominator, jnp.float32(0.0))


def solution(mesh):
    in_specs = (
        P(("row", "col"), None),
        P(("row", "col"), None),
        P(("row", "col"), None),
        P(),
        P(),
        P(),
    )
    out_specs = P(("row", "col"), None)
    return jax.shard_map(local, mesh=mesh, in_specs=in_specs, out_specs=out_specs, check_vma=False)
```

profile of v0, /device:TPU:1, one launch (start us, length us, event | category | flops | bytes accessed | tf_op | source)
XLA Modules:
  0.0 560.1 jit_solution(17202576277084582026)
XLA Ops:
  6.5 0.7 select_reduce_fusion.2
  7.3 1.6 broadcast_select_fusion
  9.0 0.0 all-gather.2.cloned.1.call-update
  9.0 0.0 all-reduce.3.cloned.1.call-start
  9.0 3.6 reshape.101
  12.6 2.9 copy.21
  15.5 5.1 reshape.106
  20.6 53.8 %all_to_all.15 = bf16[32,2,6144]{2,1,0:T(2,128)(2,1)} all-to-all(bf16[32,2,6144]{2,1,0:T(2,128)(2,1)S(1)} %reshape.106), channel_id=1, replica_groups=mesh['row'=32,'col'=32] {'col'}, dimensions={0} | all-to-all | bytes 1572864 | tf_op jit(solution)/shard_map/all_to_all | solution.py:34
  74.3 4.0 reshape.107
  78.3 2.2 bitcast_bitcast_fusion
  80.6 4.8 reshape.102
  85.4 80.1 %all-gather.2.cloned.1.call-done = bf16[1024,2048]{1,0:T(8,128)(2,1)} async-done(((bf16[32,2048]{1,0:T(8,128)(2,1)}), bf16[1024,2048]{1,0:T(8,128)(2,1)}) %all-gather.2.cloned.1.call-update) | async-done | bytes 4194320 | tf_op jit(solution)/shard_map/all_gather | solution.py:36
  165.5 6.3 %convolution_bitcast_fusion = f32[384,2048]{0,1:T(8,128)} fusion(bf16[1024,2048]{1,0:T(8,128)(2,1)} %all-gather.2.cloned.1.call-done, bf16[384,1024]{1,0:T(8,128)(2,1)S(1)} %reshape.102), kind=kOutput, calls=%fused_computation | convolution fusion | flops 1610612736 | bytes 8126464 | tf_op jit(solution)/shard_map/dot_general | solution.py:11
  171.8 0.0 all-reduce.3.cloned.1.call-update
  171.8 0.6 copy-done.3
  172.4 0.5 slice.3
  172.9 0.1 copy.16
  173.0 1.3 dynamic-slice
  175.0 0.5 broadcast_compare_fusion
  175.5 0.3 fusion.1
  175.8 1.3 select_reduce_fusion.1
  177.1 371.8 %all-reduce.3.cloned.1.call-done = f32[384,2048]{0,1:T(8,128)} async-done(((f32[384,2048]{0,1:T(8,128)}), f32[384,2048]{0,1:T(8,128)}) %all-reduce.3.cloned.1.call-update) | async-done | bytes 3145744
  548.9 3.3 fusion
  552.2 1.0 copy.17
  (11 shorter events, 0.1 us)
Async XLA Ops:
  6.5 158.9 %all-gather.2.cloned.1.call-start = ((), (), s32[]{:S(2)}) async-start(), calls=%async_computation.1 | async-start | bytes 4325376 | tf_op jit(solution)/shard_map/all_gather | solution.py:36
  9.0 539.9 %all-reduce.3.cloned.1.call-start = ((), (), s32[]{:S(2)}) async-start(), calls=%async_computation.2 | async-start | bytes 6291456
  171.7 0.7 copy-start.3
  171.7 1.2 copy-start
  171.7 3.8 copy-start.1
  171.7 4.1 copy-start.2
Sparse Core Ops, SparseCore 0:
  10.0 155.4 all-gather.1
  171.9 376.9 all-reduce.2
where the time goes:
time: 561 us; the launch traced here: 560 us
  waiting for transfers between devices  452 us (81%)
  blocking collectives  53.8 us (10%)
  local copies, waits for them, and re-layouts  26.1 us (5%)
  between operations  14.1 us (3%)
  other arithmetic  7.85 us (1%)
  matrix products  6.26 us (1%)
    unnamed x3, waiting for transfers between devices  372 us
    all_gather x1, waiting for transfers between devices, local(): lax.all_gather(masked_panel, 'row', axis=0, tiled=True)  80.1 us
    all_to_all x1, blocking collectives, local(): lax.all_to_all(blocked, 'col', split_axis=2, concat_axis=0, tiled=True)  53.8 us
  transfers between devices with their start and end apart: 2, of which 2 were waited for; matrix products, arithmetic and copies ran while one was open for 5% of the time, Pallas kernels for 0%

commit v1 on v0

v1 whole, which is shorter than its diff:
```python
import jax
import jax.numpy as jnp
from jax import lax
from jax.sharding import Mesh, PartitionSpec as P

NIRREP = 8
NV = 128
AXES = ("ylo", "x", "yhi", "z", "core")
PLANE = ("yhi", "ylo", "x")


def table_lookup(indices, table, table_length):
    matches = indices[..., None] == jnp.arange(table_length, dtype=jnp.int32)
    return jnp.sum(jnp.where(matches, table, jnp.zeros((), table.dtype)), axis=-1)


def local(amplitudes, integrals, pair_list, block_sizes, occ_energy, virt_energy):
    size = {axis: lax.axis_size(axis) for axis in AXES}
    pairs_local, summed = amplitudes.shape
    slab_rows, out_width = integrals.shape
    half = out_width // size["core"]

    halves = integrals.reshape(slab_rows, size["core"], half).transpose(1, 0, 2)
    swapped = lax.all_to_all(halves, "core", split_axis=0, concat_axis=0, tiled=True)
    panel = lax.all_gather(
        swapped.reshape(size["core"] * slab_rows, half), PLANE, axis=0, tiled=True
    )

    pair_index = jnp.arange(summed, dtype=jnp.int32)
    size_here = jnp.where(pair_index < NV * NV, block_sizes[0], block_sizes[1])
    live = (pair_index // NV % NV < size_here) & (pair_index % NV < size_here)
    masked = jnp.where(live[None, :], amplitudes, jnp.zeros((), jnp.bfloat16))
    blocked = masked.reshape(
        pairs_local, size["ylo"], size["x"], size["yhi"], size["z"], size["core"] * slab_rows
    ).transpose(4, 0, 3, 1, 2, 5)
    blocked = blocked.reshape(size["z"], pairs_local, summed // size["z"])
    columns = lax.all_to_all(blocked, "z", split_axis=0, concat_axis=0, tiled=True)
    both = lax.all_gather(columns, "core", axis=1, tiled=True)
    lhs = both.reshape(size["z"] * size["core"] * pairs_local, summed // size["z"])

    partial_value = jnp.dot(lhs, panel, preferred_element_type=jnp.float32)
    partial_value = partial_value.reshape(size["z"], size["core"] * pairs_local, half)
    reduced = lax.psum_scatter(partial_value, "z", scatter_dimension=0, tiled=False)
    reduced = reduced.reshape(size["core"], pairs_local, half)
    joined = lax.all_to_all(reduced, "core", split_axis=0, concat_axis=0, tiled=True)
    ladder = joined.transpose(1, 0, 2).reshape(pairs_local, out_width)

    pair_energy = jnp.sum(table_lookup(pair_list, occ_energy, occ_energy.shape[0]), axis=1)
    out_index = jnp.arange(out_width, dtype=jnp.int32)
    outer_virt = out_index // NV
    inner_virt = out_index % NV
    outer_energy = table_lookup(outer_virt, virt_energy, NV)
    inner_energy = table_lookup(inner_virt, virt_energy, NV)
    denominator = pair_energy[:, None] - outer_energy[None, :] - inner_energy[None, :]
    live_column = inner_virt < block_sizes[NIRREP - 1]
    return jnp.where(live_column[None, :], ladder / denominator, jnp.float32(0.0))


def solution(mesh):
    fine = Mesh(mesh.devices.reshape(4, 8, 2, 8, 2), AXES)
    split = P(AXES, None)
    return jax.shard_map(
        local,
        mesh=fine,
        in_specs=(split, split, split, P(), P(), P()),
        out_specs=split,
        check_vma=False,
    )
```

time: 561 us -> 255 us (0.45)
  waiting for transfers between devices: 452 us -> 161 us
  local copies, waits for them, and re-layouts: 26.1 us -> 7.65 us
  blocking collectives: 53.8 us -> 59.5 us
    unnamed x3, waiting for transfers between devices: 372 us -> 0.05 us
    all_gather x1 -> x2, waiting for transfers between devices: 80.1 us -> 122 us  [the longest x1 107 us: local(): lax.all_gather(swapped.reshape(size['core'] * slab_rows, half), PLANE, ax...]
    reduce_scatter x0 -> x1, waiting for transfers between devices: none -> 38.3 us  [local(): lax.psum_scatter(partial_value, 'z', scatter_dimension=0, tiled=False)]
    unnamed x12 -> x11, local copies, waits for them, and re-layouts: 11.1 us -> 0.2 us
    reshape x3 -> x5, local copies, waits for them, and re-layouts: 11.3 us -> 3.77 us  [the longest x2 1.99 us: local(): masked.reshape(pairs_local, size['ylo'], size['x'], size['yhi'], size['z'...]
    all_to_all x1 -> x3, blocking collectives: 53.8 us -> 59.5 us  [the longest x1 44.3 us: local(): lax.all_to_all(blocked, 'z', split_axis=0, concat_axis=0, tiled=True)]
  transfers between devices with their start and end apart: 2 -> 3, of which waited for: 2 -> 3; matrix products, arithmetic and copies ran while one was open for 5% -> 1% of each run, Pallas kernels for 0% -> 0%
where the time goes in v1:
time: 255 us
  waiting for transfers between devices  161 us (63%)
  blocking collectives  59.5 us (23%)
  between operations  13.2 us (5%)
  matrix products  7.74 us (3%)
  local copies, waits for them, and re-layouts  7.65 us (3%)
  other arithmetic  5.58 us (2%)
    all_gather x1, waiting for transfers between devices, local(): lax.all_gather(swapped.reshape(size['core'] * slab_rows, half), PLANE, ax...  107 us
    all_to_all x1, blocking collectives, local(): lax.all_to_all(blocked, 'z', split_axis=0, concat_axis=0, tiled=True)  44.3 us
    reduce_scatter x1, waiting for transfers between devices, local(): lax.psum_scatter(partial_value, 'z', scatter_dimension=0, tiled=False)  38.3 us
    all_gather x1, waiting for transfers between devices, local(): both = lax.all_gather(columns, 'core', axis=1, tiled=True)  15 us
    all_to_all x1, blocking collectives, local(): lax.all_to_all(reduced, 'core', split_axis=0, concat_axis=0, tiled=True)  8.56 us
    dot_general x1, matrix products, local(): partial_value = jnp.dot(lhs, panel, preferred_element_type=jnp.float32)  7.74 us
    all_to_all x1, blocking collectives, local(): lax.all_to_all(halves, 'core', split_axis=0, concat_axis=0, tiled=True)  6.65 us
  transfers between devices with their start and end apart: 3, of which 3 were waited for; matrix products, arithmetic and copies ran while one was open for 1% of the time, Pallas kernels for 0%

profile of v1, /device:TPU:1, one launch (start us, length us, event | category | flops | bytes accessed | tf_op | source)
XLA Modules:
  0.0 254.7 jit_solution(16409833902298928338)
XLA Ops:
  6.5 1.4 fusion.18
  7.9 1.2 fusion.11
  9.1 1.4 broadcast_select_fusion
  10.5 1.6 reshape.92
  12.1 0.4 copy.45
  12.5 1.3 reshape.93
  13.9 0.5 copy.33
  14.3 44.3 %all_to_all.15 = bf16[8,12,4096]{2,1,0:T(8,128)(2,1)S(1)} all-to-all(bf16[8,12,4096]{2,1,0:T(8,128)(2,1)S(1)} %copy.33), channel_id=1, replica_groups=mesh['ylo'=4,'x'=8,'yhi'=2,'z'=8,'core'=2] {'z'}, dimensions={0} | all-to-all | bytes 1572864 | tf_op jit(solution)/shard_map/all_to_all | solution.py:37
  58.6 1.3 copy.34
  60.0 0.0 all-gather.5.cloned.1.call-start
  60.0 6.7 %all_to_all.16 = bf16[2,32,1024]{2,1,0:T(8,128)(2,1)} all-to-all(bf16[2,32,1024]{2,1,0:T(8,128)(2,1)S(1)} %bitcast.30), channel_id=1, replica_groups=mesh['ylo'=4,'x'=8,'yhi'=2,'z'=8,'core'=2] {'core'}, dimensions={0} | all-to-all | bytes 262144 | tf_op jit(solution)/shard_map/all_to_all | solution.py:24
  66.7 0.0 reduce-scatter.2.cloned.1.call-start
  66.8 15.0 %all-gather.3.cloned.1.call-done = bf16[8,24,4096]{2,0,1:T(8,128)(2,1)} async-done(((bf16[8,12,4096]{2,0,1:T(8,128)(2,1)}), bf16[8,24,4096]{2,0,1:T(8,128)(2,1)}) %all-gather.3.cloned.1.call-update) | async-done | bytes 1572880 | tf_op jit(solution)/shard_map/all_gather | solution.py:38
  81.8 107.4 %all-gather.5.cloned.1.call-done = bf16[4096,1024]{1,0:T(8,128)(2,1)} async-done(((bf16[64,1024]{1,0:T(8,128)(2,1)}), bf16[4096,1024]{1,0:T(8,128)(2,1)}) %all-gather.5.cloned.1.call-update) | async-done | bytes 8388624 | tf_op jit(solution)/shard_map/all_gather | solution.py:25
  189.3 7.7 %fusion = f32[8,24,1024]{2,1,0:T(8,128)} fusion(bf16[4096,1024]{1,0:T(8,128)(2,1)} %all-gather.5.cloned.1.call-done, bf16[8,24,4096]{2,0,1:T(8,128)(2,1)} %all-gather.3.cloned.1.call-done), kind=kOutput, calls=%fused_computation | convolution fusion | flops 1610612736 | bytes 10747904 | tf_op jit(solution)/shard_map/dot_general | solution.py:41
  197.1 0.1 copy.38
  197.2 0.7 broadcast_compare_fusion
  197.8 0.3 fusion.12
  198.1 1.3 select_reduce_fusion.1
  199.4 38.3 %reduce-scatter.2.cloned.1.call-done = f32[1,24,1024]{2,1,0:T(8,128)} async-done(((f32[8,24,1024]{2,1,0:T(8,128)}), f32[1,24,1024]{2,1,0:T(8,128)}) %reduce-scatter.2.cloned.1.call-update) | async-done | bytes 98320 | tf_op jit(solution)/shard_map/reduce_scatter | solution.py:43
  237.7 0.9 reshape_reduce_scatter.3
  238.6 8.6 %all_to_all.17 = f32[2,12,1024]{2,1,0:T(8,128)S(1)} all-to-all(f32[2,12,1024]{2,1,0:T(8,128)S(1)} %reshape_reduce_scatter.3), channel_id=1, replica_groups=mesh['ylo'=4,'x'=8,'yhi'=2,'z'=8,'core'=2] {'core'}, dimensions={0} | all-to-all | bytes 196608 | tf_op jit(solution)/shard_map/all_to_all | solution.py:45
  247.2 0.1 copy.37
  247.4 0.8 divide_select_fusion
  (16 shorter events, 0.2 us)
Async XLA Ops:
  6.5 75.3 %all-gather.3.cloned.1.call-start = ((), (), s32[]{:S(2)}) async-start(), calls=%async_computation.4 | async-start | bytes 2359296 | tf_op jit(solution)/shard_map/all_gather | solution.py:38
  58.6 1.4 copy-start
  60.0 129.3 %all-gather.5.cloned.1.call-start = ((), (), s32[]{:S(2)}) async-start(), calls=%async_computation.5 | async-start | bytes 8519680 | tf_op jit(solution)/shard_map/all_gather | solution.py:25
  66.7 130.3 %copy-start.1 = (s32[12,2]{0,1:T(2,128)S(1)}, s32[12,2]{0,1:T(2,128)}, u32[]{:S(2)}) copy-start(s32[12,2]{0,1:T(2,128)} %param.8) | copy-start | bytes 292
  66.7 131.1 %copy-start.2 = (f32[200]{0:T(256)S(1)}, f32[200]{0:T(256)}, u32[]{:S(2)}) copy-start(f32[200]{0:T(256)} %param.10) | copy-start | bytes 2404
  66.7 131.4 %copy-start.3 = (f32[128]{0:T(128)S(1)}, f32[128]{0:T(128)}, u32[]{:S(2)}) copy-start(f32[128]{0:T(128)} %param.11) | copy-start | bytes 1540
  66.7 171.0 %reduce-scatter.2.cloned.1.call-start = ((), (), s32[]{:S(2)}) async-start(), calls=%async_computation.6 | async-start | bytes 884736 | tf_op jit(solution)/shard_map/reduce_scatter | solution.py:43
Sparse Core Ops, SparseCore 0:
  60.1 21.7 all-gather.2
  86.1 103.1 all-gather.4
  197.2 40.5 reduce-scatter.1

commit v2 on v1

v2 whole, which is shorter than its diff:
```python
import jax
import jax.numpy as jnp
from jax import lax
from jax.sharding import Mesh, PartitionSpec as P

NIRREP = 8
NV = 128
AXES = ("ylo", "x", "yhi", "zhi", "zlo", "core")
RING = ("yhi", "ylo")
SWAP = [(0, 1), (1, 0)]


def table_lookup(indices, table, table_length):
    matches = indices[..., None] == jnp.arange(table_length, dtype=jnp.int32)
    return jnp.sum(jnp.where(matches, table, jnp.zeros((), table.dtype)), axis=-1)


def local(amplitudes, integrals, pair_list, block_sizes, occ_energy, virt_energy):
    size = {axis: lax.axis_size(axis) for axis in AXES}
    pairs_local, summed = amplitudes.shape
    slab_rows, out_width = integrals.shape
    parts = size["zlo"] * size["core"]
    quarter = out_width // parts
    stripe = size["zhi"] * size["zlo"] * size["core"] * slab_rows

    quarters = integrals.reshape(slab_rows, parts, quarter).transpose(1, 0, 2)
    quarters = jnp.tile(quarters, (size["zhi"], 1, 1))
    rows = lax.all_to_all(quarters, ("zhi", "zlo", "core"), split_axis=0, concat_axis=0, tiled=True)
    panel = lax.all_gather(rows.reshape(stripe, quarter), RING, axis=0, tiled=True)

    pair_index = jnp.arange(summed, dtype=jnp.int32)
    size_here = jnp.where(pair_index < NV * NV, block_sizes[0], block_sizes[1])
    live = (pair_index // NV % NV < size_here) & (pair_index % NV < size_here)
    masked = jnp.where(live[None, :], amplitudes, jnp.zeros((), jnp.bfloat16))
    blocked = masked.reshape(pairs_local, size["ylo"], size["x"], size["yhi"], stripe)
    blocked = blocked.transpose(2, 3, 0, 1, 4)
    blocked = blocked.reshape(size["x"], 1, size["yhi"] * pairs_local, size["ylo"] * stripe)
    blocked = jnp.tile(blocked, (1, size["zlo"], 1, 1))
    groups = size["x"] * size["zlo"]
    blocked = blocked.reshape(groups, size["yhi"] * pairs_local, size["ylo"] * stripe)
    own = lax.all_to_all(blocked, ("x", "zlo"), split_axis=0, concat_axis=0, tiled=True)
    other = lax.ppermute(own, "core", SWAP)
    lhs = jnp.stack([own, other], axis=1)
    lhs = lhs.reshape(groups, size["core"], size["yhi"], pairs_local, size["ylo"] * stripe)
    lhs = lhs.transpose(0, 1, 3, 2, 4).reshape(groups * size["core"] * pairs_local, -1)

    partial_value = jnp.dot(lhs, panel, preferred_element_type=jnp.float32)
    partial_value = partial_value.reshape(groups, size["core"] * pairs_local, quarter)
    pieces = lax.all_to_all(partial_value, ("x", "zlo"), split_axis=0, concat_axis=0, tiled=True)
    pieces = pieces.reshape(size["x"], size["zlo"], size["core"], pairs_local, quarter)
    reduced = jnp.sum(pieces, axis=0)
    mine, theirs = reduced[:, 0], reduced[:, 1]
    arrived = lax.ppermute(theirs, "core", SWAP)
    first = lax.axis_index("core") == 0
    low = jnp.where(first, mine, arrived)
    high = jnp.where(first, arrived, mine)
    ladder = jnp.stack([low, high], axis=1).reshape(parts, pairs_local, quarter)
    ladder = ladder.transpose(1, 0, 2).reshape(pairs_local, out_width)

    pair_energy = jnp.sum(table_lookup(pair_list, occ_energy, occ_energy.shape[0]), axis=1)
    out_index = jnp.arange(out_width, dtype=jnp.int32)
    outer_virt = out_index // NV
    inner_virt = out_index % NV
    outer_energy = table_lookup(outer_virt, virt_energy, NV)
    inner_energy = table_lookup(inner_virt, virt_energy, NV)
    denominator = pair_energy[:, None] - outer_energy[None, :] - inner_energy[None, :]
    live_column = inner_virt < block_sizes[NIRREP - 1]
    return jnp.where(live_column[None, :], ladder / denominator, jnp.float32(0.0))


def solution(mesh):
    fine = Mesh(mesh.devices.reshape(4, 8, 2, 4, 2, 2), AXES)
    split = P(AXES, None)
    return jax.shard_map(
        local,
        mesh=fine,
        in_specs=(split, split, split, P(), P(), P()),
        out_specs=split,
        check_vma=False,
    )
```

time: 255 us -> 153 us (0.60)
  waiting for transfers between devices: 161 us -> 37.8 us
  starting transfers between devices: 0.09 us -> 28.7 us
  blocking collectives: 59.5 us -> 46.6 us
  local copies, waits for them, and re-layouts: 7.65 us -> 15.6 us
    all_gather x2 -> x1, waiting for transfers between devices: 122 us -> 0.01 us  [local(): lax.all_gather(rows.reshape(stripe, quarter), RING, axis=0, tiled=True)]
    reduce_scatter x1 -> x0, waiting for transfers between devices: 38.3 us -> none  [local(): lax.psum_scatter(partial_value, 'z', scatter_dimension=0, tiled=False)]
    all_to_all x0 -> x2, waiting for transfers between devices: none -> 34.2 us  [the longest x1 19.6 us: local(): lax.all_to_all(partial_value, ('x', 'zlo'), split_axis=0, concat_axis=0,...]
    all_to_all x0 -> x2, starting transfers between devices: none -> 21.8 us  [the longest x1 18.2 us: local(): lax.all_to_all(quarters, ('zhi', 'zlo', 'core'), split_axis=0, concat_axi...]
    all_to_all x3 -> x1, blocking collectives: 59.5 us -> 46.6 us  [local(): lax.all_to_all(blocked, ('x', 'zlo'), split_axis=0, concat_axis=0, tiled=...]
    ppermute x0 -> x2, starting transfers between devices: none -> 6.85 us  [the longest x1 4.93 us: local(): arrived = lax.ppermute(theirs, 'core', SWAP)]
    dot_general x0 -> x1, local copies, waits for them, and re-layouts: none -> 4.02 us  [local(): partial_value = jnp.dot(lhs, panel, preferred_element_type=jnp.float32)]
    ppermute x0 -> x2, waiting for transfers between devices: none -> 3.57 us  [the longest x1 3.38 us: local(): other = lax.ppermute(own, 'core', SWAP)]
  transfers between devices with their start and end apart: 3 -> 5, of which waited for: 3 -> 4; matrix products, arithmetic and copies ran while one was open for 1% -> 11% of each run, Pallas kernels for 0% -> 0%
where the time goes in v2:
time: 153 us
  blocking collectives  46.6 us (30%)
  waiting for transfers between devices  37.8 us (25%)
  starting transfers between devices  28.7 us (19%)
  local copies, waits for them, and re-layouts  15.6 us (10%)
  between operations  13.6 us (9%)
  matrix products  5.84 us (4%)
  other arithmetic  4.84 us (3%)
    all_to_all x1, blocking collectives, local(): lax.all_to_all(blocked, ('x', 'zlo'), split_axis=0, concat_axis=0, tiled=...  46.6 us
    all_to_all x1, waiting for transfers between devices, local(): lax.all_to_all(partial_value, ('x', 'zlo'), split_axis=0, concat_axis=0,...  19.6 us
    all_to_all x1, starting transfers between devices, local(): lax.all_to_all(quarters, ('zhi', 'zlo', 'core'), split_axis=0, concat_axi...  18.2 us
    all_to_all x1, waiting for transfers between devices, local(): lax.all_to_all(quarters, ('zhi', 'zlo', 'core'), split_axis=0, concat_axi...  14.7 us
    dot_general x1, matrix products, local(): partial_value = jnp.dot(lhs, panel, preferred_element_type=jnp.float32)  5.84 us
    ppermute x1, starting transfers between devices, local(): arrived = lax.ppermute(theirs, 'core', SWAP)  4.93 us
    dot_general x1, local copies, waits for them, and re-layouts, local(): partial_value = jnp.dot(lhs, panel, preferred_element_type=jnp.float32)  4.02 us
    all_to_all x1, starting transfers between devices, local(): lax.all_to_all(partial_value, ('x', 'zlo'), split_axis=0, concat_axis=0,...  3.61 us
  transfers between devices with their start and end apart: 5, of which 4 were waited for; matrix products, arithmetic and copies ran while one was open for 11% of the time, Pallas kernels for 0%

profile of v2, /device:TPU:1, one launch (start us, length us, event | category | flops | bytes accessed | tf_op | source)
XLA Modules:
  0.0 153.0 jit_solution(16836715132856091521)
XLA Ops:
  6.5 1.1 reshape.109
  7.6 0.8 tile.21
  8.5 18.2 %all-to-all-start.1 = ((bf16[16,32,512]{2,1,0:T(8,128)(2,1)}), bf16[16,32,512]{2,1,0:T(8,128)(2,1)S(1)}, u32[]{:S(2)}, u32[]{:S(2)}) async-start(bf16[16,32,512]{2,1,0:T(8,128)(2,1)} %bitcast.9), calls=%async_computation.1 | async-start | bytes 1048576 | tf_op jit(solution)/shard_map/all_to_all | solution.py:28
  26.7 1.4 fusion.17
  28.1 1.2 fusion.10
  29.3 14.7 %all-to-all-done.1 = bf16[16,32,512]{2,1,0:T(8,128)(2,1)S(1)} async-done(((bf16[16,32,512]{2,1,0:T(8,128)(2,1)}), bf16[16,32,512]{2,1,0:T(8,128)(2,1)S(1)}, u32[]{:S(2)}, u32[]{:S(2)}) %all-to-all-start.1) | async-done | bytes 524320 | tf_op jit(solution)/shard_map/all_to_all | solution.py:28
  44.0 0.8 copy-done
  45.0 1.6 %reshape.108 = bf16[12,4,8,2,512]{4,3,2,1,0:T(2,128)(2,1)S(1)} reshape(bf16[12,32768]{1,0:T(8,128)(2,1)S(1)} %broadcast_select_fusion) | data formatting | bytes 1572864 | tf_op jit(solution)/shard_map/reshape | solution.py:35
  46.6 0.6 copy.36
  47.2 0.6 tile.18
  48.0 46.6 %all_to_all.15 = bf16[16,24,2048]{2,1,0:T(8,128)(2,1)S(1)} all-to-all(bf16[16,24,2048]{2,1,0:T(8,128)(2,1)S(1)} %bitcast.38), channel_id=1, replica_groups=mesh['ylo'=4,'x'=8,'yhi'=2,'zhi'=4,'zlo'=2,'core'=2] {'x','zlo'}, dimensions={0} | all-to-all | bytes 3145728 | tf_op jit(solution)/shard_map/all_to_all | solution.py:41
  94.6 0.9 copy.26
  95.4 1.9 %collective-permute-start = (bf16[16,24,2048]{2,0,1:T(8,128)(2,1)S(1)}, bf16[16,24,2048]{2,0,1:T(8,128)(2,1)S(1)}, u32[]{:S(2)}, u32[]{:S(2)}) collective-permute-start(bf16[16,24,2048]{2,0,1:T(8,128)(2,1)S(1)} %copy.26), channel_id=1, source_target_pairs={{0,1},{1,0},{2,3},{3,2},{4,5},{5,4},{6,7},{7,6},{8,9},{9,8},{10,11... | collective-permute-start | bytes 4718600 | tf_op jit(solution)/shard_map/ppermute | solution.py:42
  97.3 3.4 %collective-permute-done = bf16[16,24,2048]{2,0,1:T(8,128)(2,1)S(1)} collective-permute-done((bf16[16,24,2048]{2,0,1:T(8,128)(2,1)S(1)}, bf16[16,24,2048]{2,0,1:T(8,128)(2,1)S(1)}, u32[]{:S(2)}, u32[]{:S(2)}) %collective-permute-start) | collective-permute-done | bytes 1572896 | tf_op jit(solution)/shard_map/ppermute | solution.py:42
  100.7 0.3 maximum_bitcast_fusion
  101.0 3.2 %copy.28 = bf16[16,2,12,2,2048]{4,3,2,1,0:T(2,128)(2,1)S(1)} copy(bf16[16,2,12,2,2048]{4,0,2,3,1:T(8,128)(2,1)S(1)} %maximum_bitcast_fusion) | data formatting | bytes 6291456 | tf_op jit(solution)/shard_map/transpose | solution.py:45
  104.3 4.0 %dot_general.5 = bf16[16,24,4096]{2,1,0:T(8,128)(2,1)} reshape(bf16[16,2,12,2,2048]{4,3,2,1,0:T(2,128)(2,1)S(1)} %copy.28) | data formatting | bytes 6291456 | tf_op jit(solution)/shard_map/dot_general | solution.py:47
  108.3 5.8 %fusion = f32[16,24,512]{2,1,0:T(8,128)} fusion(bf16[16,24,4096]{2,1,0:T(8,128)(2,1)} %dot_general.5, bf16[4096,512]{1,0:T(8,128)(2,1)} %all-gather.2.cloned.1.call-done), kind=kOutput, calls=%fused_computation | convolution fusion | flops 1610612736 | bytes 8126464 | tf_op jit(solution)/shard_map/dot_general | solution.py:47
  114.2 3.6 %all-to-all-start.2 = ((f32[16,24,512]{2,1,0:T(8,128)}), f32[16,24,512]{2,1,0:T(8,128)S(1)}, u32[]{:S(2)}, u32[]{:S(2)}) async-start(f32[16,24,512]{2,1,0:T(8,128)} %fusion), calls=%async_computation.2 | async-start | bytes 1572864 | tf_op jit(solution)/shard_map/all_to_all | solution.py:49
  118.1 1.3 select_reduce_fusion.1
  119.4 19.6 %all-to-all-done.2 = f32[16,24,512]{2,1,0:T(8,128)S(1)} async-done(((f32[16,24,512]{2,1,0:T(8,128)}), f32[16,24,512]{2,1,0:T(8,128)S(1)}, u32[]{:S(2)}, u32[]{:S(2)}) %all-to-all-start.2) | async-done | bytes 786464 | tf_op jit(solution)/shard_map/all_to_all | solution.py:49
  139.2 4.9 %collective-permute-start.1 = (f32[2,12,512]{2,0,1:T(2,128)S(1)}, f32[2,12,512]{2,0,1:T(2,128)S(1)}, u32[]{:S(2)}, u32[]{:S(2)}) collective-permute-start(f32[2,12,512]{2,0,1:T(2,128)S(1)} %slice_bitcast_fusion), channel_id=1, source_target_pairs={{0,1},{1,0},{2,3},{3,2},{4,5},{5,4},{6,7},{7,6},{8,9},{9,8},{10,11... | collective-permute-start | bytes 147464 | tf_op jit(solution)/shard_map/ppermute | solution.py:53
  144.1 0.7 broadcast_compare_fusion
  145.4 0.8 divide_select_fusion
  (29 shorter events, 1.5 us)
Async XLA Ops:
  6.5 38.3 %copy-start.1 = (bf16[12,32768]{1,0:T(8,128)(2,1)S(1)}, bf16[12,32768]{1,0:T(8,128)(2,1)}, u32[]{:S(2)}) copy-start(bf16[12,32768]{1,0:T(8,128)(2,1)} %param.6) | copy-start | bytes 2359300
  8.5 35.5 %all-to-all-start.1 = ((bf16[16,32,512]{2,1,0:T(8,128)(2,1)}), bf16[16,32,512]{2,1,0:T(8,128)(2,1)S(1)}, u32[]{:S(2)}, u32[]{:S(2)}) async-start(bf16[16,32,512]{2,1,0:T(8,128)(2,1)} %bitcast.9), calls=%async_computation.1 | async-start | bytes 1048576 | tf_op jit(solution)/shard_map/all_to_all | solution.py:28
  26.7 81.6 %all-gather.2.cloned.1.call-start = ((), (), s32[]{:S(2)}) async-start(), calls=%async_computation.3 | async-start | bytes 4718592 | tf_op jit(solution)/shard_map/all_gather | solution.py:29
  44.0 0.8 copy-start
  95.4 5.3 %collective-permute-start = (bf16[16,24,2048]{2,0,1:T(8,128)(2,1)S(1)}, bf16[16,24,2048]{2,0,1:T(8,128)(2,1)S(1)}, u32[]{:S(2)}, u32[]{:S(2)}) collective-permute-start(bf16[16,24,2048]{2,0,1:T(8,128)(2,1)S(1)} %copy.26), channel_id=1, source_target_pairs={{0,1},{1,0},{2,3},{3,2},{4,5},{5,4},{6,7},{7,6},{8,9},{9,8},{10,11... | collective-permute-start | bytes 4718600 | tf_op jit(solution)/shard_map/ppermute | solution.py:42
  108.3 9.5 %copy-start.2 = (s32[12,2]{0,1:T(2,128)S(1)}, s32[12,2]{0,1:T(2,128)}, u32[]{:S(2)}) copy-start(s32[12,2]{0,1:T(2,128)} %param.8) | copy-start | bytes 292
  108.3 9.6 %copy-start.3 = (f32[200]{0:T(256)S(1)}, f32[200]{0:T(256)}, u32[]{:S(2)}) copy-start(f32[200]{0:T(256)} %param.10) | copy-start | bytes 2404
  108.3 9.9 %copy-start.4 = (f32[128]{0:T(128)S(1)}, f32[128]{0:T(128)}, u32[]{:S(2)}) copy-start(f32[128]{0:T(128)} %param.11) | copy-start | bytes 1540
  114.2 24.8 %all-to-all-start.2 = ((f32[16,24,512]{2,1,0:T(8,128)}), f32[16,24,512]{2,1,0:T(8,128)S(1)}, u32[]{:S(2)}, u32[]{:S(2)}) async-start(f32[16,24,512]{2,1,0:T(8,128)} %fusion), calls=%async_computation.2 | async-start | bytes 1572864 | tf_op jit(solution)/shard_map/all_to_all | solution.py:49
  139.2 5.8 %collective-permute-start.1 = (f32[2,12,512]{2,0,1:T(2,128)S(1)}, f32[2,12,512]{2,0,1:T(2,128)S(1)}, u32[]{:S(2)}, u32[]{:S(2)}) collective-permute-start(f32[2,12,512]{2,0,1:T(2,128)S(1)} %slice_bitcast_fusion), channel_id=1, source_target_pairs={{0,1},{1,0},{2,3},{3,2},{4,5},{5,4},{6,7},{7,6},{8,9},{9,8},{10,11... | collective-permute-start | bytes 147464 | tf_op jit(solution)/shard_map/ppermute | solution.py:53
Sparse Core Ops, SparseCore 0:
  44.9 56.7 all-gather.1

commit v3 on v2

--- a/solution.py
+++ b/solution.py
@@ -1,6 +1,10 @@
+import functools
+
 import jax
 import jax.numpy as jnp
 from jax import lax
+from jax.experimental import pallas as pl
+from jax.experimental.pallas import tpu as pltpu
 from jax.sharding import Mesh, PartitionSpec as P
 
 NIRREP = 8
@@ -8,11 +12,89 @@
 AXES = ("ylo", "x", "yhi", "zhi", "zlo", "core")
 RING = ("yhi", "ylo")
 SWAP = [(0, 1), (1, 0)]
+RING_COLUMNS = 128
 
 
 def table_lookup(indices, table, table_length):
     matches = indices[..., None] == jnp.arange(table_length, dtype=jnp.int32)
     return jnp.sum(jnp.where(matches, table, jnp.zeros((), table.dtype)), axis=-1)
+
+
+def ring_blocks(block, yhi, ylo):
+    length = yhi * ylo
+
+    def flat(place):
+        return place % length % ylo * yhi + place % length // ylo
+
+    def move(value, shift):
+        pairs = [(flat(place), flat(place + shift)) for place in range(length)]
+        return lax.ppermute(value, ("ylo", "yhi"), pairs)
+
+    up = [block]
+    down = [block]
+    for step in range(length // 2):
+        up.append(move(up[-1], 1))
+        if step < length // 2 - 1:
+            down.append(move(down[-1], -1))
+    return jnp.stack(up + down[:0:-1])
+
+
+def multiply_kernel(pairs, place_ref, own_ref, other_ref, panel_ref, ring_ref, out_ref, sums):
+    half = pl.program_id(0)
+    length, stripe, _ = ring_ref.shape
+    wide = panel_ref.shape[1]
+    width = out_ref.shape[1]
+    blocks = own_ref.shape[1] // stripe
+    for side, lhs_ref in enumerate((own_ref, other_ref)):
+        sums[2 * side + half, :, :wide] = jnp.dot(
+            lhs_ref[...], panel_ref[...], preferred_element_type=jnp.float32
+        )
+        total = jnp.zeros((lhs_ref.shape[0], width - wide), jnp.float32)
+        for block in range(blocks):
+            entry = lax.rem(place_ref[0] - (half * blocks + block) + length, length)
+            total += jnp.dot(
+                lhs_ref[:, block * stripe : (block + 1) * stripe],
+                ring_ref[entry],
+                preferred_element_type=jnp.float32,
+            )
+        sums[2 * side + half, :, wide:] = total
+
+    @pl.when(half == 1)
+    def _():
+        for start in range(0, out_ref.shape[0], 2 * pairs):
+            first = slice(start, start + pairs)
+            second = slice(start + pairs, start + 2 * pairs)
+            out_ref[first, :] = sums[0, first, :] + sums[1, second, :]
+            out_ref[second, :] = sums[2, first, :] + sums[3, second, :]
+
+
+def multiply(own, other, panel, ring, place, pairs):
+    rows, half_depth = own.shape
+    depth, wide = panel.shape
+    width = wide + ring.shape[2]
+    return pl.pallas_call(
+        functools.partial(multiply_kernel, pairs),
+        grid=(depth // half_depth,),
+        out_shape=jax.ShapeDtypeStruct((rows, width), jnp.float32),
+        in_specs=[
+            pl.BlockSpec(memory_space=pltpu.SMEM),
+            pl.BlockSpec((rows, half_depth), lambda k: (0, 0)),
+            pl.BlockSpec((rows, half_depth), lambda k: (0, 0)),
+            pl.BlockSpec((half_depth, wide), lambda k: (k, 0)),
+            pl.BlockSpec(ring.shape, lambda k: (0, 0, 0)),
+        ],
+        out_specs=pl.BlockSpec((rows, width), lambda k: (0, 0)),
+        scratch_shapes=[pltpu.VMEM((4, rows, width), jnp.float32)],
+        compiler_params=pltpu.CompilerParams(
+            dimension_semantics=("arbitrary",), vmem_limit_bytes=56 * 1024 * 1024
+        ),
+        cost_estimate=pl.CostEstimate(
+            flops=4 * rows * depth * width,
+            bytes_accessed=2 * (rows + width) * depth + 4 * rows * width,
+            transcendentals=0,
+        ),
+        name="multiply",
+    )(place.reshape(1), own, other, panel, ring)
 
 
 def local(amplitudes, integrals, pair_list, block_sizes, occ_energy, virt_energy):
@@ -26,7 +108,6 @@
     quarters = integrals.reshape(slab_rows, parts, quarter).transpose(1, 0, 2)
     quarters = jnp.tile(quarters, (size["zhi"], 1, 1))
     rows = lax.all_to_all(quarters, ("zhi", "zlo", "core"), split_axis=0, concat_axis=0, tiled=True)
-    panel = lax.all_gather(rows.reshape(stripe, quarter), RING, axis=0, tiled=True)
 
     pair_index = jnp.arange(summed, dtype=jnp.int32)
     size_here = jnp.where(pair_index < NV * NV, block_sizes[0], block_sizes[1])
@@ -38,13 +119,17 @@
     blocked = jnp.tile(blocked, (1, size["zlo"], 1, 1))
     groups = size["x"] * size["zlo"]
     blocked = blocked.reshape(groups, size["yhi"] * pairs_local, size["ylo"] * stripe)
+    rows, blocked = lax.optimization_barrier((rows, blocked))
+    rows = rows.reshape(stripe, quarter)
+    wide = quarter - RING_COLUMNS
+    panel = lax.all_gather(rows[:, :wide], RING, axis=0, tiled=True)
     own = lax.all_to_all(blocked, ("x", "zlo"), split_axis=0, concat_axis=0, tiled=True)
+    ring = ring_blocks(rows[:, wide:], size["yhi"], size["ylo"])
+    own, ring = lax.optimization_barrier((own, ring))
+    own = own.reshape(groups * size["yhi"] * pairs_local, size["ylo"] * stripe)
     other = lax.ppermute(own, "core", SWAP)
-    lhs = jnp.stack([own, other], axis=1)
-    lhs = lhs.reshape(groups, size["core"], size["yhi"], pairs_local, size["ylo"] * stripe)
-    lhs = lhs.transpose(0, 1, 3, 2, 4).reshape(groups * size["core"] * pairs_local, -1)
-
-    partial_value = jnp.dot(lhs, panel, preferred_element_type=jnp.float32)
+    place = lax.axis_index("yhi") * size["ylo"] + lax.axis_index("ylo")
+    partial_value = multiply(own, other, panel, ring, place, pairs_local)
     partial_value = partial_value.reshape(groups, size["core"] * pairs_local, quarter)
     pieces = lax.all_to_all(partial_value, ("x", "zlo"), split_axis=0, concat_axis=0, tiled=True)
     pieces = pieces.reshape(size["x"], size["zlo"], size["core"], pairs_local, quarter)

time: 153 us -> 155 us (1.013)
  blocking collectives: 46.6 us -> 0 us
  starting transfers between devices: 28.7 us -> 66.6 us
  waiting for transfers between devices: 37.8 us -> 52.7 us
  Pallas kernels: 0 us -> 8.89 us
  local copies, waits for them, and re-layouts: 15.6 us -> 8.04 us
  matrix products: 5.84 us -> 0 us
    all_to_all x1 -> x0, blocking collectives: 46.6 us -> none  [local(): lax.all_to_all(blocked, ('x', 'zlo'), split_axis=0, concat_axis=0, tiled=...]
    ppermute x0 -> x7, starting transfers between devices: none -> 24.4 us  [move(): return lax.ppermute(value, ('ylo', 'yhi'), pairs)]
    ppermute x0 -> x7, waiting for transfers between devices: none -> 17.8 us  [move(): return lax.ppermute(value, ('ylo', 'yhi'), pairs)]
    pallas_call x0 -> x1, Pallas kernels: none -> 8.89 us  [multiply(): pl.pallas_call(functools.partial(multiply_kernel, pairs), grid=(depth //...]
    all_to_all x0 -> x1, starting transfers between devices: none -> 6.6 us  [local(): lax.all_to_all(blocked, ('x', 'zlo'), split_axis=0, concat_axis=0, tiled=...]
    dot_general x1 -> x0, matrix products: 5.84 us -> none  [local(): partial_value = jnp.dot(lhs, panel, preferred_element_type=jnp.float32)]
    all_to_all x1, starting transfers between devices: 3.61 us -> 7.98 us  [local(): lax.all_to_all(partial_value, ('x', 'zlo'), split_axis=0, concat_axis=0,...]
    dot_general x1 -> x0, local copies, waits for them, and re-layouts: 4.02 us -> none  [local(): partial_value = jnp.dot(lhs, panel, preferred_element_type=jnp.float32)]
  transfers between devices with their start and end apart: 5 -> 13, of which waited for: 4 -> 10; matrix products, arithmetic and copies ran while one was open for 11% -> 5% of each run, Pallas kernels for 0% -> 0%
where the time goes in v3:
time: 155 us
  starting transfers between devices  66.6 us (43%)
  waiting for transfers between devices  52.7 us (34%)
  between operations  13.8 us (9%)
  Pallas kernels  8.89 us (6%)
  local copies, waits for them, and re-layouts  8.04 us (5%)
  other arithmetic  4.57 us (3%)
    ppermute x7, starting transfers between devices, move(): return lax.ppermute(value, ('ylo', 'yhi'), pairs)  24.4 us
    all_to_all x1, waiting for transfers between devices, local(): lax.all_to_all(partial_value, ('x', 'zlo'), split_axis=0, concat_axis=0,...  19.1 us
    all_to_all x1, starting transfers between devices, local(): lax.all_to_all(quarters, ('zhi', 'zlo', 'core'), split_axis=0, concat_axi...  18.2 us
    ppermute x7, waiting for transfers between devices, move(): return lax.ppermute(value, ('ylo', 'yhi'), pairs)  17.8 us
    all_to_all x1, waiting for transfers between devices, local(): lax.all_to_all(quarters, ('zhi', 'zlo', 'core'), split_axis=0, concat_axi...  12.4 us
    pallas_call x1, Pallas kernels, multiply(): pl.pallas_call(functools.partial(multiply_kernel, pairs), grid=(depth //...  8.89 us
    all_to_all x1, starting transfers between devices, local(): lax.all_to_all(partial_value, ('x', 'zlo'), split_axis=0, concat_axis=0,...  7.98 us
    all_to_all x1, starting transfers between devices, local(): lax.all_to_all(blocked, ('x', 'zlo'), split_axis=0, concat_axis=0, tiled=...  6.6 us
  transfers between devices with their start and end apart: 13, of which 10 were waited for; matrix products, arithmetic and copies ran while one was open for 5% of the time, Pallas kernels for 0%

profile of v3, /device:TPU:1, one launch (start us, length us, event | category | flops | bytes accessed | tf_op | source)
XLA Modules:
  0.0 154.6 jit_solution(14812941429127213885)
XLA Ops:
  8.5 18.2 %all-to-all-start = ((bf16[16,32,512]{2,1,0:T(8,128)(2,1)}), bf16[16,32,512]{2,1,0:T(8,128)(2,1)S(1)}, u32[]{:S(2)}, u32[]{:S(2)}) async-start(bf16[16,32,512]{2,1,0:T(8,128)(2,1)} %bitcast.3), calls=%async_computation | async-start | bytes 1048576 | tf_op jit(solution)/shard_map/all_to_all | solution.py:110
  27.4 1.3 fusion.8
  28.9 1.6 %reshape.110 = bf16[12,4,8,2,512]{4,3,2,1,0:T(2,128)(2,1)S(1)} reshape(bf16[12,32768]{1,0:T(8,128)(2,1)S(1)} %broadcast_select_fusion) | data formatting | bytes 1572864 | tf_op jit(solution)/shard_map/reshape | solution.py:116
  31.7 12.4 %all-to-all-done = bf16[16,32,512]{2,1,0:T(8,128)(2,1)S(1)} async-done(((bf16[16,32,512]{2,1,0:T(8,128)(2,1)}), bf16[16,32,512]{2,1,0:T(8,128)(2,1)S(1)}, u32[]{:S(2)}, u32[]{:S(2)}) %all-to-all-start) | async-done | bytes 524320 | tf_op jit(solution)/shard_map/all_to_all | solution.py:110
  44.0 1.3 tile.21
  46.2 6.6 %all-to-all-start.1 = ((bf16[16,24,2048]{2,1,0:T(8,128)(2,1)}), bf16[16,24,2048]{2,1,0:T(8,128)(2,1)S(1)}, u32[]{:S(2)}, u32[]{:S(2)}) async-start(bf16[16,24,2048]{2,1,0:T(8,128)(2,1)} %bitcast.7), calls=%async_computation.1 | async-start | bytes 3145728 | tf_op jit(solution)/shard_map/all_to_all | solution.py:126
  52.8 3.3 %collective-permute-start = (bf16[512,128]{1,0:T(8,128)(2,1)S(1)}, bf16[512,128]{1,0:T(8,128)(2,1)S(1)}, u32[]{:S(2)}, u32[]{:S(2)}) collective-permute-start(bf16[512,128]{1,0:T(8,128)(2,1)S(1)} %slice.28), channel_id=1, source_target_pairs={{0,256},{256,512},{512,768},{768,16},{16,272},{272,528},{528,784},... | collective-permute-start | bytes 393224 | tf_op jit(solution)/shard_map/ppermute | solution.py:31
  56.1 4.5 %collective-permute-start.4 = (bf16[512,128]{1,0:T(8,128)(2,1)S(1)}, bf16[512,128]{1,0:T(8,128)(2,1)S(1)}, u32[]{:S(2)}, u32[]{:S(2)}) collective-permute-start(bf16[512,128]{1,0:T(8,128)(2,1)S(1)} %slice.28), channel_id=1, source_target_pairs={{0,784},{256,0},{512,256},{768,512},{16,768},{272,16},{528,272},{7... | collective-permute-start | bytes 393224 | tf_op jit(solution)/shard_map/ppermute | solution.py:31
  60.7 1.4 collective-permute-done
  62.0 1.9 %collective-permute-start.1 = (bf16[512,128]{1,0:T(8,128)(2,1)S(1)}, bf16[512,128]{1,0:T(8,128)(2,1)S(1)}, u32[]{:S(2)}, u32[]{:S(2)}) collective-permute-start(bf16[512,128]{1,0:T(8,128)(2,1)S(1)} %collective-permute-done), channel_id=1, source_target_pairs={{0,256},{256,512},{512,768},{768,16},{16,272},{272,528},{528,784},... | collective-permute-start | bytes 393224 | tf_op jit(solution)/shard_map/ppermute | solution.py:31
  63.9 1.7 %collective-permute-done.4 = bf16[512,128]{1,0:T(8,128)(2,1)S(1)} collective-permute-done((bf16[512,128]{1,0:T(8,128)(2,1)S(1)}, bf16[512,128]{1,0:T(8,128)(2,1)S(1)}, u32[]{:S(2)}, u32[]{:S(2)}) %collective-permute-start.4) | collective-permute-done | bytes 131104 | tf_op jit(solution)/shard_map/ppermute | solution.py:31
  65.6 5.4 %collective-permute-start.5 = (bf16[512,128]{1,0:T(8,128)(2,1)S(1)}, bf16[512,128]{1,0:T(8,128)(2,1)S(1)}, u32[]{:S(2)}, u32[]{:S(2)}) collective-permute-start(bf16[512,128]{1,0:T(8,128)(2,1)S(1)} %collective-permute-done.4), channel_id=1, source_target_pairs={{0,784},{256,0},{512,256},{768,512},{16,768},{272,16},{528,272},{7... | collective-permute-start | bytes 393224 | tf_op jit(solution)/shard_map/ppermute | solution.py:31
  71.1 2.2 %collective-permute-done.1 = bf16[512,128]{1,0:T(8,128)(2,1)S(1)} collective-permute-done((bf16[512,128]{1,0:T(8,128)(2,1)S(1)}, bf16[512,128]{1,0:T(8,128)(2,1)S(1)}, u32[]{:S(2)}, u32[]{:S(2)}) %collective-permute-start.1) | collective-permute-done | bytes 131104 | tf_op jit(solution)/shard_map/ppermute | solution.py:31
  73.3 1.9 %collective-permute-start.2 = (bf16[512,128]{1,0:T(8,128)(2,1)S(1)}, bf16[512,128]{1,0:T(8,128)(2,1)S(1)}, u32[]{:S(2)}, u32[]{:S(2)}) collective-permute-start(bf16[512,128]{1,0:T(8,128)(2,1)S(1)} %collective-permute-done.1), channel_id=1, source_target_pairs={{0,256},{256,512},{512,768},{768,16},{16,272},{272,528},{528,784},... | collective-permute-start | bytes 393224 | tf_op jit(solution)/shard_map/ppermute | solution.py:31
  76.5 5.4 %collective-permute-start.6 = (bf16[512,128]{1,0:T(8,128)(2,1)S(1)}, bf16[512,128]{1,0:T(8,128)(2,1)S(1)}, u32[]{:S(2)}, u32[]{:S(2)}) collective-permute-start(bf16[512,128]{1,0:T(8,128)(2,1)S(1)} %collective-permute-done.5), channel_id=1, source_target_pairs={{0,784},{256,0},{512,256},{768,512},{16,768},{272,16},{528,272},{7... | collective-permute-start | bytes 393224 | tf_op jit(solution)/shard_map/ppermute | solution.py:31
  81.9 2.5 %collective-permute-done.2 = bf16[512,128]{1,0:T(8,128)(2,1)S(1)} collective-permute-done((bf16[512,128]{1,0:T(8,128)(2,1)S(1)}, bf16[512,128]{1,0:T(8,128)(2,1)S(1)}, u32[]{:S(2)}, u32[]{:S(2)}) %collective-permute-start.2) | collective-permute-done | bytes 131104 | tf_op jit(solution)/shard_map/ppermute | solution.py:31
  84.5 1.9 %collective-permute-start.3 = (bf16[512,128]{1,0:T(8,128)(2,1)S(1)}, bf16[512,128]{1,0:T(8,128)(2,1)S(1)}, u32[]{:S(2)}, u32[]{:S(2)}) collective-permute-start(bf16[512,128]{1,0:T(8,128)(2,1)S(1)} %collective-permute-done.2), channel_id=1, source_target_pairs={{0,256},{256,512},{512,768},{768,16},{16,272},{272,528},{528,784},... | collective-permute-start | bytes 393224 | tf_op jit(solution)/shard_map/ppermute | solution.py:31
  86.4 8.7 %collective-permute-done.3 = bf16[512,128]{1,0:T(8,128)(2,1)S(1)} collective-permute-done((bf16[512,128]{1,0:T(8,128)(2,1)S(1)}, bf16[512,128]{1,0:T(8,128)(2,1)S(1)}, u32[]{:S(2)}, u32[]{:S(2)}) %collective-permute-start.3) | collective-permute-done | bytes 131104 | tf_op jit(solution)/shard_map/ppermute | solution.py:31
  95.2 4.1 %collective-permute-start.7 = (bf16[384,2048]{1,0:T(8,128)(2,1)S(1)}, bf16[384,2048]{1,0:T(8,128)(2,1)}, u32[]{:S(2)}, u32[]{:S(2)}) collective-permute-start(bf16[384,2048]{1,0:T(8,128)(2,1)S(1)} %bitcast.54), channel_id=1, source_target_pairs={{0,1},{1,0},{2,3},{3,2},{4,5},{5,4},{6,7},{7,6},{8,9},{9,8},{10,11... | collective-permute-start | bytes 4718600 | tf_op jit(solution)/shard_map/ppermute | solution.py:130
  99.3 3.1 %collective-permute-done.7.other_ref = bf16[384,2048]{1,0:T(8,128)(2,1)} collective-permute-done((bf16[384,2048]{1,0:T(8,128)(2,1)S(1)}, bf16[384,2048]{1,0:T(8,128)(2,1)}, u32[]{:S(2)}, u32[]{:S(2)}) %collective-permute-start.7) | collective-permute-done | bytes 1572896 | tf_op jit(solution)/shard_map/ppermute | solution.py:130
  102.5 8.9 %multiply.1 = f32[384,512]{1,0:T(8,128)} custom-call(s32[1]{0:T(128)} %bitcast.1.place_ref, bf16[384,2048]{1,0:T(8,128)(2,1)} %bitcast.55, bf16[384,2048]{1,0:T(8,128)(2,1)} %collective-permute-done.7.other_ref, bf16[4096,384]{1,0:T(8,128)(2,1)} %all-gather.2.cloned.1.call-done.panel_ref, bf16[8,512,128]{2,1,0:T(8,128)(2,1)} %copy-done.2), custom_call_target="tpu_custom_call" | custom-call | flops 3221225472 | bytes 8126464 | tf_op jit(solution)/shard_map/multiply/pallas_call | solution.py:75
  111.4 8.0 %all-to-all-start.2 = ((f32[16,24,512]{2,1,0:T(8,128)}), f32[16,24,512]{2,1,0:T(8,128)S(1)}, u32[]{:S(2)}, u32[]{:S(2)}) async-start(f32[16,24,512]{2,1,0:T(8,128)} %bitcast.56), calls=%async_computation.2 | async-start | bytes 1572864 | tf_op jit(solution)/shard_map/all_to_all | solution.py:134
  121.0 19.1 %all-to-all-done.2 = f32[16,24,512]{2,1,0:T(8,128)S(1)} async-done(((f32[16,24,512]{2,1,0:T(8,128)}), f32[16,24,512]{2,1,0:T(8,128)S(1)}, u32[]{:S(2)}, u32[]{:S(2)}) %all-to-all-start.2) | async-done | bytes 786464 | tf_op jit(solution)/shard_map/all_to_all | solution.py:134
  140.3 5.3 %collective-permute-start.8 = (f32[2,12,512]{2,0,1:T(2,128)S(1)}, f32[2,12,512]{2,0,1:T(2,128)S(1)}, u32[]{:S(2)}, u32[]{:S(2)}) collective-permute-start(f32[2,12,512]{2,0,1:T(2,128)S(1)} %slice_bitcast_fusion), channel_id=1, source_target_pairs={{0,1},{1,0},{2,3},{3,2},{4,5},{5,4},{6,7},{7,6},{8,9},{9,8},{10,11... | collective-permute-start | bytes 147464 | tf_op jit(solution)/shard_map/ppermute | solution.py:138
  (54 shorter events, 10.0 us)
Async XLA Ops:
  6.5 20.2 %copy-start.3 = (s32[8]{0:T(128)S(1)}, s32[8]{0:T(128)}, u32[]{:S(2)}) copy-start(s32[8]{0:T(128)} %param.9) | copy-start | bytes 100
  6.5 22.2 %copy-start.1 = (bf16[12,32768]{1,0:T(8,128)(2,1)S(1)}, bf16[12,32768]{1,0:T(8,128)(2,1)}, u32[]{:S(2)}) copy-start(bf16[12,32768]{1,0:T(8,128)(2,1)} %param.6) | copy-start | bytes 2359300
  8.5 35.5 %all-to-all-start = ((bf16[16,32,512]{2,1,0:T(8,128)(2,1)}), bf16[16,32,512]{2,1,0:T(8,128)(2,1)S(1)}, u32[]{:S(2)}, u32[]{:S(2)}) async-start(bf16[16,32,512]{2,1,0:T(8,128)(2,1)} %bitcast.3), calls=%async_computation | async-start | bytes 1048576 | tf_op jit(solution)/shard_map/all_to_all | solution.py:110
  26.7 75.8 %all-gather.2.cloned.1.call-start = ((), (), s32[]{:S(2)}) async-start(), calls=%async_computation.3 | async-start | bytes 3538944 | tf_op jit(solution)/shard_map/all_gather | solution.py:125
  46.2 49.1 %all-to-all-start.1 = ((bf16[16,24,2048]{2,1,0:T(8,128)(2,1)}), bf16[16,24,2048]{2,1,0:T(8,128)(2,1)S(1)}, u32[]{:S(2)}, u32[]{:S(2)}) async-start(bf16[16,24,2048]{2,1,0:T(8,128)(2,1)} %bitcast.7), calls=%async_computation.1 | async-start | bytes 3145728 | tf_op jit(solution)/shard_map/all_to_all | solution.py:126
  52.8 9.2 %collective-permute-start = (bf16[512,128]{1,0:T(8,128)(2,1)S(1)}, bf16[512,128]{1,0:T(8,128)(2,1)S(1)}, u32[]{:S(2)}, u32[]{:S(2)}) collective-permute-start(bf16[512,128]{1,0:T(8,128)(2,1)S(1)} %slice.28), channel_id=1, source_target_pairs={{0,256},{256,512},{512,768},{768,16},{16,272},{272,528},{528,784},... | collective-permute-start | bytes 393224 | tf_op jit(solution)/shard_map/ppermute | solution.py:31
  56.1 9.5 %collective-permute-start.4 = (bf16[512,128]{1,0:T(8,128)(2,1)S(1)}, bf16[512,128]{1,0:T(8,128)(2,1)S(1)}, u32[]{:S(2)}, u32[]{:S(2)}) collective-permute-start(bf16[512,128]{1,0:T(8,128)(2,1)S(1)} %slice.28), channel_id=1, source_target_pairs={{0,784},{256,0},{512,256},{768,512},{16,768},{272,16},{528,272},{7... | collective-permute-start | bytes 393224 | tf_op jit(solution)/shard_map/ppermute | solution.py:31
  62.0 11.3 %collective-permute-start.1 = (bf16[512,128]{1,0:T(8,128)(2,1)S(1)}, bf16[512,128]{1,0:T(8,128)(2,1)S(1)}, u32[]{:S(2)}, u32[]{:S(2)}) collective-permute-start(bf16[512,128]{1,0:T(8,128)(2,1)S(1)} %collective-permute-done), channel_id=1, source_target_pairs={{0,256},{256,512},{512,768},{768,16},{16,272},{272,528},{528,784},... | collective-permute-start | bytes 393224 | tf_op jit(solution)/shard_map/ppermute | solution.py:31
  65.6 10.9 %collective-permute-start.5 = (bf16[512,128]{1,0:T(8,128)(2,1)S(1)}, bf16[512,128]{1,0:T(8,128)(2,1)S(1)}, u32[]{:S(2)}, u32[]{:S(2)}) collective-permute-start(bf16[512,128]{1,0:T(8,128)(2,1)S(1)} %collective-permute-done.4), channel_id=1, source_target_pairs={{0,784},{256,0},{512,256},{768,512},{16,768},{272,16},{528,272},{7... | collective-permute-start | bytes 393224 | tf_op jit(solution)/shard_map/ppermute | solution.py:31
  73.3 11.2 %collective-permute-start.2 = (bf16[512,128]{1,0:T(8,128)(2,1)S(1)}, bf16[512,128]{1,0:T(8,128)(2,1)S(1)}, u32[]{:S(2)}, u32[]{:S(2)}) collective-permute-start(bf16[512,128]{1,0:T(8,128)(2,1)S(1)} %collective-permute-done.1), channel_id=1, source_target_pairs={{0,256},{256,512},{512,768},{768,16},{16,272},{272,528},{528,784},... | collective-permute-start | bytes 393224 | tf_op jit(solution)/shard_map/ppermute | solution.py:31
  76.5 18.6 %collective-permute-start.6 = (bf16[512,128]{1,0:T(8,128)(2,1)S(1)}, bf16[512,128]{1,0:T(8,128)(2,1)S(1)}, u32[]{:S(2)}, u32[]{:S(2)}) collective-permute-start(bf16[512,128]{1,0:T(8,128)(2,1)S(1)} %collective-permute-done.5), channel_id=1, source_target_pairs={{0,784},{256,0},{512,256},{768,512},{16,768},{272,16},{528,272},{7... | collective-permute-start | bytes 393224 | tf_op jit(solution)/shard_map/ppermute | solution.py:31
  84.5 10.6 %collective-permute-start.3 = (bf16[512,128]{1,0:T(8,128)(2,1)S(1)}, bf16[512,128]{1,0:T(8,128)(2,1)S(1)}, u32[]{:S(2)}, u32[]{:S(2)}) collective-permute-start(bf16[512,128]{1,0:T(8,128)(2,1)S(1)} %collective-permute-done.2), channel_id=1, source_target_pairs={{0,256},{256,512},{512,768},{768,16},{16,272},{272,528},{528,784},... | collective-permute-start | bytes 393224 | tf_op jit(solution)/shard_map/ppermute | solution.py:31
  95.2 7.3 %copy-start.2 = (bf16[8,512,128]{2,1,0:T(8,128)(2,1)}, bf16[8,512,128]{2,1,0:T(8,128)(2,1)S(1)}, u32[]{:S(2)}) copy-start(bf16[8,512,128]{2,1,0:T(8,128)(2,1)S(1)} %bitcast_dynamic-update-slice_fusion.ring_ref) | copy-start | bytes 3145732
  95.2 7.3 %copy-start = (bf16[16,24,2048]{2,1,0:T(8,128)(2,1)}, bf16[16,24,2048]{2,1,0:T(8,128)(2,1)S(1)}, u32[]{:S(2)}) copy-start(bf16[16,24,2048]{2,1,0:T(8,128)(2,1)S(1)} %all-to-all-done.1) | copy-start | bytes 4718596
  95.2 7.2 %collective-permute-start.7 = (bf16[384,2048]{1,0:T(8,128)(2,1)S(1)}, bf16[384,2048]{1,0:T(8,128)(2,1)}, u32[]{:S(2)}, u32[]{:S(2)}) collective-permute-start(bf16[384,2048]{1,0:T(8,128)(2,1)S(1)} %bitcast.54), channel_id=1, source_target_pairs={{0,1},{1,0},{2,3},{3,2},{4,5},{5,4},{6,7},{7,6},{8,9},{9,8},{10,11... | collective-permute-start | bytes 4718600 | tf_op jit(solution)/shard_map/ppermute | solution.py:130
  111.4 8.0 %copy-start.4 = (s32[12,2]{0,1:T(2,128)S(1)}, s32[12,2]{0,1:T(2,128)}, u32[]{:S(2)}) copy-start(s32[12,2]{0,1:T(2,128)} %param.8) | copy-start | bytes 292
  111.4 8.1 %copy-start.5 = (f32[200]{0:T(256)S(1)}, f32[200]{0:T(256)}, u32[]{:S(2)}) copy-start(f32[200]{0:T(256)} %param.10) | copy-start | bytes 2404
  111.4 8.4 %copy-start.6 = (f32[128]{0:T(128)S(1)}, f32[128]{0:T(128)}, u32[]{:S(2)}) copy-start(f32[128]{0:T(128)} %param.11) | copy-start | bytes 1540
  111.4 28.8 %all-to-all-start.2 = ((f32[16,24,512]{2,1,0:T(8,128)}), f32[16,24,512]{2,1,0:T(8,128)S(1)}, u32[]{:S(2)}, u32[]{:S(2)}) async-start(f32[16,24,512]{2,1,0:T(8,128)} %bitcast.56), calls=%async_computation.2 | async-start | bytes 1572864 | tf_op jit(solution)/shard_map/all_to_all | solution.py:134
  140.3 6.2 %collective-permute-start.8 = (f32[2,12,512]{2,0,1:T(2,128)S(1)}, f32[2,12,512]{2,0,1:T(2,128)S(1)}, u32[]{:S(2)}, u32[]{:S(2)}) collective-permute-start(f32[2,12,512]{2,0,1:T(2,128)S(1)} %slice_bitcast_fusion), channel_id=1, source_target_pairs={{0,1},{1,0},{2,3},{3,2},{4,5},{5,4},{6,7},{7,6},{8,9},{9,8},{10,11... | collective-permute-start | bytes 147464 | tf_op jit(solution)/shard_map/ppermute | solution.py:138
Sparse Core Ops, SparseCore 0:
  46.3 54.9 all-gather.1

commit v4 on v2

--- a/solution.py
+++ b/solution.py
@@ -1,6 +1,10 @@
+import functools
+
 import jax
 import jax.numpy as jnp
 from jax import lax
+from jax.experimental import pallas as pl
+from jax.experimental.pallas import tpu as pltpu
 from jax.sharding import Mesh, PartitionSpec as P
 
 NIRREP = 8
@@ -15,6 +19,95 @@
     return jnp.sum(jnp.where(matches, table, jnp.zeros((), table.dtype)), axis=-1)
 
 
+def spread_kernel(parts, copies, x_ref, out_ref):
+    width = out_ref.shape[2]
+    for part in range(parts):
+        value = x_ref[:, part * width : (part + 1) * width]
+        for copy in range(copies):
+            out_ref[copy * parts + part] = value
+
+
+def spread_quarters(integrals, parts, copies):
+    rows, width = integrals.shape
+    return pl.pallas_call(
+        functools.partial(spread_kernel, parts, copies),
+        out_shape=jax.ShapeDtypeStruct((parts * copies, rows, width // parts), integrals.dtype),
+        in_specs=[pl.BlockSpec(memory_space=pltpu.VMEM)],
+        out_specs=pl.BlockSpec(memory_space=pltpu.VMEM),
+        cost_estimate=pl.CostEstimate(
+            flops=0, bytes_accessed=2 * rows * width * (1 + copies), transcendentals=0
+        ),
+        name="spread_quarters",
+    )(integrals)
+
+
+def assemble_kernel(pairs, own_ref, other_ref, out_ref):
+    depth = own_ref.shape[2]
+    halves = own_ref.shape[1] // pairs
+    for group in range(own_ref.shape[0]):
+        for half in range(halves):
+            rows = slice(half * pairs, (half + 1) * pairs)
+            both = jnp.concatenate(
+                [ref[group].astype(jnp.float32)[rows] for ref in (own_ref, other_ref)], axis=0
+            )
+            out_ref[group, :, half * depth : (half + 1) * depth] = both.astype(out_ref.dtype)
+
+
+def assemble(own, other, pairs):
+    groups, rows, depth = own.shape
+    halves = rows // pairs
+    block = pl.BlockSpec((4, rows, depth), lambda g: (g, 0, 0))
+    return pl.pallas_call(
+        functools.partial(assemble_kernel, pairs),
+        grid=(groups // 4,),
+        out_shape=jax.ShapeDtypeStruct((groups, 2 * pairs, halves * depth), own.dtype),
+        in_specs=[block, block],
+        out_specs=pl.BlockSpec((4, 2 * pairs, halves * depth), lambda g: (g, 0, 0)),
+        compiler_params=pltpu.CompilerParams(vmem_limit_bytes=16 * 1024 * 1024),
+        cost_estimate=pl.CostEstimate(
+            flops=2 * own.size, bytes_accessed=8 * own.size, transcendentals=0
+        ),
+        name="assemble",
+    )(own, other)
+
+
+def multiply_kernel(lhs_ref, panel_ref, out_ref):
+    product = jnp.dot(lhs_ref[...], panel_ref[...], preferred_element_type=jnp.float32)
+
+    @pl.when(pl.program_id(0) == 0)
+    def _():
+        out_ref[...] = product
+
+    @pl.when(pl.program_id(0) > 0)
+    def _():
+        out_ref[...] += product
+
+
+def multiply(lhs, panel):
+    rows, depth = lhs.shape
+    width = panel.shape[1]
+    block = 1024
+    return pl.pallas_call(
+        multiply_kernel,
+        grid=(depth // block,),
+        out_shape=jax.ShapeDtypeStruct((rows, width), jnp.float32),
+        in_specs=[
+            pl.BlockSpec((rows, block), lambda k: (0, k)),
+            pl.BlockSpec((block, width), lambda k: (k, 0)),
+        ],
+        out_specs=pl.BlockSpec((rows, width), lambda k: (0, 0)),
+        compiler_params=pltpu.CompilerParams(
+            dimension_semantics=("arbitrary",), vmem_limit_bytes=56 * 1024 * 1024
+        ),
+        cost_estimate=pl.CostEstimate(
+            flops=2 * rows * depth * width,
+            bytes_accessed=2 * (rows + width) * depth + 4 * rows * width,
+            transcendentals=0,
+        ),
+        name="multiply",
+    )(lhs, panel)
+
+
 def local(amplitudes, integrals, pair_list, block_sizes, occ_energy, virt_energy):
     size = {axis: lax.axis_size(axis) for axis in AXES}
     pairs_local, summed = amplitudes.shape
@@ -23,10 +116,8 @@
     quarter = out_width // parts
     stripe = size["zhi"] * size["zlo"] * size["core"] * slab_rows
 
-    quarters = integrals.reshape(slab_rows, parts, quarter).transpose(1, 0, 2)
-    quarters = jnp.tile(quarters, (size["zhi"], 1, 1))
+    quarters = spread_quarters(integrals, parts, size["zhi"])
     rows = lax.all_to_all(quarters, ("zhi", "zlo", "core"), split_axis=0, concat_axis=0, tiled=True)
-    panel = lax.all_gather(rows.reshape(stripe, quarter), RING, axis=0, tiled=True)
 
     pair_index = jnp.arange(summed, dtype=jnp.int32)
     size_here = jnp.where(pair_index < NV * NV, block_sizes[0], block_sizes[1])
@@ -34,17 +125,16 @@
     masked = jnp.where(live[None, :], amplitudes, jnp.zeros((), jnp.bfloat16))
     blocked = masked.reshape(pairs_local, size["ylo"], size["x"], size["yhi"], stripe)
     blocked = blocked.transpose(2, 3, 0, 1, 4)
-    blocked = blocked.reshape(size["x"], 1, size["yhi"] * pairs_local, size["ylo"] * stripe)
-    blocked = jnp.tile(blocked, (1, size["zlo"], 1, 1))
+    blocked = blocked.reshape(size["x"], size["yhi"] * pairs_local, size["ylo"] * stripe)
+    rows, blocked = lax.optimization_barrier((rows, blocked))
+    panel = lax.all_gather(rows.reshape(stripe, quarter), RING, axis=0, tiled=True)
     groups = size["x"] * size["zlo"]
-    blocked = blocked.reshape(groups, size["yhi"] * pairs_local, size["ylo"] * stripe)
+    blocked = jnp.broadcast_to(blocked[:, None], (size["x"], size["zlo"]) + blocked.shape[1:])
+    blocked = blocked.reshape((groups,) + blocked.shape[2:])
     own = lax.all_to_all(blocked, ("x", "zlo"), split_axis=0, concat_axis=0, tiled=True)
     other = lax.ppermute(own, "core", SWAP)
-    lhs = jnp.stack([own, other], axis=1)
-    lhs = lhs.reshape(groups, size["core"], size["yhi"], pairs_local, size["ylo"] * stripe)
-    lhs = lhs.transpose(0, 1, 3, 2, 4).reshape(groups * size["core"] * pairs_local, -1)
-
-    partial_value = jnp.dot(lhs, panel, preferred_element_type=jnp.float32)
+    lhs = assemble(own, other, pairs_local)
+    partial_value = multiply(lhs.reshape(groups * size["core"] * pairs_local, -1), panel)
     partial_value = partial_value.reshape(groups, size["core"] * pairs_local, quarter)
     pieces = lax.all_to_all(partial_value, ("x", "zlo"), split_axis=0, concat_axis=0, tiled=True)
     pieces = pieces.reshape(size["x"], size["zlo"], size["core"], pairs_local, quarter)

time: 153 us -> 151 us (0.987)
  local copies, waits for them, and re-layouts: 15.6 us -> 6.44 us
  Pallas kernels: 0 us -> 8.25 us
  matrix products: 5.84 us -> 0 us
  starting transfers between devices: 28.7 us -> 33 us
    pallas_call x0 -> x3, Pallas kernels: none -> 8.25 us  [the longest x1 5.87 us: multiply(): pl.pallas_call(multiply_kernel, grid=(depth // block,), out_shape=jax.Sha...]
    dot_general x1 -> x0, matrix products: 5.84 us -> none  [local(): partial_value = jnp.dot(lhs, panel, preferred_element_type=jnp.float32)]
    all_to_all x1, starting transfers between devices: 3.61 us -> 7.9 us  [local(): lax.all_to_all(partial_value, ('x', 'zlo'), split_axis=0, concat_axis=0,...]
    dot_general x1 -> x0, local copies, waits for them, and re-layouts: 4.02 us -> none  [local(): partial_value = jnp.dot(lhs, panel, preferred_element_type=jnp.float32)]
    transpose x2 -> x0, local copies, waits for them, and re-layouts: 3.27 us -> none  [the longest x1 3.24 us: local(): lhs.transpose(0, 1, 3, 2, 4)]
    all_gather x1, waiting for transfers between devices: 0.01 us -> 2.64 us  [local(): lax.all_gather(rows.reshape(stripe, quarter), RING, axis=0, tiled=True)]
    all_to_all x1, waiting for transfers between devices: 14.7 us -> 12.4 us  [local(): lax.all_to_all(quarters, ('zhi', 'zlo', 'core'), split_axis=0, concat_axi...]
    unnamed x14 -> x18, local copies, waits for them, and re-layouts: 1.04 us -> 2.7 us
  transfers between devices with their start and end apart: 5 -> 5, of which waited for: 4 -> 5; matrix products, arithmetic and copies ran while one was open for 11% -> 5% of each run, Pallas kernels for 0% -> 0%
where the time goes in v4:
time: 151 us; the launch traced here: 150 us
  blocking collectives  46.6 us (31%)
  waiting for transfers between devices  37.7 us (25%)
  starting transfers between devices  33 us (22%)
  between operations  13.6 us (9%)
  Pallas kernels  8.25 us (5%)
  local copies, waits for them, and re-layouts  6.44 us (4%)
  other arithmetic  4.62 us (3%)
    all_to_all x1, blocking collectives, local(): lax.all_to_all(blocked, ('x', 'zlo'), split_axis=0, concat_axis=0, tiled=...  46.6 us
    all_to_all x1, waiting for transfers between devices, local(): lax.all_to_all(partial_value, ('x', 'zlo'), split_axis=0, concat_axis=0,...  19.1 us
    all_to_all x1, starting transfers between devices, local(): lax.all_to_all(quarters, ('zhi', 'zlo', 'core'), split_axis=0, concat_axi...  18.2 us
    all_to_all x1, waiting for transfers between devices, local(): lax.all_to_all(quarters, ('zhi', 'zlo', 'core'), split_axis=0, concat_axi...  12.4 us
    all_to_all x1, starting transfers between devices, local(): lax.all_to_all(partial_value, ('x', 'zlo'), split_axis=0, concat_axis=0,...  7.9 us
    pallas_call x1, Pallas kernels, multiply(): pl.pallas_call(multiply_kernel, grid=(depth // block,), out_shape=jax.Sha...  5.87 us
    ppermute x1, starting transfers between devices, local(): arrived = lax.ppermute(theirs, 'core', SWAP)  5 us
    ppermute x1, waiting for transfers between devices, local(): other = lax.ppermute(own, 'core', SWAP)  3.38 us
  transfers between devices with their start and end apart: 5, of which 5 were waited for; matrix products, arithmetic and copies ran while one was open for 5% of the time, Pallas kernels for 0%

profile of v4, /device:TPU:1, one launch (start us, length us, event | category | flops | bytes accessed | tf_op | source)
XLA Modules:
  0.0 150.2 jit_solution(7480332477196299557)
XLA Ops:
  6.5 1.8 %spread_quarters.1 = bf16[16,32,512]{2,1,0:T(8,128)(2,1)} custom-call(bf16[32,2048]{1,0:T(8,128)(2,1)} %x_ref.1), custom_call_target="tpu_custom_call" | custom-call | bytes 655360 | tf_op jit(solution)/shard_map/spread_quarters/pallas_call | solution.py:32
  8.4 18.2 %all-to-all-start = ((bf16[16,32,512]{2,1,0:T(8,128)(2,1)}), bf16[16,32,512]{2,1,0:T(8,128)(2,1)S(1)}, u32[]{:S(2)}, u32[]{:S(2)}) async-start(bf16[16,32,512]{2,1,0:T(8,128)(2,1)} %spread_quarters.1), calls=%async_computation | async-start | bytes 1048576 | tf_op jit(solution)/shard_map/all_to_all | solution.py:120
  26.6 0.6 fusion.15
  27.3 1.3 fusion.8
  28.8 1.6 %reshape.101 = bf16[12,4,8,2,512]{4,3,2,1,0:T(2,128)(2,1)S(1)} reshape(bf16[12,32768]{1,0:T(8,128)(2,1)S(1)} %broadcast_select_fusion) | data formatting | bytes 1572864 | tf_op jit(solution)/shard_map/reshape | solution.py:126
  30.3 0.6 copy.24
  30.9 0.6 reshape.102
  31.5 12.4 %all-to-all-done = bf16[16,32,512]{2,1,0:T(8,128)(2,1)S(1)} async-done(((bf16[16,32,512]{2,1,0:T(8,128)(2,1)}), bf16[16,32,512]{2,1,0:T(8,128)(2,1)S(1)}, u32[]{:S(2)}, u32[]{:S(2)}) %all-to-all-start) | async-done | bytes 524320 | tf_op jit(solution)/shard_map/all_to_all | solution.py:120
  43.9 0.8 copy-done.1
  44.9 46.6 %all_to_all.15.own_ref = bf16[16,24,2048]{2,1,0:T(8,128)(2,1)S(1)} all-to-all(bf16[16,24,2048]{2,1,0:T(8,128)(2,1)S(1)} %bitcast.31), channel_id=1, replica_groups=mesh['ylo'=4,'x'=8,'yhi'=2,'zhi'=4,'zlo'=2,'core'=2] {'x','zlo'}, dimensions={0} | all-to-all | bytes 3145728 | tf_op jit(solution)/shard_map/all_to_all | solution.py:134
  91.5 1.9 %collective-permute-start = (bf16[16,24,2048]{2,1,0:T(8,128)(2,1)S(1)}, bf16[16,24,2048]{2,1,0:T(8,128)(2,1)S(1)}, u32[]{:S(2)}, u32[]{:S(2)}) collective-permute-start(bf16[16,24,2048]{2,1,0:T(8,128)(2,1)S(1)} %all_to_all.15.own_ref), channel_id=1, source_target_pairs={{0,1},{1,0},{2,3},{3,2},{4,5},{5,4},{6,7},{7,6},{8,9},{9,8},{10,11... | collective-permute-start | bytes 4718600 | tf_op jit(solution)/shard_map/ppermute | solution.py:135
  93.4 3.4 %collective-permute-done.other_ref = bf16[16,24,2048]{2,1,0:T(8,128)(2,1)S(1)} collective-permute-done((bf16[16,24,2048]{2,1,0:T(8,128)(2,1)S(1)}, bf16[16,24,2048]{2,1,0:T(8,128)(2,1)S(1)}, u32[]{:S(2)}, u32[]{:S(2)}) %collective-permute-start) | collective-permute-done | bytes 1572896 | tf_op jit(solution)/shard_map/ppermute | solution.py:135
  96.8 0.5 assemble.1
  97.3 1.7 %copy-done = bf16[16,24,4096]{2,1,0:T(8,128)(2,1)} copy-done((bf16[16,24,4096]{2,1,0:T(8,128)(2,1)}, bf16[16,24,4096]{2,1,0:T(8,128)(2,1)S(1)}, u32[]{:S(2)}) %copy-start) | copy-done | bytes 3145752
  99.0 2.6 %all-gather.2.cloned.1.call-done.panel_ref = bf16[4096,512]{1,0:T(8,128)(2,1)} async-done(((bf16[512,512]{1,0:T(8,128)(2,1)}), bf16[4096,512]{1,0:T(8,128)(2,1)}) %all-gather.2.cloned.1.call-update) | async-done | bytes 4194320 | tf_op jit(solution)/shard_map/all_gather | solution.py:130
  101.6 5.9 %multiply.1 = f32[384,512]{1,0:T(8,128)} custom-call(bf16[384,4096]{1,0:T(8,128)(2,1)} %bitcast.30, bf16[4096,512]{1,0:T(8,128)(2,1)} %all-gather.2.cloned.1.call-done.panel_ref), custom_call_target="tpu_custom_call" | custom-call | flops 1610612736 | bytes 8126464 | tf_op jit(solution)/shard_map/multiply/pallas_call | solution.py:90
  107.5 7.9 %all-to-all-start.2 = ((f32[16,24,512]{2,1,0:T(8,128)}), f32[16,24,512]{2,1,0:T(8,128)S(1)}, u32[]{:S(2)}, u32[]{:S(2)}) async-start(f32[16,24,512]{2,1,0:T(8,128)} %bitcast.34), calls=%async_computation.2 | async-start | bytes 1572864 | tf_op jit(solution)/shard_map/all_to_all | solution.py:139
  115.5 0.3 fusion.9
  115.8 1.3 select_reduce_fusion.1
  117.1 19.1 %all-to-all-done.2 = f32[16,24,512]{2,1,0:T(8,128)S(1)} async-done(((f32[16,24,512]{2,1,0:T(8,128)}), f32[16,24,512]{2,1,0:T(8,128)S(1)}, u32[]{:S(2)}, u32[]{:S(2)}) %all-to-all-start.2) | async-done | bytes 786464 | tf_op jit(solution)/shard_map/all_to_all | solution.py:139
  136.4 5.0 %collective-permute-start.1 = (f32[2,12,512]{2,0,1:T(2,128)S(1)}, f32[2,12,512]{2,0,1:T(2,128)S(1)}, u32[]{:S(2)}, u32[]{:S(2)}) collective-permute-start(f32[2,12,512]{2,0,1:T(2,128)S(1)} %slice_bitcast_fusion), channel_id=1, source_target_pairs={{0,1},{1,0},{2,3},{3,2},{4,5},{5,4},{6,7},{7,6},{8,9},{9,8},{10,11... | collective-permute-start | bytes 147464 | tf_op jit(solution)/shard_map/ppermute | solution.py:143
  141.4 0.7 broadcast_compare_fusion
  142.0 0.2 collective-permute-done.1
  142.6 0.8 divide_select_fusion
  (28 shorter events, 1.0 us)
Async XLA Ops:
  6.5 20.1 %copy-start.3 = (s32[8]{0:T(128)S(1)}, s32[8]{0:T(128)}, u32[]{:S(2)}) copy-start(s32[8]{0:T(128)} %param.9) | copy-start | bytes 100
  6.5 22.0 %copy-start.2 = (bf16[12,32768]{1,0:T(8,128)(2,1)S(1)}, bf16[12,32768]{1,0:T(8,128)(2,1)}, u32[]{:S(2)}) copy-start(bf16[12,32768]{1,0:T(8,128)(2,1)} %param.6) | copy-start | bytes 2359300
  8.4 35.5 %all-to-all-start = ((bf16[16,32,512]{2,1,0:T(8,128)(2,1)}), bf16[16,32,512]{2,1,0:T(8,128)(2,1)S(1)}, u32[]{:S(2)}, u32[]{:S(2)}) async-start(bf16[16,32,512]{2,1,0:T(8,128)(2,1)} %spread_quarters.1), calls=%async_computation | async-start | bytes 1048576 | tf_op jit(solution)/shard_map/all_to_all | solution.py:120
  26.6 75.1 %all-gather.2.cloned.1.call-start = ((), (), s32[]{:S(2)}) async-start(), calls=%async_computation.3 | async-start | bytes 4718592 | tf_op jit(solution)/shard_map/all_gather | solution.py:130
  43.9 0.8 copy-start.1
  91.5 5.3 %collective-permute-start = (bf16[16,24,2048]{2,1,0:T(8,128)(2,1)S(1)}, bf16[16,24,2048]{2,1,0:T(8,128)(2,1)S(1)}, u32[]{:S(2)}, u32[]{:S(2)}) collective-permute-start(bf16[16,24,2048]{2,1,0:T(8,128)(2,1)S(1)} %all_to_all.15.own_ref), channel_id=1, source_target_pairs={{0,1},{1,0},{2,3},{3,2},{4,5},{5,4},{6,7},{7,6},{8,9},{9,8},{10,11... | collective-permute-start | bytes 4718600 | tf_op jit(solution)/shard_map/ppermute | solution.py:135
  97.3 1.7 %copy-start = (bf16[16,24,4096]{2,1,0:T(8,128)(2,1)}, bf16[16,24,4096]{2,1,0:T(8,128)(2,1)S(1)}, u32[]{:S(2)}) copy-start(bf16[16,24,4096]{2,1,0:T(8,128)(2,1)S(1)} %assemble.1) | copy-start | bytes 9437188
  107.5 7.9 %copy-start.4 = (s32[12,2]{0,1:T(2,128)S(1)}, s32[12,2]{0,1:T(2,128)}, u32[]{:S(2)}) copy-start(s32[12,2]{0,1:T(2,128)} %param.8) | copy-start | bytes 292
  107.5 8.0 %copy-start.5 = (f32[200]{0:T(256)S(1)}, f32[200]{0:T(256)}, u32[]{:S(2)}) copy-start(f32[200]{0:T(256)} %param.10) | copy-start | bytes 2404
  107.5 8.3 %copy-start.6 = (f32[128]{0:T(128)S(1)}, f32[128]{0:T(128)}, u32[]{:S(2)}) copy-start(f32[128]{0:T(128)} %param.11) | copy-start | bytes 1540
  107.5 28.7 %all-to-all-start.2 = ((f32[16,24,512]{2,1,0:T(8,128)}), f32[16,24,512]{2,1,0:T(8,128)S(1)}, u32[]{:S(2)}, u32[]{:S(2)}) async-start(f32[16,24,512]{2,1,0:T(8,128)} %bitcast.34), calls=%async_computation.2 | async-start | bytes 1572864 | tf_op jit(solution)/shard_map/all_to_all | solution.py:139
  136.4 5.9 %collective-permute-start.1 = (f32[2,12,512]{2,0,1:T(2,128)S(1)}, f32[2,12,512]{2,0,1:T(2,128)S(1)}, u32[]{:S(2)}, u32[]{:S(2)}) collective-permute-start(f32[2,12,512]{2,0,1:T(2,128)S(1)} %slice_bitcast_fusion), channel_id=1, source_target_pairs={{0,1},{1,0},{2,3},{3,2},{4,5},{5,4},{6,7},{7,6},{8,9},{9,8},{10,11... | collective-permute-start | bytes 147464 | tf_op jit(solution)/shard_map/ppermute | solution.py:143
Sparse Core Ops, SparseCore 0:
  44.8 56.7 all-gather.1

commit v5 on v4

--- a/solution.py
+++ b/solution.py
@@ -71,34 +71,43 @@
     )(own, other)
 
 
-def multiply_kernel(lhs_ref, panel_ref, out_ref):
-    product = jnp.dot(lhs_ref[...], panel_ref[...], preferred_element_type=jnp.float32)
-
-    @pl.when(pl.program_id(0) == 0)
-    def _():
-        out_ref[...] = product
-
-    @pl.when(pl.program_id(0) > 0)
-    def _():
-        out_ref[...] += product
+def multiply_kernel(block, lhs_ref, panel_ref, out_ref, left, right, arrived):
+    copies = []
+    for index, start in enumerate(range(0, panel_ref.shape[0], block)):
+        span = pl.ds(start, block)
+        pair = (
+            pltpu.make_async_copy(lhs_ref.at[:, span], left.at[:, span], arrived.at[index, 0]),
+            pltpu.make_async_copy(panel_ref.at[span], right.at[span], arrived.at[index, 1]),
+        )
+        for copy in pair:
+            copy.start()
+        copies.append(pair)
+    for index, pair in enumerate(copies):
+        for copy in pair:
+            copy.wait()
+        span = slice(index * block, (index + 1) * block)
+        product = jnp.dot(left[:, span], right[span, :], preferred_element_type=jnp.float32)
+        if index == 0:
+            out_ref[...] = product
+        else:
+            out_ref[...] += product
 
 
 def multiply(lhs, panel):
     rows, depth = lhs.shape
     width = panel.shape[1]
-    block = 1024
+    block = 512
     return pl.pallas_call(
-        multiply_kernel,
-        grid=(depth // block,),
+        functools.partial(multiply_kernel, block),
         out_shape=jax.ShapeDtypeStruct((rows, width), jnp.float32),
-        in_specs=[
-            pl.BlockSpec((rows, block), lambda k: (0, k)),
-            pl.BlockSpec((block, width), lambda k: (k, 0)),
+        in_specs=[pl.BlockSpec(memory_space=pl.ANY)] * 2,
+        out_specs=pl.BlockSpec(memory_space=pltpu.VMEM),
+        scratch_shapes=[
+            pltpu.VMEM((rows, depth), lhs.dtype),
+            pltpu.VMEM((depth, width), panel.dtype),
+            pltpu.SemaphoreType.DMA((depth // block, 2)),
         ],
-        out_specs=pl.BlockSpec((rows, width), lambda k: (0, 0)),
-        compiler_params=pltpu.CompilerParams(
-            dimension_semantics=("arbitrary",), vmem_limit_bytes=56 * 1024 * 1024
-        ),
+        compiler_params=pltpu.CompilerParams(vmem_limit_bytes=56 * 1024 * 1024),
         cost_estimate=pl.CostEstimate(
             flops=2 * rows * depth * width,
             bytes_accessed=2 * (rows + width) * depth + 4 * rows * width,

time: 151 us -> 149 us (0.987)
  no operation moved by 1% of the time
where the time goes in v5:
time: 149 us
  blocking collectives  46.6 us (31%)
  waiting for transfers between devices  37.7 us (25%)
  starting transfers between devices  33 us (22%)
  between operations  13.6 us (9%)
  Pallas kernels  6.87 us (5%)
  local copies, waits for them, and re-layouts  6.44 us (4%)
  other arithmetic  4.62 us (3%)
    all_to_all x1, blocking collectives, local(): lax.all_to_all(blocked, ('x', 'zlo'), split_axis=0, concat_axis=0, tiled=...  46.6 us
    all_to_all x1, waiting for transfers between devices, local(): lax.all_to_all(partial_value, ('x', 'zlo'), split_axis=0, concat_axis=0,...  19.1 us
    all_to_all x1, starting transfers between devices, local(): lax.all_to_all(quarters, ('zhi', 'zlo', 'core'), split_axis=0, concat_axi...  18.2 us
    all_to_all x1, waiting for transfers between devices, local(): lax.all_to_all(quarters, ('zhi', 'zlo', 'core'), split_axis=0, concat_axi...  12.4 us
    all_to_all x1, starting transfers between devices, local(): lax.all_to_all(partial_value, ('x', 'zlo'), split_axis=0, concat_axis=0,...  7.9 us
    ppermute x1, starting transfers between devices, local(): arrived = lax.ppermute(theirs, 'core', SWAP)  5 us
    pallas_call x1, Pallas kernels, multiply(): pl.pallas_call(functools.partial(multiply_kernel, block), out_shape=jax.S...  4.49 us
    ppermute x1, waiting for transfers between devices, local(): other = lax.ppermute(own, 'core', SWAP)  3.38 us
  transfers between devices with their start and end apart: 5, of which 5 were waited for; matrix products, arithmetic and copies ran while one was open for 5% of the time, Pallas kernels for 0%

profile of v5, /device:TPU:1, one launch (start us, length us, event | category | flops | bytes accessed | tf_op | source)
XLA Modules:
  0.0 148.9 jit_solution(12011768835069530593)
XLA Ops:
  6.5 1.8 %spread_quarters.1 = bf16[16,32,512]{2,1,0:T(8,128)(2,1)} custom-call(bf16[32,2048]{1,0:T(8,128)(2,1)} %x_ref.1), custom_call_target="tpu_custom_call" | custom-call | bytes 655360 | tf_op jit(solution)/shard_map/spread_quarters/pallas_call | solution.py:32
  8.4 18.2 %all-to-all-start = ((bf16[16,32,512]{2,1,0:T(8,128)(2,1)}), bf16[16,32,512]{2,1,0:T(8,128)(2,1)S(1)}, u32[]{:S(2)}, u32[]{:S(2)}) async-start(bf16[16,32,512]{2,1,0:T(8,128)(2,1)} %spread_quarters.1), calls=%async_computation | async-start | bytes 1048576 | tf_op jit(solution)/shard_map/all_to_all | solution.py:129
  26.6 0.6 fusion.15
  27.3 1.3 fusion.8
  28.8 1.6 %reshape.101 = bf16[12,4,8,2,512]{4,3,2,1,0:T(2,128)(2,1)S(1)} reshape(bf16[12,32768]{1,0:T(8,128)(2,1)S(1)} %broadcast_select_fusion) | data formatting | bytes 1572864 | tf_op jit(solution)/shard_map/reshape | solution.py:135
  30.3 0.6 copy.24
  30.9 0.6 reshape.102
  31.5 12.4 %all-to-all-done = bf16[16,32,512]{2,1,0:T(8,128)(2,1)S(1)} async-done(((bf16[16,32,512]{2,1,0:T(8,128)(2,1)}), bf16[16,32,512]{2,1,0:T(8,128)(2,1)S(1)}, u32[]{:S(2)}, u32[]{:S(2)}) %all-to-all-start) | async-done | bytes 524320 | tf_op jit(solution)/shard_map/all_to_all | solution.py:129
  43.9 0.8 copy-done.1
  44.9 46.6 %all_to_all.15.own_ref = bf16[16,24,2048]{2,1,0:T(8,128)(2,1)S(1)} all-to-all(bf16[16,24,2048]{2,1,0:T(8,128)(2,1)S(1)} %bitcast.31), channel_id=1, replica_groups=mesh['ylo'=4,'x'=8,'yhi'=2,'zhi'=4,'zlo'=2,'core'=2] {'x','zlo'}, dimensions={0} | all-to-all | bytes 3145728 | tf_op jit(solution)/shard_map/all_to_all | solution.py:143
  91.5 1.9 %collective-permute-start = (bf16[16,24,2048]{2,1,0:T(8,128)(2,1)S(1)}, bf16[16,24,2048]{2,1,0:T(8,128)(2,1)S(1)}, u32[]{:S(2)}, u32[]{:S(2)}) collective-permute-start(bf16[16,24,2048]{2,1,0:T(8,128)(2,1)S(1)} %all_to_all.15.own_ref), channel_id=1, source_target_pairs={{0,1},{1,0},{2,3},{3,2},{4,5},{5,4},{6,7},{7,6},{8,9},{9,8},{10,11... | collective-permute-start | bytes 4718600 | tf_op jit(solution)/shard_map/ppermute | solution.py:144
  93.4 3.4 %collective-permute-done.other_ref = bf16[16,24,2048]{2,1,0:T(8,128)(2,1)S(1)} collective-permute-done((bf16[16,24,2048]{2,1,0:T(8,128)(2,1)S(1)}, bf16[16,24,2048]{2,1,0:T(8,128)(2,1)S(1)}, u32[]{:S(2)}, u32[]{:S(2)}) %collective-permute-start) | collective-permute-done | bytes 1572896 | tf_op jit(solution)/shard_map/ppermute | solution.py:144
  96.8 0.5 assemble.1
  97.3 1.7 %copy-done = bf16[16,24,4096]{2,1,0:T(8,128)(2,1)} copy-done((bf16[16,24,4096]{2,1,0:T(8,128)(2,1)}, bf16[16,24,4096]{2,1,0:T(8,128)(2,1)S(1)}, u32[]{:S(2)}) %copy-start) | copy-done | bytes 3145752
  99.0 2.6 %all-gather.2.cloned.1.call-done.panel_ref = bf16[4096,512]{1,0:T(8,128)(2,1)} async-done(((bf16[512,512]{1,0:T(8,128)(2,1)}), bf16[4096,512]{1,0:T(8,128)(2,1)}) %all-gather.2.cloned.1.call-update) | async-done | bytes 4194320 | tf_op jit(solution)/shard_map/all_gather | solution.py:139
  101.6 4.5 %multiply.1 = f32[384,512]{1,0:T(8,128)} custom-call(bf16[384,4096]{1,0:T(8,128)(2,1)} %bitcast.30, bf16[4096,512]{1,0:T(8,128)(2,1)} %all-gather.2.cloned.1.call-done.panel_ref), custom_call_target="tpu_custom_call" | custom-call | flops 1610612736 | bytes 8126464 | tf_op jit(solution)/shard_map/multiply/pallas_call | solution.py:100
  106.2 7.9 %all-to-all-start.2 = ((f32[16,24,512]{2,1,0:T(8,128)}), f32[16,24,512]{2,1,0:T(8,128)S(1)}, u32[]{:S(2)}, u32[]{:S(2)}) async-start(f32[16,24,512]{2,1,0:T(8,128)} %bitcast.34), calls=%async_computation.2 | async-start | bytes 1572864 | tf_op jit(solution)/shard_map/all_to_all | solution.py:148
  114.2 0.3 fusion.9
  114.4 1.3 select_reduce_fusion.1
  115.7 19.1 %all-to-all-done.2 = f32[16,24,512]{2,1,0:T(8,128)S(1)} async-done(((f32[16,24,512]{2,1,0:T(8,128)}), f32[16,24,512]{2,1,0:T(8,128)S(1)}, u32[]{:S(2)}, u32[]{:S(2)}) %all-to-all-start.2) | async-done | bytes 786464 | tf_op jit(solution)/shard_map/all_to_all | solution.py:148
  135.0 5.0 %collective-permute-start.1 = (f32[2,12,512]{2,0,1:T(2,128)S(1)}, f32[2,12,512]{2,0,1:T(2,128)S(1)}, u32[]{:S(2)}, u32[]{:S(2)}) collective-permute-start(f32[2,12,512]{2,0,1:T(2,128)S(1)} %slice_bitcast_fusion), channel_id=1, source_target_pairs={{0,1},{1,0},{2,3},{3,2},{4,5},{5,4},{6,7},{7,6},{8,9},{9,8},{10,11... | collective-permute-start | bytes 147464 | tf_op jit(solution)/shard_map/ppermute | solution.py:152
  140.0 0.7 broadcast_compare_fusion
  140.7 0.2 collective-permute-done.1
  141.3 0.8 divide_select_fusion
  (28 shorter events, 1.1 us)
Async XLA Ops:
  6.5 20.1 %copy-start.3 = (s32[8]{0:T(128)S(1)}, s32[8]{0:T(128)}, u32[]{:S(2)}) copy-start(s32[8]{0:T(128)} %param.9) | copy-start | bytes 100
  6.5 22.0 %copy-start.2 = (bf16[12,32768]{1,0:T(8,128)(2,1)S(1)}, bf16[12,32768]{1,0:T(8,128)(2,1)}, u32[]{:S(2)}) copy-start(bf16[12,32768]{1,0:T(8,128)(2,1)} %param.6) | copy-start | bytes 2359300
  8.4 35.5 %all-to-all-start = ((bf16[16,32,512]{2,1,0:T(8,128)(2,1)}), bf16[16,32,512]{2,1,0:T(8,128)(2,1)S(1)}, u32[]{:S(2)}, u32[]{:S(2)}) async-start(bf16[16,32,512]{2,1,0:T(8,128)(2,1)} %spread_quarters.1), calls=%async_computation | async-start | bytes 1048576 | tf_op jit(solution)/shard_map/all_to_all | solution.py:129
  26.6 75.1 %all-gather.2.cloned.1.call-start = ((), (), s32[]{:S(2)}) async-start(), calls=%async_computation.3 | async-start | bytes 4718592 | tf_op jit(solution)/shard_map/all_gather | solution.py:139
  43.9 0.8 copy-start.1
  91.5 5.3 %collective-permute-start = (bf16[16,24,2048]{2,1,0:T(8,128)(2,1)S(1)}, bf16[16,24,2048]{2,1,0:T(8,128)(2,1)S(1)}, u32[]{:S(2)}, u32[]{:S(2)}) collective-permute-start(bf16[16,24,2048]{2,1,0:T(8,128)(2,1)S(1)} %all_to_all.15.own_ref), channel_id=1, source_target_pairs={{0,1},{1,0},{2,3},{3,2},{4,5},{5,4},{6,7},{7,6},{8,9},{9,8},{10,11... | collective-permute-start | bytes 4718600 | tf_op jit(solution)/shard_map/ppermute | solution.py:144
  97.3 1.7 %copy-start = (bf16[16,24,4096]{2,1,0:T(8,128)(2,1)}, bf16[16,24,4096]{2,1,0:T(8,128)(2,1)S(1)}, u32[]{:S(2)}) copy-start(bf16[16,24,4096]{2,1,0:T(8,128)(2,1)S(1)} %assemble.1) | copy-start | bytes 9437188
  106.1 7.9 %copy-start.4 = (s32[12,2]{0,1:T(2,128)S(1)}, s32[12,2]{0,1:T(2,128)}, u32[]{:S(2)}) copy-start(s32[12,2]{0,1:T(2,128)} %param.8) | copy-start | bytes 292
  106.1 8.0 %copy-start.5 = (f32[200]{0:T(256)S(1)}, f32[200]{0:T(256)}, u32[]{:S(2)}) copy-start(f32[200]{0:T(256)} %param.10) | copy-start | bytes 2404
  106.1 8.3 %copy-start.6 = (f32[128]{0:T(128)S(1)}, f32[128]{0:T(128)}, u32[]{:S(2)}) copy-start(f32[128]{0:T(128)} %param.11) | copy-start | bytes 1540
  106.2 28.7 %all-to-all-start.2 = ((f32[16,24,512]{2,1,0:T(8,128)}), f32[16,24,512]{2,1,0:T(8,128)S(1)}, u32[]{:S(2)}, u32[]{:S(2)}) async-start(f32[16,24,512]{2,1,0:T(8,128)} %bitcast.34), calls=%async_computation.2 | async-start | bytes 1572864 | tf_op jit(solution)/shard_map/all_to_all | solution.py:148
  135.0 5.9 %collective-permute-start.1 = (f32[2,12,512]{2,0,1:T(2,128)S(1)}, f32[2,12,512]{2,0,1:T(2,128)S(1)}, u32[]{:S(2)}, u32[]{:S(2)}) collective-permute-start(f32[2,12,512]{2,0,1:T(2,128)S(1)} %slice_bitcast_fusion), channel_id=1, source_target_pairs={{0,1},{1,0},{2,3},{3,2},{4,5},{5,4},{6,7},{7,6},{8,9},{9,8},{10,11... | collective-permute-start | bytes 147464 | tf_op jit(solution)/shard_map/ppermute | solution.py:152
Sparse Core Ops, SparseCore 0:
  44.8 56.7 all-gather.1

commit v6 on v5

--- a/solution.py
+++ b/solution.py
@@ -19,21 +19,29 @@
     return jnp.sum(jnp.where(matches, table, jnp.zeros((), table.dtype)), axis=-1)
 
 
-def spread_kernel(parts, copies, x_ref, out_ref):
+def spread_kernel(parts, x_ref, out_ref, done):
     width = out_ref.shape[2]
-    for part in range(parts):
-        value = x_ref[:, part * width : (part + 1) * width]
-        for copy in range(copies):
-            out_ref[copy * parts + part] = value
+    copies = []
+    for index in range(out_ref.shape[0]):
+        start = index % parts * width
+        copies.append(
+            pltpu.make_async_copy(
+                x_ref.at[:, pl.ds(start, width)], out_ref.at[index], done.at[index]
+            )
+        )
+        copies[-1].start()
+    for copy in copies:
+        copy.wait()
 
 
 def spread_quarters(integrals, parts, copies):
     rows, width = integrals.shape
     return pl.pallas_call(
-        functools.partial(spread_kernel, parts, copies),
+        functools.partial(spread_kernel, parts),
         out_shape=jax.ShapeDtypeStruct((parts * copies, rows, width // parts), integrals.dtype),
-        in_specs=[pl.BlockSpec(memory_space=pltpu.VMEM)],
-        out_specs=pl.BlockSpec(memory_space=pltpu.VMEM),
+        in_specs=[pl.BlockSpec(memory_space=pl.ANY)],
+        out_specs=pl.BlockSpec(memory_space=pl.ANY),
+        scratch_shapes=[pltpu.SemaphoreType.DMA((parts * copies,))],
         cost_estimate=pl.CostEstimate(
             flops=0, bytes_accessed=2 * rows * width * (1 + copies), transcendentals=0
         ),
@@ -71,7 +79,9 @@
     )(own, other)
 
 
-def multiply_kernel(block, lhs_ref, panel_ref, out_ref, left, right, arrived):
+def multiply_kernel(
+    block, pairs, core_ref, lhs_ref, panel_ref, out_ref, left, right, total, arrived
+):
     copies = []
     for index, start in enumerate(range(0, panel_ref.shape[0], block)):
         span = pl.ds(start, block)
@@ -88,23 +98,35 @@
         span = slice(index * block, (index + 1) * block)
         product = jnp.dot(left[:, span], right[span, :], preferred_element_type=jnp.float32)
         if index == 0:
-            out_ref[...] = product
+            total[...] = product
         else:
-            out_ref[...] += product
+            total[...] += product
+
+    width = out_ref.shape[2]
+    for group in range(out_ref.shape[0] // 2):
+        for side in range(2):
+            device = 2 * group + (core_ref[0] if side == 0 else 1 - core_ref[0])
+            start = (2 * group + side) * pairs
+            for part in range(total.shape[1] // width):
+                out_ref[device, part * pairs : (part + 1) * pairs, :] = total[
+                    start : start + pairs, part * width : (part + 1) * width
+                ]
 
 
-def multiply(lhs, panel):
+def multiply(lhs, panel, core, pairs):
     rows, depth = lhs.shape
     width = panel.shape[1]
     block = 512
     return pl.pallas_call(
-        functools.partial(multiply_kernel, block),
-        out_shape=jax.ShapeDtypeStruct((rows, width), jnp.float32),
-        in_specs=[pl.BlockSpec(memory_space=pl.ANY)] * 2,
+        functools.partial(multiply_kernel, block, pairs),
+        out_shape=jax.ShapeDtypeStruct((rows // pairs, 2 * pairs, width // 2), jnp.float32),
+        in_specs=[pl.BlockSpec(memory_space=pltpu.SMEM)]
+        + [pl.BlockSpec(memory_space=pl.ANY)] * 2,
         out_specs=pl.BlockSpec(memory_space=pltpu.VMEM),
         scratch_shapes=[
             pltpu.VMEM((rows, depth), lhs.dtype),
             pltpu.VMEM((depth, width), panel.dtype),
+            pltpu.VMEM((rows, width), jnp.float32),
             pltpu.SemaphoreType.DMA((depth // block, 2)),
         ],
         compiler_params=pltpu.CompilerParams(vmem_limit_bytes=56 * 1024 * 1024),
@@ -114,7 +136,7 @@
             transcendentals=0,
         ),
         name="multiply",
-    )(lhs, panel)
+    )(core.reshape(1), lhs, panel)
 
 
 def local(amplitudes, integrals, pair_list, block_sizes, occ_energy, virt_energy):
@@ -143,18 +165,14 @@
     own = lax.all_to_all(blocked, ("x", "zlo"), split_axis=0, concat_axis=0, tiled=True)
     other = lax.ppermute(own, "core", SWAP)
     lhs = assemble(own, other, pairs_local)
-    partial_value = multiply(lhs.reshape(groups * size["core"] * pairs_local, -1), panel)
-    partial_value = partial_value.reshape(groups, size["core"] * pairs_local, quarter)
-    pieces = lax.all_to_all(partial_value, ("x", "zlo"), split_axis=0, concat_axis=0, tiled=True)
-    pieces = pieces.reshape(size["x"], size["zlo"], size["core"], pairs_local, quarter)
-    reduced = jnp.sum(pieces, axis=0)
-    mine, theirs = reduced[:, 0], reduced[:, 1]
-    arrived = lax.ppermute(theirs, "core", SWAP)
-    first = lax.axis_index("core") == 0
-    low = jnp.where(first, mine, arrived)
-    high = jnp.where(first, arrived, mine)
-    ladder = jnp.stack([low, high], axis=1).reshape(parts, pairs_local, quarter)
-    ladder = ladder.transpose(1, 0, 2).reshape(pairs_local, out_width)
+    lhs = lhs.reshape(groups * size["core"] * pairs_local, -1)
+    partial_value = multiply(lhs, panel, lax.axis_index("core"), pairs_local)
+    pieces = lax.all_to_all(
+        partial_value, ("x", "zlo", "core"), split_axis=0, concat_axis=0, tiled=True
+    )
+    ladder = jnp.sum(pieces.reshape((size["x"], parts) + pieces.shape[1:]), axis=0)
+    ladder = ladder.reshape(parts, 2, pairs_local, quarter // 2)
+    ladder = ladder.transpose(2, 0, 1, 3).reshape(pairs_local, out_width)
 
     pair_energy = jnp.sum(table_lookup(pair_list, occ_energy, occ_energy.shape[0]), axis=1)
     out_index = jnp.arange(out_width, dtype=jnp.int32)

time: 149 us -> 161 us (1.081)
  Pallas kernels: 6.87 us -> 22.2 us
  starting transfers between devices: 33 us -> 29.1 us
    pallas_call x2, Pallas kernels: 6.32 us -> 21.7 us  [the longest x1 17.1 us: spread_quarters(): pl.pallas_call(functools.partial(spread_kernel, parts), out_shape=jax.Sha...]
    ppermute x1 -> x0, starting transfers between devices: 5 us -> none  [local(): arrived = lax.ppermute(theirs, 'core', SWAP)]
  transfers between devices with their start and end apart: 5 -> 4, of which waited for: 5 -> 4; matrix products, arithmetic and copies ran while one was open for 5% -> 4% of each run, Pallas kernels for 0% -> 0%
where the time goes in v6:
time: 161 us
  blocking collectives  46.6 us (29%)
  waiting for transfers between devices  38.8 us (24%)
  starting transfers between devices  29.1 us (18%)
  Pallas kernels  22.2 us (14%)
  between operations  13.6 us (8%)
  local copies, waits for them, and re-layouts  6.27 us (4%)
  other arithmetic  4.34 us (3%)
    all_to_all x1, blocking collectives, local(): lax.all_to_all(blocked, ('x', 'zlo'), split_axis=0, concat_axis=0, tiled=...  46.6 us
    all_to_all x1, waiting for transfers between devices, local(): lax.all_to_all(partial_value, ('x', 'zlo', 'core'), split_axis=0, concat_...  20.4 us
    all_to_all x1, starting transfers between devices, local(): lax.all_to_all(quarters, ('zhi', 'zlo', 'core'), split_axis=0, concat_axi...  18.2 us
    pallas_call x1, Pallas kernels, spread_quarters(): pl.pallas_call(functools.partial(spread_kernel, parts), out_shape=jax.Sha...  17.1 us
    all_to_all x1, waiting for transfers between devices, local(): lax.all_to_all(quarters, ('zhi', 'zlo', 'core'), split_axis=0, concat_axi...  12.5 us
    all_to_all x1, starting transfers between devices, local(): lax.all_to_all(partial_value, ('x', 'zlo', 'core'), split_axis=0, concat_...  8.91 us
    pallas_call x1, Pallas kernels, multiply(): pl.pallas_call(functools.partial(multiply_kernel, block, pairs), out_shap...  4.53 us
    ppermute x1, waiting for transfers between devices, local(): other = lax.ppermute(own, 'core', SWAP)  3.37 us
  transfers between devices with their start and end apart: 4, of which 4 were waited for; matrix products, arithmetic and copies ran while one was open for 4% of the time, Pallas kernels for 0%

profile of v6, /device:TPU:1, one launch (start us, length us, event | category | flops | bytes accessed | tf_op | source)
XLA Modules:
  0.0 160.9 jit_solution(8745835255440923579)
XLA Ops:
  6.5 17.1 %spread_quarters.1 = bf16[16,32,512]{2,1,0:T(8,128)(2,1)} custom-call(bf16[32,2048]{1,0:T(8,128)(2,1)} %x_ref.1), custom_call_target="tpu_custom_call" | custom-call | bytes 655360 | tf_op jit(solution)/shard_map/spread_quarters/pallas_call | solution.py:39
  23.7 18.2 %all-to-all-start = ((bf16[16,32,512]{2,1,0:T(8,128)(2,1)}), bf16[16,32,512]{2,1,0:T(8,128)(2,1)S(1)}, u32[]{:S(2)}, u32[]{:S(2)}) async-start(bf16[16,32,512]{2,1,0:T(8,128)(2,1)} %spread_quarters.1), calls=%async_computation | async-start | bytes 1048576 | tf_op jit(solution)/shard_map/all_to_all | solution.py:151
  41.9 0.6 fusion.15
  42.5 1.3 fusion.8
  43.8 0.2 broadcast_select_fusion
  44.0 1.6 reshape.102
  45.5 0.6 copy.22
  46.2 0.6 reshape.103
  46.7 12.5 %all-to-all-done = bf16[16,32,512]{2,1,0:T(8,128)(2,1)S(1)} async-done(((bf16[16,32,512]{2,1,0:T(8,128)(2,1)}), bf16[16,32,512]{2,1,0:T(8,128)(2,1)S(1)}, u32[]{:S(2)}, u32[]{:S(2)}) %all-to-all-start) | async-done | bytes 524320 | tf_op jit(solution)/shard_map/all_to_all | solution.py:151
  59.2 0.8 copy-done.1
  60.0 0.2 broadcast_in_dim.72
  60.2 46.6 %all_to_all.15.own_ref = bf16[16,24,2048]{2,1,0:T(8,128)(2,1)S(1)} all-to-all(bf16[16,24,2048]{2,1,0:T(8,128)(2,1)S(1)} %bitcast.15), channel_id=1, replica_groups=mesh['ylo'=4,'x'=8,'yhi'=2,'zhi'=4,'zlo'=2,'core'=2] {'x','zlo'}, dimensions={0} | all-to-all | bytes 3145728 | tf_op jit(solution)/shard_map/all_to_all | solution.py:165
  106.8 1.9 %collective-permute-start = (bf16[16,24,2048]{2,1,0:T(8,128)(2,1)S(1)}, bf16[16,24,2048]{2,1,0:T(8,128)(2,1)S(1)}, u32[]{:S(2)}, u32[]{:S(2)}) collective-permute-start(bf16[16,24,2048]{2,1,0:T(8,128)(2,1)S(1)} %all_to_all.15.own_ref), channel_id=1, source_target_pairs={{0,1},{1,0},{2,3},{3,2},{4,5},{5,4},{6,7},{7,6},{8,9},{9,8},{10,11... | collective-permute-start | bytes 4718600 | tf_op jit(solution)/shard_map/ppermute | solution.py:166
  108.7 3.4 %collective-permute-done.other_ref = bf16[16,24,2048]{2,1,0:T(8,128)(2,1)S(1)} collective-permute-done((bf16[16,24,2048]{2,1,0:T(8,128)(2,1)S(1)}, bf16[16,24,2048]{2,1,0:T(8,128)(2,1)S(1)}, u32[]{:S(2)}, u32[]{:S(2)}) %collective-permute-start) | collective-permute-done | bytes 1572896 | tf_op jit(solution)/shard_map/ppermute | solution.py:166
  112.1 0.5 assemble.1
  112.6 1.7 %copy-done = bf16[16,24,4096]{2,1,0:T(8,128)(2,1)} copy-done((bf16[16,24,4096]{2,1,0:T(8,128)(2,1)}, bf16[16,24,4096]{2,1,0:T(8,128)(2,1)S(1)}, u32[]{:S(2)}) %copy-start) | copy-done | bytes 3145752
  114.3 2.6 %all-gather.2.cloned.1.call-done.panel_ref = bf16[4096,512]{1,0:T(8,128)(2,1)} async-done(((bf16[512,512]{1,0:T(8,128)(2,1)}), bf16[4096,512]{1,0:T(8,128)(2,1)}) %all-gather.2.cloned.1.call-update) | async-done | bytes 4194320 | tf_op jit(solution)/shard_map/all_gather | solution.py:161
  116.9 4.5 %multiply.1 = f32[32,24,256]{2,1,0:T(8,128)} custom-call(s32[1]{0:T(128)} %bitcast.1.core_ref, bf16[384,4096]{1,0:T(8,128)(2,1)} %bitcast.14, bf16[4096,512]{1,0:T(8,128)(2,1)} %all-gather.2.cloned.1.call-done.panel_ref), custom_call_target="tpu_custom_call" | custom-call | flops 1610612736 | bytes 8126464 | tf_op jit(solution)/shard_map/multiply/pallas_call | solution.py:120
  121.5 8.9 %all-to-all-start.2 = ((f32[32,24,256]{2,1,0:T(8,128)}), f32[32,24,256]{2,1,0:T(8,128)S(1)}, u32[]{:S(2)}, u32[]{:S(2)}) async-start(f32[32,24,256]{2,1,0:T(8,128)} %multiply.1), calls=%async_computation.2 | async-start | bytes 1572864 | tf_op jit(solution)/shard_map/all_to_all | solution.py:170
  130.5 0.6 broadcast_compare_fusion
  131.1 0.3 fusion.9
  131.4 1.3 select_reduce_fusion.1
  132.7 20.4 %all-to-all-done.2 = f32[32,24,256]{2,1,0:T(8,128)S(1)} async-done(((f32[32,24,256]{2,1,0:T(8,128)}), f32[32,24,256]{2,1,0:T(8,128)S(1)}, u32[]{:S(2)}, u32[]{:S(2)}) %all-to-all-start.2) | async-done | bytes 786464 | tf_op jit(solution)/shard_map/all_to_all | solution.py:170
  153.3 0.8 divide_select_fusion
  (20 shorter events, 0.4 us)
Async XLA Ops:
  6.5 35.4 %copy-start.3 = (s32[8]{0:T(128)S(1)}, s32[8]{0:T(128)}, u32[]{:S(2)}) copy-start(s32[8]{0:T(128)} %param.9) | copy-start | bytes 100
  6.5 37.2 %copy-start.2 = (bf16[12,32768]{1,0:T(8,128)(2,1)S(1)}, bf16[12,32768]{1,0:T(8,128)(2,1)}, u32[]{:S(2)}) copy-start(bf16[12,32768]{1,0:T(8,128)(2,1)} %param.6) | copy-start | bytes 2359300
  23.7 35.5 %all-to-all-start = ((bf16[16,32,512]{2,1,0:T(8,128)(2,1)}), bf16[16,32,512]{2,1,0:T(8,128)(2,1)S(1)}, u32[]{:S(2)}, u32[]{:S(2)}) async-start(bf16[16,32,512]{2,1,0:T(8,128)(2,1)} %spread_quarters.1), calls=%async_computation | async-start | bytes 1048576 | tf_op jit(solution)/shard_map/all_to_all | solution.py:151
  41.9 75.0 %all-gather.2.cloned.1.call-start = ((), (), s32[]{:S(2)}) async-start(), calls=%async_computation.3 | async-start | bytes 4718592 | tf_op jit(solution)/shard_map/all_gather | solution.py:161
  59.2 0.8 copy-start.1
  106.8 5.3 %collective-permute-start = (bf16[16,24,2048]{2,1,0:T(8,128)(2,1)S(1)}, bf16[16,24,2048]{2,1,0:T(8,128)(2,1)S(1)}, u32[]{:S(2)}, u32[]{:S(2)}) collective-permute-start(bf16[16,24,2048]{2,1,0:T(8,128)(2,1)S(1)} %all_to_all.15.own_ref), channel_id=1, source_target_pairs={{0,1},{1,0},{2,3},{3,2},{4,5},{5,4},{6,7},{7,6},{8,9},{9,8},{10,11... | collective-permute-start | bytes 4718600 | tf_op jit(solution)/shard_map/ppermute | solution.py:166
  112.6 1.7 %copy-start = (bf16[16,24,4096]{2,1,0:T(8,128)(2,1)}, bf16[16,24,4096]{2,1,0:T(8,128)(2,1)S(1)}, u32[]{:S(2)}) copy-start(bf16[16,24,4096]{2,1,0:T(8,128)(2,1)S(1)} %assemble.1) | copy-start | bytes 9437188
  121.5 9.0 %copy-start.4 = (s32[12,2]{0,1:T(2,128)S(1)}, s32[12,2]{0,1:T(2,128)}, u32[]{:S(2)}) copy-start(s32[12,2]{0,1:T(2,128)} %param.8) | copy-start | bytes 292
  121.5 9.6 %copy-start.5 = (f32[200]{0:T(256)S(1)}, f32[200]{0:T(256)}, u32[]{:S(2)}) copy-start(f32[200]{0:T(256)} %param.10) | copy-start | bytes 2404
  121.5 9.9 %copy-start.6 = (f32[128]{0:T(128)S(1)}, f32[128]{0:T(128)}, u32[]{:S(2)}) copy-start(f32[128]{0:T(128)} %param.11) | copy-start | bytes 1540
  121.5 31.5 %all-to-all-start.2 = ((f32[32,24,256]{2,1,0:T(8,128)}), f32[32,24,256]{2,1,0:T(8,128)S(1)}, u32[]{:S(2)}, u32[]{:S(2)}) async-start(f32[32,24,256]{2,1,0:T(8,128)} %multiply.1), calls=%async_computation.2 | async-start | bytes 1572864 | tf_op jit(solution)/shard_map/all_to_all | solution.py:170
Sparse Core Ops, SparseCore 0:
  60.1 56.7 all-gather.1

commit v7 on v6

--- a/solution.py
+++ b/solution.py
@@ -19,29 +19,21 @@
     return jnp.sum(jnp.where(matches, table, jnp.zeros((), table.dtype)), axis=-1)
 
 
-def spread_kernel(parts, x_ref, out_ref, done):
+def spread_kernel(parts, copies, x_ref, out_ref):
     width = out_ref.shape[2]
-    copies = []
-    for index in range(out_ref.shape[0]):
-        start = index % parts * width
-        copies.append(
-            pltpu.make_async_copy(
-                x_ref.at[:, pl.ds(start, width)], out_ref.at[index], done.at[index]
-            )
-        )
-        copies[-1].start()
-    for copy in copies:
-        copy.wait()
+    for part in range(parts):
+        value = x_ref[:, part * width : (part + 1) * width]
+        for copy in range(copies):
+            out_ref[copy * parts + part] = value
 
 
 def spread_quarters(integrals, parts, copies):
     rows, width = integrals.shape
     return pl.pallas_call(
-        functools.partial(spread_kernel, parts),
+        functools.partial(spread_kernel, parts, copies),
         out_shape=jax.ShapeDtypeStruct((parts * copies, rows, width // parts), integrals.dtype),
-        in_specs=[pl.BlockSpec(memory_space=pl.ANY)],
-        out_specs=pl.BlockSpec(memory_space=pl.ANY),
-        scratch_shapes=[pltpu.SemaphoreType.DMA((parts * copies,))],
+        in_specs=[pl.BlockSpec(memory_space=pltpu.VMEM)],
+        out_specs=pl.BlockSpec(memory_space=pltpu.VMEM),
         cost_estimate=pl.CostEstimate(
             flops=0, bytes_accessed=2 * rows * width * (1 + copies), transcendentals=0
         ),
@@ -129,7 +121,7 @@
             pltpu.VMEM((rows, width), jnp.float32),
             pltpu.SemaphoreType.DMA((depth // block, 2)),
         ],
-        compiler_params=pltpu.CompilerParams(vmem_limit_bytes=56 * 1024 * 1024),
+        compiler_params=pltpu.CompilerParams(vmem_limit_bytes=48 * 1024 * 1024),
         cost_estimate=pl.CostEstimate(
             flops=2 * rows * depth * width,
             bytes_accessed=2 * (rows + width) * depth + 4 * rows * width,

time: 161 us -> 146 us (0.907)
  Pallas kernels: 22.2 us -> 5.78 us
  local copies, waits for them, and re-layouts: 6.27 us -> 10.7 us
  waiting for transfers between devices: 38.8 us -> 35.2 us
    pallas_call x1, Pallas kernels: 17.1 us -> 1.82 us  [spread_quarters(): pl.pallas_call(functools.partial(spread_kernel, parts, copies), out_shape...]
    unnamed x15 -> x23, local copies, waits for them, and re-layouts: 2.57 us -> 6.93 us
    all_gather x1, waiting for transfers between devices: 2.63 us -> 0.32 us  [local(): lax.all_gather(rows.reshape(stripe, quarter), RING, axis=0, tiled=True)]
  transfers between devices with their start and end apart: 4 -> 4, of which waited for: 4 -> 4; matrix products, arithmetic and copies ran while one was open for 4% -> 5% of each run, Pallas kernels for 0% -> 0%
where the time goes in v7:
time: 146 us; the launch traced here: 145 us
  blocking collectives  46.6 us (32%)
  waiting for transfers between devices  35.2 us (24%)
  starting transfers between devices  29 us (20%)
  between operations  13.6 us (9%)
  local copies, waits for them, and re-layouts  10.7 us (7%)
  Pallas kernels  5.78 us (4%)
  other arithmetic  4.43 us (3%)
    all_to_all x1, blocking collectives, local(): lax.all_to_all(blocked, ('x', 'zlo'), split_axis=0, concat_axis=0, tiled=...  46.6 us
    all_to_all x1, waiting for transfers between devices, local(): lax.all_to_all(partial_value, ('x', 'zlo', 'core'), split_axis=0, concat_...  20.3 us
    all_to_all x1, starting transfers between devices, local(): lax.all_to_all(quarters, ('zhi', 'zlo', 'core'), split_axis=0, concat_axi...  18.2 us
    all_to_all x1, waiting for transfers between devices, local(): lax.all_to_all(quarters, ('zhi', 'zlo', 'core'), split_axis=0, concat_axi...  12.4 us
    all_to_all x1, starting transfers between devices, local(): lax.all_to_all(partial_value, ('x', 'zlo', 'core'), split_axis=0, concat_...  8.89 us
    unnamed x23, local copies, waits for them, and re-layouts  6.93 us
    pallas_call x1, Pallas kernels, multiply(): pl.pallas_call(functools.partial(multiply_kernel, block, pairs), out_shap...  3.42 us
  transfers between devices with their start and end apart: 4, of which 4 were waited for; matrix products, arithmetic and copies ran while one was open for 5% of the time, Pallas kernels for 0%

profile of v7, /device:TPU:1, one launch (start us, length us, event | category | flops | bytes accessed | tf_op | source)
XLA Modules:
  0.0 145.3 jit_solution(13130497886861633149)
XLA Ops:
  6.5 1.8 %spread_quarters.1 = bf16[16,32,512]{2,1,0:T(8,128)(2,1)} custom-call(bf16[32,2048]{1,0:T(8,128)(2,1)} %x_ref.1), custom_call_target="tpu_custom_call" | custom-call | bytes 655360 | tf_op jit(solution)/shard_map/spread_quarters/pallas_call | solution.py:32
  8.4 18.2 %all-to-all-start = ((bf16[16,32,512]{2,1,0:T(8,128)(2,1)}), bf16[16,32,512]{2,1,0:T(8,128)(2,1)S(1)}, u32[]{:S(2)}, u32[]{:S(2)}) async-start(bf16[16,32,512]{2,1,0:T(8,128)(2,1)} %spread_quarters.1), calls=%async_computation | async-start | bytes 1048576 | tf_op jit(solution)/shard_map/all_to_all | solution.py:143
  26.6 0.7 fusion.15
  27.3 1.3 fusion.8
  28.7 1.6 %reshape.102 = bf16[12,4,8,2,512]{4,3,2,1,0:T(2,128)(2,1)S(1)} reshape(bf16[12,32768]{1,0:T(8,128)(2,1)S(1)} %broadcast_select_fusion) | data formatting | bytes 1572864 | tf_op jit(solution)/shard_map/reshape | solution.py:149
  30.3 0.6 copy.22
  30.9 0.6 reshape.103
  31.5 12.4 %all-to-all-done = bf16[16,32,512]{2,1,0:T(8,128)(2,1)S(1)} async-done(((bf16[16,32,512]{2,1,0:T(8,128)(2,1)}), bf16[16,32,512]{2,1,0:T(8,128)(2,1)S(1)}, u32[]{:S(2)}, u32[]{:S(2)}) %all-to-all-start) | async-done | bytes 524320 | tf_op jit(solution)/shard_map/all_to_all | solution.py:143
  43.9 0.8 copy-done.5
  44.9 46.6 %all_to_all.15.own_ref = bf16[16,24,2048]{2,1,0:T(8,128)(2,1)S(1)} all-to-all(bf16[16,24,2048]{2,1,0:T(8,128)(2,1)S(1)} %bitcast.15), channel_id=1, replica_groups=mesh['ylo'=4,'x'=8,'yhi'=2,'zhi'=4,'zlo'=2,'core'=2] {'x','zlo'}, dimensions={0} | all-to-all | bytes 3145728 | tf_op jit(solution)/shard_map/all_to_all | solution.py:157
  91.5 1.9 %collective-permute-start = (bf16[16,24,2048]{2,1,0:T(8,128)(2,1)S(1)}, bf16[16,24,2048]{2,1,0:T(8,128)(2,1)S(1)}, u32[]{:S(2)}, u32[]{:S(2)}) collective-permute-start(bf16[16,24,2048]{2,1,0:T(8,128)(2,1)S(1)} %all_to_all.15.own_ref), channel_id=1, source_target_pairs={{0,1},{1,0},{2,3},{3,2},{4,5},{5,4},{6,7},{7,6},{8,9},{9,8},{10,11... | collective-permute-start | bytes 4718600 | tf_op jit(solution)/shard_map/ppermute | solution.py:158
  93.4 1.2 copy-done
  94.6 2.2 %collective-permute-done.other_ref = bf16[16,24,2048]{2,1,0:T(8,128)(2,1)S(1)} collective-permute-done((bf16[16,24,2048]{2,1,0:T(8,128)(2,1)S(1)}, bf16[16,24,2048]{2,1,0:T(8,128)(2,1)S(1)}, u32[]{:S(2)}, u32[]{:S(2)}) %collective-permute-start) | collective-permute-done | bytes 1572896 | tf_op jit(solution)/shard_map/ppermute | solution.py:158
  96.8 1.2 copy-done.3
  97.9 1.4 copy-done.1
  99.3 1.4 copy-done.4
  100.8 0.5 assemble.1
  101.6 3.4 %multiply.1 = f32[32,24,256]{2,1,0:T(8,128)S(1)} custom-call(s32[1]{0:T(128)} %bitcast.1.core_ref, bf16[384,4096]{1,0:T(8,128)(2,1)S(1)} %bitcast.14, bf16[4096,512]{1,0:T(8,128)(2,1)} %all-gather.2.cloned.1.call-done.panel_ref), custom_call_target="tpu_custom_call" | custom-call | flops 1610612736 | bytes 8126464 | tf_op jit(solution)/shard_map/multiply/pallas_call | solution.py:112
  105.1 0.9 copy-done.2
  105.9 8.9 %all-to-all-start.2 = ((f32[32,24,256]{2,1,0:T(8,128)}), f32[32,24,256]{2,1,0:T(8,128)S(1)}, u32[]{:S(2)}, u32[]{:S(2)}) async-start(f32[32,24,256]{2,1,0:T(8,128)} %copy-done.2), calls=%async_computation.2 | async-start | bytes 1572864 | tf_op jit(solution)/shard_map/all_to_all | solution.py:162
  114.9 0.6 broadcast_compare_fusion
  115.9 1.3 select_reduce_fusion.1
  117.1 20.3 %all-to-all-done.2 = f32[32,24,256]{2,1,0:T(8,128)S(1)} async-done(((f32[32,24,256]{2,1,0:T(8,128)}), f32[32,24,256]{2,1,0:T(8,128)S(1)}, u32[]{:S(2)}, u32[]{:S(2)}) %all-to-all-start.2) | async-done | bytes 786464 | tf_op jit(solution)/shard_map/all_to_all | solution.py:162
  137.7 0.8 divide_select_fusion
  (28 shorter events, 1.4 us)
Async XLA Ops:
  6.5 20.1 %copy-start.7 = (s32[8]{0:T(128)S(1)}, s32[8]{0:T(128)}, u32[]{:S(2)}) copy-start(s32[8]{0:T(128)} %param.9) | copy-start | bytes 100
  6.5 22.0 %copy-start.6 = (bf16[12,32768]{1,0:T(8,128)(2,1)S(1)}, bf16[12,32768]{1,0:T(8,128)(2,1)}, u32[]{:S(2)}) copy-start(bf16[12,32768]{1,0:T(8,128)(2,1)} %param.6) | copy-start | bytes 2359300
  8.4 35.5 %all-to-all-start = ((bf16[16,32,512]{2,1,0:T(8,128)(2,1)}), bf16[16,32,512]{2,1,0:T(8,128)(2,1)S(1)}, u32[]{:S(2)}, u32[]{:S(2)}) async-start(bf16[16,32,512]{2,1,0:T(8,128)(2,1)} %spread_quarters.1), calls=%async_computation | async-start | bytes 1048576 | tf_op jit(solution)/shard_map/all_to_all | solution.py:143
  26.6 75.1 %all-gather.2.cloned.1.call-start = ((), (), s32[]{:S(2)}) async-start(), calls=%async_computation.3 | async-start | bytes 4718592 | tf_op jit(solution)/shard_map/all_gather | solution.py:153
  43.9 0.8 copy-start.5
  91.5 5.3 %collective-permute-start = (bf16[16,24,2048]{2,1,0:T(8,128)(2,1)S(1)}, bf16[16,24,2048]{2,1,0:T(8,128)(2,1)S(1)}, u32[]{:S(2)}, u32[]{:S(2)}) collective-permute-start(bf16[16,24,2048]{2,1,0:T(8,128)(2,1)S(1)} %all_to_all.15.own_ref), channel_id=1, source_target_pairs={{0,1},{1,0},{2,3},{3,2},{4,5},{5,4},{6,7},{7,6},{8,9},{9,8},{10,11... | collective-permute-start | bytes 4718600 | tf_op jit(solution)/shard_map/ppermute | solution.py:158
  93.4 1.2 copy-start
  96.8 1.2 copy-start.3
  97.9 1.4 copy-start.1
  99.3 1.4 copy-start.4
  105.0 0.9 copy-start.2
  105.9 8.9 %copy-start.8 = (s32[12,2]{0,1:T(2,128)S(1)}, s32[12,2]{0,1:T(2,128)}, u32[]{:S(2)}) copy-start(s32[12,2]{0,1:T(2,128)} %param.8) | copy-start | bytes 292
  105.9 9.7 %copy-start.9 = (f32[200]{0:T(256)S(1)}, f32[200]{0:T(256)}, u32[]{:S(2)}) copy-start(f32[200]{0:T(256)} %param.10) | copy-start | bytes 2404
  105.9 9.9 %copy-start.10 = (f32[128]{0:T(128)S(1)}, f32[128]{0:T(128)}, u32[]{:S(2)}) copy-start(f32[128]{0:T(128)} %param.11) | copy-start | bytes 1540
  105.9 31.5 %all-to-all-start.2 = ((f32[32,24,256]{2,1,0:T(8,128)}), f32[32,24,256]{2,1,0:T(8,128)S(1)}, u32[]{:S(2)}, u32[]{:S(2)}) async-start(f32[32,24,256]{2,1,0:T(8,128)} %copy-done.2), calls=%async_computation.2 | async-start | bytes 1572864 | tf_op jit(solution)/shard_map/all_to_all | solution.py:162
Sparse Core Ops, SparseCore 0:
  44.8 56.7 all-gather.1

commit v8 on v7

--- a/solution.py
+++ b/solution.py
@@ -10,7 +10,6 @@
 NIRREP = 8
 NV = 128
 AXES = ("ylo", "x", "yhi", "zhi", "zlo", "core")
-RING = ("yhi", "ylo")
 SWAP = [(0, 1), (1, 0)]
 
 
@@ -63,7 +62,7 @@
         out_shape=jax.ShapeDtypeStruct((groups, 2 * pairs, halves * depth), own.dtype),
         in_specs=[block, block],
         out_specs=pl.BlockSpec((4, 2 * pairs, halves * depth), lambda g: (g, 0, 0)),
-        compiler_params=pltpu.CompilerParams(vmem_limit_bytes=16 * 1024 * 1024),
+        compiler_params=pltpu.CompilerParams(vmem_limit_bytes=8 * 1024 * 1024),
         cost_estimate=pl.CostEstimate(
             flops=2 * own.size, bytes_accessed=8 * own.size, transcendentals=0
         ),
@@ -71,28 +70,34 @@
     )(own, other)
 
 
+def ring_move(yhi, ylo, value, shift):
+    length = yhi * ylo
+
+    def flat(place):
+        return place % length % ylo * yhi + place % length // ylo
+
+    pairs = [(flat(place), flat(place + shift)) for place in range(length)]
+    return lax.ppermute(value, ("ylo", "yhi"), pairs)
+
+
 def multiply_kernel(
-    block, pairs, core_ref, lhs_ref, panel_ref, out_ref, left, right, total, arrived
+    order, length, pairs, place_ref, core_ref, lhs_ref, *refs
 ):
-    copies = []
-    for index, start in enumerate(range(0, panel_ref.shape[0], block)):
-        span = pl.ds(start, block)
-        pair = (
-            pltpu.make_async_copy(lhs_ref.at[:, span], left.at[:, span], arrived.at[index, 0]),
-            pltpu.make_async_copy(panel_ref.at[span], right.at[span], arrived.at[index, 1]),
-        )
-        for copy in pair:
-            copy.start()
-        copies.append(pair)
-    for index, pair in enumerate(copies):
-        for copy in pair:
-            copy.wait()
-        span = slice(index * block, (index + 1) * block)
-        product = jnp.dot(left[:, span], right[span, :], preferred_element_type=jnp.float32)
-        if index == 0:
-            total[...] = product
+    near_refs, far_refs, (out_ref, total) = refs[: len(order)], refs[len(order) : -2], refs[-2:]
+    stripe = near_refs[0].shape[0]
+    entries = [(0, shift, ref) for shift, ref in zip(order, near_refs)]
+    entries += [
+        (index * ref.shape[1], length // 2, ref) for index, ref in enumerate(far_refs)
+    ]
+    for column, shift, block_ref in entries:
+        source = lax.rem(place_ref[0] - shift + length, length)
+        lanes = pl.ds(pl.multiple_of(source * stripe, stripe), stripe)
+        product = jnp.dot(lhs_ref[:, lanes], block_ref[...], preferred_element_type=jnp.float32)
+        columns = slice(column, column + block_ref.shape[1])
+        if shift == 0:
+            total[:, columns] = product
         else:
-            total[...] += product
+            total[:, columns] += product
 
     width = out_ref.shape[2]
     for group in range(out_ref.shape[0] // 2):
@@ -105,30 +110,24 @@
                 ]
 
 
-def multiply(lhs, panel, core, pairs):
+def multiply(lhs, near, far, order, length, place, core, pairs):
     rows, depth = lhs.shape
-    width = panel.shape[1]
-    block = 512
+    width = near[0].shape[1]
     return pl.pallas_call(
-        functools.partial(multiply_kernel, block, pairs),
+        functools.partial(multiply_kernel, order, length, pairs),
         out_shape=jax.ShapeDtypeStruct((rows // pairs, 2 * pairs, width // 2), jnp.float32),
-        in_specs=[pl.BlockSpec(memory_space=pltpu.SMEM)]
-        + [pl.BlockSpec(memory_space=pl.ANY)] * 2,
+        in_specs=[pl.BlockSpec(memory_space=pltpu.SMEM)] * 2
+        + [pl.BlockSpec(memory_space=pltpu.VMEM)] * (1 + len(near) + len(far)),
         out_specs=pl.BlockSpec(memory_space=pltpu.VMEM),
-        scratch_shapes=[
-            pltpu.VMEM((rows, depth), lhs.dtype),
-            pltpu.VMEM((depth, width), panel.dtype),
-            pltpu.VMEM((rows, width), jnp.float32),
-            pltpu.SemaphoreType.DMA((depth // block, 2)),
-        ],
-        compiler_params=pltpu.CompilerParams(vmem_limit_bytes=48 * 1024 * 1024),
+        scratch_shapes=[pltpu.VMEM((rows, width), jnp.float32)],
+        compiler_params=pltpu.CompilerParams(vmem_limit_bytes=12 * 1024 * 1024),
         cost_estimate=pl.CostEstimate(
             flops=2 * rows * depth * width,
             bytes_accessed=2 * (rows + width) * depth + 4 * rows * width,
             transcendentals=0,
         ),
         name="multiply",
-    )(core.reshape(1), lhs, panel)
+    )(place.reshape(1), core.reshape(1), lhs, *near, *far)
 
 
 def local(amplitudes, integrals, pair_list, block_sizes, occ_energy, virt_energy):
@@ -150,15 +149,26 @@
     blocked = blocked.transpose(2, 3, 0, 1, 4)
     blocked = blocked.reshape(size["x"], size["yhi"] * pairs_local, size["ylo"] * stripe)
     rows, blocked = lax.optimization_barrier((rows, blocked))
-    panel = lax.all_gather(rows.reshape(stripe, quarter), RING, axis=0, tiled=True)
     groups = size["x"] * size["zlo"]
     blocked = jnp.broadcast_to(blocked[:, None], (size["x"], size["zlo"]) + blocked.shape[1:])
     blocked = blocked.reshape((groups,) + blocked.shape[2:])
     own = lax.all_to_all(blocked, ("x", "zlo"), split_axis=0, concat_axis=0, tiled=True)
+    length = size["yhi"] * size["ylo"]
+    move = functools.partial(ring_move, size["yhi"], size["ylo"])
+    ring = {0: rows.reshape(stripe, quarter)}
+    for step in range(1, length // 2):
+        for sign in (1, -1):
+            ring[sign * step] = move(ring[sign * (step - 1)], sign)
+    order = sorted(ring, key=abs)
+    near = [ring[shift] for shift in order]
+    ends = (ring[length // 2 - 1][:, : quarter // 2], ring[1 - length // 2][:, quarter // 2 :])
+    own, ends = lax.optimization_barrier((own, ends))
+    far = [move(end, sign) for end, sign in zip(ends, (1, -1))]
     other = lax.ppermute(own, "core", SWAP)
     lhs = assemble(own, other, pairs_local)
     lhs = lhs.reshape(groups * size["core"] * pairs_local, -1)
-    partial_value = multiply(lhs, panel, lax.axis_index("core"), pairs_local)
+    place = lax.axis_index("yhi") * size["ylo"] + lax.axis_index("ylo")
+    partial_value = multiply(lhs, near, far, order, length, place, lax.axis_index("core"), pairs_local)
     pieces = lax.all_to_all(
         partial_value, ("x", "zlo", "core"), split_axis=0, concat_axis=0, tiled=True
     )

time: 146 us -> 154 us (1.055)
  blocking collectives: 46.6 us -> 0 us
  starting transfers between devices: 29 us -> 65.3 us
  waiting for transfers between devices: 35.2 us -> 65.3 us
  between operations: 13.6 us -> 0.3 us
  Pallas kernels: 5.78 us -> 8.07 us
  local copies, waits for them, and re-layouts: 10.7 us -> 8.93 us
    all_to_all x1 -> x0, blocking collectives: 46.6 us -> none  [local(): lax.all_to_all(blocked, ('x', 'zlo'), split_axis=0, concat_axis=0, tiled=...]
    ppermute x0 -> x8, waiting for transfers between devices: none -> 32.6 us  [ring_move(): return lax.ppermute(value, ('ylo', 'yhi'), pairs)]
    ppermute x0 -> x8, starting transfers between devices: none -> 28 us  [ring_move(): return lax.ppermute(value, ('ylo', 'yhi'), pairs)]
    all_to_all x0 -> x1, starting transfers between devices: none -> 6.58 us  [local(): lax.all_to_all(blocked, ('x', 'zlo'), split_axis=0, concat_axis=0, tiled=...]
    unnamed x23 -> x27, local copies, waits for them, and re-layouts: 6.93 us -> 2.53 us
    ppermute x1, waiting for transfers between devices: 2.2 us -> 0.01 us  [local(): other = lax.ppermute(own, 'core', SWAP)]
    pallas_call x1, Pallas kernels: 0.54 us -> 2.58 us  [assemble(): pl.pallas_call(functools.partial(assemble_kernel, pairs), grid=(groups //...]
    ppermute x1, starting transfers between devices: 1.91 us -> 3.63 us  [local(): other = lax.ppermute(own, 'core', SWAP)]
  transfers between devices with their start and end apart: 4 -> 12, of which waited for: 4 -> 8; matrix products, arithmetic and copies ran while one was open for 5% -> 6% of each run, Pallas kernels for 0% -> 2%
where the time goes in v8:
time: 154 us; the launch traced here: 152 us
  starting transfers between devices  65.3 us (42%)
  waiting for transfers between devices  65.3 us (42%)
  local copies, waits for them, and re-layouts  8.93 us (6%)
  Pallas kernels  8.07 us (5%)
  other arithmetic  4.49 us (3%)
    ppermute x8, waiting for transfers between devices, ring_move(): return lax.ppermute(value, ('ylo', 'yhi'), pairs)  32.6 us
    ppermute x8, starting transfers between devices, ring_move(): return lax.ppermute(value, ('ylo', 'yhi'), pairs)  28 us
    all_to_all x1, waiting for transfers between devices, local(): lax.all_to_all(partial_value, ('x', 'zlo', 'core'), split_axis=0, concat_...  20.3 us
    all_to_all x1, starting transfers between devices, local(): lax.all_to_all(quarters, ('zhi', 'zlo', 'core'), split_axis=0, concat_axi...  18.2 us
    all_to_all x1, waiting for transfers between devices, local(): lax.all_to_all(quarters, ('zhi', 'zlo', 'core'), split_axis=0, concat_axi...  12.4 us
    all_to_all x1, starting transfers between devices, local(): lax.all_to_all(partial_value, ('x', 'zlo', 'core'), split_axis=0, concat_...  8.85 us
    all_to_all x1, starting transfers between devices, local(): lax.all_to_all(blocked, ('x', 'zlo'), split_axis=0, concat_axis=0, tiled=...  6.58 us
    pallas_call x1, Pallas kernels, multiply(): pl.pallas_call(functools.partial(multiply_kernel, order, length, pairs),...  3.67 us
  transfers between devices with their start and end apart: 12, of which 8 were waited for; matrix products, arithmetic and copies ran while one was open for 6% of the time, Pallas kernels for 2%

profile of v8, /device:TPU:1, one launch (start us, length us, event | category | flops | bytes accessed | tf_op | source)
XLA Modules:
  0.0 152.3 jit_solution(6570108663887732838)
XLA Ops:
  0.0 1.8 %spread_quarters.1 = bf16[16,32,512]{2,1,0:T(8,128)(2,1)} custom-call(bf16[32,2048]{1,0:T(8,128)(2,1)} %x_ref.1), custom_call_target="tpu_custom_call" | custom-call | bytes 655360 | tf_op jit(solution)/shard_map/spread_quarters/pallas_call | solution.py:31
  1.8 18.2 %all-to-all-start = ((bf16[16,32,512]{2,1,0:T(8,128)(2,1)}), bf16[16,32,512]{2,1,0:T(8,128)(2,1)S(1)}, u32[]{:S(2)}, u32[]{:S(2)}) async-start(bf16[16,32,512]{2,1,0:T(8,128)(2,1)} %spread_quarters.1), calls=%async_computation | async-start | bytes 1048576 | tf_op jit(solution)/shard_map/all_to_all | solution.py:142
  22.2 1.6 %reshape.106 = bf16[12,4,8,2,512]{4,3,2,1,0:T(2,128)(2,1)S(1)} reshape(bf16[12,32768]{1,0:T(8,128)(2,1)S(1)} %broadcast_select_fusion) | data formatting | bytes 1572864 | tf_op jit(solution)/shard_map/reshape | solution.py:148
  25.0 12.4 %all-to-all-done = bf16[16,32,512]{2,1,0:T(8,128)(2,1)S(1)} async-done(((bf16[16,32,512]{2,1,0:T(8,128)(2,1)}), bf16[16,32,512]{2,1,0:T(8,128)(2,1)S(1)}, u32[]{:S(2)}, u32[]{:S(2)}) %all-to-all-start) | async-done | bytes 524320 | tf_op jit(solution)/shard_map/all_to_all | solution.py:142
  37.4 1.4 broadcast_in_dim.72
  38.7 6.6 %all-to-all-start.1 = ((bf16[16,24,2048]{2,1,0:T(8,128)(2,1)}), bf16[16,24,2048]{2,1,0:T(8,128)(2,1)S(1)}, u32[]{:S(2)}, u32[]{:S(2)}) async-start(bf16[16,24,2048]{2,1,0:T(8,128)(2,1)} %bitcast.19), calls=%async_computation.1 | async-start | bytes 3145728 | tf_op jit(solution)/shard_map/all_to_all | solution.py:155
  45.3 3.3 %collective-permute-start = (bf16[512,512]{1,0:T(8,128)(2,1)S(1)}, bf16[512,512]{1,0:T(8,128)(2,1)S(1)}, u32[]{:S(2)}, u32[]{:S(2)}) collective-permute-start(bf16[512,512]{1,0:T(8,128)(2,1)S(1)} %bitcast.16), channel_id=1, source_target_pairs={{0,256},{256,512},{512,768},{768,16},{16,272},{272,528},{528,784},... | collective-permute-start | bytes 1572872 | tf_op jit(solution)/shard_map/ppermute | solution.py:80
  48.6 4.5 %collective-permute-start.3 = (bf16[512,512]{1,0:T(8,128)(2,1)S(1)}, bf16[512,512]{1,0:T(8,128)(2,1)S(1)}, u32[]{:S(2)}, u32[]{:S(2)}) collective-permute-start(bf16[512,512]{1,0:T(8,128)(2,1)S(1)} %bitcast.17), channel_id=1, source_target_pairs={{0,784},{256,0},{512,256},{768,512},{16,768},{272,16},{528,272},{7... | collective-permute-start | bytes 1572872 | tf_op jit(solution)/shard_map/ppermute | solution.py:80
  53.1 9.8 %collective-permute-done.refs_1_ = bf16[512,512]{1,0:T(8,128)(2,1)S(1)} collective-permute-done((bf16[512,512]{1,0:T(8,128)(2,1)S(1)}, bf16[512,512]{1,0:T(8,128)(2,1)S(1)}, u32[]{:S(2)}, u32[]{:S(2)}) %collective-permute-start) | collective-permute-done | bytes 524320 | tf_op jit(solution)/shard_map/ppermute | solution.py:80
  62.9 1.9 %collective-permute-start.1 = (bf16[512,512]{1,0:T(8,128)(2,1)S(1)}, bf16[512,512]{1,0:T(8,128)(2,1)S(1)}, u32[]{:S(2)}, u32[]{:S(2)}) collective-permute-start(bf16[512,512]{1,0:T(8,128)(2,1)S(1)} %collective-permute-done.refs_1_), channel_id=1, source_target_pairs={{0,256},{256,512},{512,768},{768,16},{16,272},{272,528},{528,784},... | collective-permute-start | bytes 1572872 | tf_op jit(solution)/shard_map/ppermute | solution.py:80
  65.7 4.6 %collective-permute-start.4 = (bf16[512,512]{1,0:T(8,128)(2,1)S(1)}, bf16[512,512]{1,0:T(8,128)(2,1)S(1)}, u32[]{:S(2)}, u32[]{:S(2)}) collective-permute-start(bf16[512,512]{1,0:T(8,128)(2,1)S(1)} %collective-permute-done.3.refs_2_), channel_id=1, source_target_pairs={{0,784},{256,0},{512,256},{768,512},{16,768},{272,16},{528,272},{7... | collective-permute-start | bytes 1572872 | tf_op jit(solution)/shard_map/ppermute | solution.py:80
  71.1 8.8 %collective-permute-done.1.refs_3_ = bf16[512,512]{1,0:T(8,128)(2,1)S(1)} collective-permute-done((bf16[512,512]{1,0:T(8,128)(2,1)S(1)}, bf16[512,512]{1,0:T(8,128)(2,1)S(1)}, u32[]{:S(2)}, u32[]{:S(2)}) %collective-permute-start.1) | collective-permute-done | bytes 524320 | tf_op jit(solution)/shard_map/ppermute | solution.py:80
  79.8 1.9 %collective-permute-start.2 = (bf16[512,512]{1,0:T(8,128)(2,1)S(1)}, bf16[512,512]{1,0:T(8,128)(2,1)S(1)}, u32[]{:S(2)}, u32[]{:S(2)}) collective-permute-start(bf16[512,512]{1,0:T(8,128)(2,1)S(1)} %collective-permute-done.1.refs_3_), channel_id=1, source_target_pairs={{0,256},{256,512},{512,768},{768,16},{16,272},{272,528},{528,784},... | collective-permute-start | bytes 1572872 | tf_op jit(solution)/shard_map/ppermute | solution.py:80
  82.5 4.6 %collective-permute-start.5 = (bf16[512,512]{1,0:T(8,128)(2,1)S(1)}, bf16[512,512]{1,0:T(8,128)(2,1)S(1)}, u32[]{:S(2)}, u32[]{:S(2)}) collective-permute-start(bf16[512,512]{1,0:T(8,128)(2,1)S(1)} %collective-permute-done.4.refs_4_), channel_id=1, source_target_pairs={{0,784},{256,0},{512,256},{768,512},{16,768},{272,16},{528,272},{7... | collective-permute-start | bytes 1572872 | tf_op jit(solution)/shard_map/ppermute | solution.py:80
  87.1 8.7 %collective-permute-done.2.refs_5_ = bf16[512,512]{1,0:T(8,128)(2,1)S(1)} collective-permute-done((bf16[512,512]{1,0:T(8,128)(2,1)S(1)}, bf16[512,512]{1,0:T(8,128)(2,1)S(1)}, u32[]{:S(2)}, u32[]{:S(2)}) %collective-permute-start.2) | collective-permute-done | bytes 524320 | tf_op jit(solution)/shard_map/ppermute | solution.py:80
  98.2 3.6 %collective-permute-start.6 = (bf16[16,24,2048]{2,1,0:T(8,128)(2,1)S(1)}, bf16[16,24,2048]{2,1,0:T(8,128)(2,1)}, u32[]{:S(2)}, u32[]{:S(2)}) collective-permute-start(bf16[16,24,2048]{2,1,0:T(8,128)(2,1)S(1)} %all-to-all-done.1.own_ref), channel_id=1, source_target_pairs={{0,1},{1,0},{2,3},{3,2},{4,5},{5,4},{6,7},{7,6},{8,9},{9,8},{10,11... | collective-permute-start | bytes 4718600 | tf_op jit(solution)/shard_map/ppermute | solution.py:167
  101.9 2.9 %collective-permute-start.7 = (bf16[512,256]{1,0:T(8,128)(2,1)}, bf16[512,256]{1,0:T(8,128)(2,1)S(1)}, u32[]{:S(2)}, u32[]{:S(2)}) collective-permute-start(bf16[512,256]{1,0:T(8,128)(2,1)} %slice.20), channel_id=1, source_target_pairs={{0,256},{256,512},{512,768},{768,16},{16,272},{272,528},{528,784},... | collective-permute-start | bytes 786440 | tf_op jit(solution)/shard_map/ppermute | solution.py:80
  104.8 4.3 %collective-permute-start.8 = (bf16[512,256]{1,0:T(8,128)(2,1)}, bf16[512,256]{1,0:T(8,128)(2,1)}, u32[]{:S(2)}, u32[]{:S(2)}) collective-permute-start(bf16[512,256]{1,0:T(8,128)(2,1)} %slice.21), channel_id=1, source_target_pairs={{0,784},{256,0},{512,256},{768,512},{16,768},{272,16},{528,272},{7... | collective-permute-start | bytes 786440 | tf_op jit(solution)/shard_map/ppermute | solution.py:80
  109.2 2.6 %assemble.1 = bf16[16,24,4096]{2,1,0:T(8,128)(2,1)S(1)} custom-call(bf16[16,24,2048]{2,1,0:T(8,128)(2,1)S(1)} %all-to-all-done.1.own_ref, bf16[16,24,2048]{2,1,0:T(8,128)(2,1)} %collective-permute-done.6.other_ref), custom_call_target="tpu_custom_call" | custom-call | flops 1572864 | bytes 6291456 | tf_op jit(solution)/shard_map/assemble/pallas_call | solution.py:59
  111.8 2.3 %collective-permute-done.7.refs_7_ = bf16[512,256]{1,0:T(8,128)(2,1)S(1)} collective-permute-done((bf16[512,256]{1,0:T(8,128)(2,1)}, bf16[512,256]{1,0:T(8,128)(2,1)S(1)}, u32[]{:S(2)}, u32[]{:S(2)}) %collective-permute-start.7) | collective-permute-done | bytes 262176 | tf_op jit(solution)/shard_map/ppermute | solution.py:80
  114.1 2.0 %collective-permute-done.8.refs_8_ = bf16[512,256]{1,0:T(8,128)(2,1)} collective-permute-done((bf16[512,256]{1,0:T(8,128)(2,1)}, bf16[512,256]{1,0:T(8,128)(2,1)}, u32[]{:S(2)}, u32[]{:S(2)}) %collective-permute-start.8) | collective-permute-done | bytes 262176 | tf_op jit(solution)/shard_map/ppermute | solution.py:80
  116.1 3.7 %multiply.1 = f32[32,24,256]{2,1,0:T(8,128)} custom-call(s32[1]{0:T(128)} %bitcast.1.place_ref, s32[1]{0:T(128)} %bitcast.2.core_ref, bf16[384,4096]{1,0:T(8,128)(2,1)S(1)} %bitcast.15, bf16[512,512]{1,0:T(8,128)(2,1)S(1)} %bitcast.18, bf16[512,512]{1,0:T(8,128)(2,1)S(1)} %copy-done.1, bf16[512,512]{1,0:T(8,128)(2,1)S(1)} %copy-done.3, ...), custom_call_target="tpu_custom_call" | custom-call | flops 1610612736 | bytes 8126464 | tf_op jit(solution)/shard_map/multiply/pallas_call | solution.py:116
  119.8 8.9 %all-to-all-start.2 = ((f32[32,24,256]{2,1,0:T(8,128)}), f32[32,24,256]{2,1,0:T(8,128)S(1)}, u32[]{:S(2)}, u32[]{:S(2)}) async-start(f32[32,24,256]{2,1,0:T(8,128)} %multiply.1), calls=%async_computation.2 | async-start | bytes 1572864 | tf_op jit(solution)/shard_map/all_to_all | solution.py:172
  131.0 20.3 %all-to-all-done.2 = f32[32,24,256]{2,1,0:T(8,128)S(1)} async-done(((f32[32,24,256]{2,1,0:T(8,128)}), f32[32,24,256]{2,1,0:T(8,128)S(1)}, u32[]{:S(2)}, u32[]{:S(2)}) %all-to-all-start.2) | async-done | bytes 786464 | tf_op jit(solution)/shard_map/all_to_all | solution.py:172
  (48 shorter events, 11.5 us)
Async XLA Ops:
  0.0 20.0 %copy-start.9 = (s32[8]{0:T(128)S(1)}, s32[8]{0:T(128)}, u32[]{:S(2)}) copy-start(s32[8]{0:T(128)} %param.9) | copy-start | bytes 100
  0.0 22.0 %copy-start.8 = (bf16[12,32768]{1,0:T(8,128)(2,1)S(1)}, bf16[12,32768]{1,0:T(8,128)(2,1)}, u32[]{:S(2)}) copy-start(bf16[12,32768]{1,0:T(8,128)(2,1)} %param.6) | copy-start | bytes 2359300
  1.8 35.5 %all-to-all-start = ((bf16[16,32,512]{2,1,0:T(8,128)(2,1)}), bf16[16,32,512]{2,1,0:T(8,128)(2,1)S(1)}, u32[]{:S(2)}, u32[]{:S(2)}) async-start(bf16[16,32,512]{2,1,0:T(8,128)(2,1)} %spread_quarters.1), calls=%async_computation | async-start | bytes 1048576 | tf_op jit(solution)/shard_map/all_to_all | solution.py:142
  38.7 59.5 %all-to-all-start.1 = ((bf16[16,24,2048]{2,1,0:T(8,128)(2,1)}), bf16[16,24,2048]{2,1,0:T(8,128)(2,1)S(1)}, u32[]{:S(2)}, u32[]{:S(2)}) async-start(bf16[16,24,2048]{2,1,0:T(8,128)(2,1)} %bitcast.19), calls=%async_computation.1 | async-start | bytes 3145728 | tf_op jit(solution)/shard_map/all_to_all | solution.py:155
  45.3 17.6 %collective-permute-start = (bf16[512,512]{1,0:T(8,128)(2,1)S(1)}, bf16[512,512]{1,0:T(8,128)(2,1)S(1)}, u32[]{:S(2)}, u32[]{:S(2)}) collective-permute-start(bf16[512,512]{1,0:T(8,128)(2,1)S(1)} %bitcast.16), channel_id=1, source_target_pairs={{0,256},{256,512},{512,768},{768,16},{16,272},{272,528},{528,784},... | collective-permute-start | bytes 1572872 | tf_op jit(solution)/shard_map/ppermute | solution.py:80
  48.6 17.1 %collective-permute-start.3 = (bf16[512,512]{1,0:T(8,128)(2,1)S(1)}, bf16[512,512]{1,0:T(8,128)(2,1)S(1)}, u32[]{:S(2)}, u32[]{:S(2)}) collective-permute-start(bf16[512,512]{1,0:T(8,128)(2,1)S(1)} %bitcast.17), channel_id=1, source_target_pairs={{0,784},{256,0},{512,256},{768,512},{16,768},{272,16},{528,272},{7... | collective-permute-start | bytes 1572872 | tf_op jit(solution)/shard_map/ppermute | solution.py:80
  62.9 16.9 %collective-permute-start.1 = (bf16[512,512]{1,0:T(8,128)(2,1)S(1)}, bf16[512,512]{1,0:T(8,128)(2,1)S(1)}, u32[]{:S(2)}, u32[]{:S(2)}) collective-permute-start(bf16[512,512]{1,0:T(8,128)(2,1)S(1)} %collective-permute-done.refs_1_), channel_id=1, source_target_pairs={{0,256},{256,512},{512,768},{768,16},{16,272},{272,528},{528,784},... | collective-permute-start | bytes 1572872 | tf_op jit(solution)/shard_map/ppermute | solution.py:80
  64.9 0.8 copy-start
  65.7 16.8 %collective-permute-start.4 = (bf16[512,512]{1,0:T(8,128)(2,1)S(1)}, bf16[512,512]{1,0:T(8,128)(2,1)S(1)}, u32[]{:S(2)}, u32[]{:S(2)}) collective-permute-start(bf16[512,512]{1,0:T(8,128)(2,1)S(1)} %collective-permute-done.3.refs_2_), channel_id=1, source_target_pairs={{0,784},{256,0},{512,256},{768,512},{16,768},{272,16},{528,272},{7... | collective-permute-start | bytes 1572872 | tf_op jit(solution)/shard_map/ppermute | solution.py:80
  70.3 0.8 copy-start.2
  79.8 16.0 %collective-permute-start.2 = (bf16[512,512]{1,0:T(8,128)(2,1)S(1)}, bf16[512,512]{1,0:T(8,128)(2,1)S(1)}, u32[]{:S(2)}, u32[]{:S(2)}) collective-permute-start(bf16[512,512]{1,0:T(8,128)(2,1)S(1)} %collective-permute-done.1.refs_3_), channel_id=1, source_target_pairs={{0,256},{256,512},{512,768},{768,16},{16,272},{272,528},{528,784},... | collective-permute-start | bytes 1572872 | tf_op jit(solution)/shard_map/ppermute | solution.py:80
  82.5 15.0 %copy-start.6 = (bf16[512,512]{1,0:T(8,128)(2,1)}, bf16[512,512]{1,0:T(8,128)(2,1)S(1)}, u32[]{:S(2)}) copy-start(bf16[512,512]{1,0:T(8,128)(2,1)S(1)} %collective-permute-done.4.refs_4_) | copy-start | bytes 1572868
  82.5 15.0 %collective-permute-start.5 = (bf16[512,512]{1,0:T(8,128)(2,1)S(1)}, bf16[512,512]{1,0:T(8,128)(2,1)S(1)}, u32[]{:S(2)}, u32[]{:S(2)}) collective-permute-start(bf16[512,512]{1,0:T(8,128)(2,1)S(1)} %collective-permute-done.4.refs_4_), channel_id=1, source_target_pairs={{0,784},{256,0},{512,256},{768,512},{16,768},{272,16},{528,272},{7... | collective-permute-start | bytes 1572872 | tf_op jit(solution)/shard_map/ppermute | solution.py:80
  98.2 10.9 %collective-permute-start.6 = (bf16[16,24,2048]{2,1,0:T(8,128)(2,1)S(1)}, bf16[16,24,2048]{2,1,0:T(8,128)(2,1)}, u32[]{:S(2)}, u32[]{:S(2)}) collective-permute-start(bf16[16,24,2048]{2,1,0:T(8,128)(2,1)S(1)} %all-to-all-done.1.own_ref), channel_id=1, source_target_pairs={{0,1},{1,0},{2,3},{3,2},{4,5},{5,4},{6,7},{7,6},{8,9},{9,8},{10,11... | collective-permute-start | bytes 4718600 | tf_op jit(solution)/shard_map/ppermute | solution.py:167
  101.9 12.2 %collective-permute-start.7 = (bf16[512,256]{1,0:T(8,128)(2,1)}, bf16[512,256]{1,0:T(8,128)(2,1)S(1)}, u32[]{:S(2)}, u32[]{:S(2)}) collective-permute-start(bf16[512,256]{1,0:T(8,128)(2,1)} %slice.20), channel_id=1, source_target_pairs={{0,256},{256,512},{512,768},{768,16},{16,272},{272,528},{528,784},... | collective-permute-start | bytes 786440 | tf_op jit(solution)/shard_map/ppermute | solution.py:80
  104.8 11.3 %collective-permute-start.8 = (bf16[512,256]{1,0:T(8,128)(2,1)}, bf16[512,256]{1,0:T(8,128)(2,1)}, u32[]{:S(2)}, u32[]{:S(2)}) collective-permute-start(bf16[512,256]{1,0:T(8,128)(2,1)} %slice.21), channel_id=1, source_target_pairs={{0,784},{256,0},{512,256},{768,512},{16,768},{272,16},{528,272},{7... | collective-permute-start | bytes 786440 | tf_op jit(solution)/shard_map/ppermute | solution.py:80
  109.1 7.0 %copy-start.1 = (bf16[512,512]{1,0:T(8,128)(2,1)S(1)}, bf16[512,512]{1,0:T(8,128)(2,1)}, u32[]{:S(2)}) copy-start(bf16[512,512]{1,0:T(8,128)(2,1)} %copy-done) | copy-start | bytes 1572868
  109.1 7.0 %copy-start.3 = (bf16[512,512]{1,0:T(8,128)(2,1)S(1)}, bf16[512,512]{1,0:T(8,128)(2,1)}, u32[]{:S(2)}) copy-start(bf16[512,512]{1,0:T(8,128)(2,1)} %copy-done.2) | copy-start | bytes 1572868
  109.2 7.0 %copy-start.5 = (bf16[512,512]{1,0:T(8,128)(2,1)S(1)}, bf16[512,512]{1,0:T(8,128)(2,1)}, u32[]{:S(2)}) copy-start(bf16[512,512]{1,0:T(8,128)(2,1)} %copy-done.4) | copy-start | bytes 1572868
  109.2 7.0 %copy-start.7 = (bf16[512,512]{1,0:T(8,128)(2,1)S(1)}, bf16[512,512]{1,0:T(8,128)(2,1)}, u32[]{:S(2)}) copy-start(bf16[512,512]{1,0:T(8,128)(2,1)} %copy-done.6) | copy-start | bytes 1572868
  119.8 8.9 %copy-start.10 = (s32[12,2]{0,1:T(2,128)S(1)}, s32[12,2]{0,1:T(2,128)}, u32[]{:S(2)}) copy-start(s32[12,2]{0,1:T(2,128)} %param.8) | copy-start | bytes 292
  119.8 9.6 %copy-start.11 = (f32[200]{0:T(256)S(1)}, f32[200]{0:T(256)}, u32[]{:S(2)}) copy-start(f32[200]{0:T(256)} %param.10) | copy-start | bytes 2404
  119.8 9.9 %copy-start.12 = (f32[128]{0:T(128)S(1)}, f32[128]{0:T(128)}, u32[]{:S(2)}) copy-start(f32[128]{0:T(128)} %param.11) | copy-start | bytes 1540
  119.8 31.5 %all-to-all-start.2 = ((f32[32,24,256]{2,1,0:T(8,128)}), f32[32,24,256]{2,1,0:T(8,128)S(1)}, u32[]{:S(2)}, u32[]{:S(2)}) async-start(f32[32,24,256]{2,1,0:T(8,128)} %multiply.1), calls=%async_computation.2 | async-start | bytes 1572864 | tf_op jit(solution)/shard_map/all_to_all | solution.py:172
  (1 other events, 0.8 us)

commit v9 on v8

--- a/solution.py
+++ b/solution.py
@@ -9,7 +9,7 @@
 
 NIRREP = 8
 NV = 128
-AXES = ("ylo", "x", "yhi", "zhi", "zlo", "core")
+AXES = ("ylo", "x", "yhi", "za", "zb", "zc", "core")
 SWAP = [(0, 1), (1, 0)]
 
 
@@ -134,25 +134,28 @@
     size = {axis: lax.axis_size(axis) for axis in AXES}
     pairs_local, summed = amplitudes.shape
     slab_rows, out_width = integrals.shape
-    parts = size["zlo"] * size["core"]
+    parts = size["zc"] * size["core"]
     quarter = out_width // parts
-    stripe = size["zhi"] * size["zlo"] * size["core"] * slab_rows
-
-    quarters = spread_quarters(integrals, parts, size["zhi"])
-    rows = lax.all_to_all(quarters, ("zhi", "zlo", "core"), split_axis=0, concat_axis=0, tiled=True)
+    slab = parts * slab_rows
+    stripe = size["za"] * slab
+
+    quarters = spread_quarters(integrals, parts, size["za"])
+    rows = lax.all_to_all(quarters, ("za", "zc", "core"), split_axis=0, concat_axis=0, tiled=True)
 
     pair_index = jnp.arange(summed, dtype=jnp.int32)
     size_here = jnp.where(pair_index < NV * NV, block_sizes[0], block_sizes[1])
     live = (pair_index // NV % NV < size_here) & (pair_index % NV < size_here)
     masked = jnp.where(live[None, :], amplitudes, jnp.zeros((), jnp.bfloat16))
-    blocked = masked.reshape(pairs_local, size["ylo"], size["x"], size["yhi"], stripe)
-    blocked = blocked.transpose(2, 3, 0, 1, 4)
-    blocked = blocked.reshape(size["x"], size["yhi"] * pairs_local, size["ylo"] * stripe)
+    blocked = masked.reshape(
+        pairs_local, size["ylo"], size["x"], size["yhi"], size["za"], size["zb"], slab
+    ).transpose(2, 5, 3, 0, 1, 4, 6)
+    owners = size["x"] * size["zb"]
+    blocked = blocked.reshape(owners, size["yhi"] * pairs_local, size["ylo"] * stripe)
     rows, blocked = lax.optimization_barrier((rows, blocked))
-    groups = size["x"] * size["zlo"]
-    blocked = jnp.broadcast_to(blocked[:, None], (size["x"], size["zlo"]) + blocked.shape[1:])
+    groups = owners * size["zc"]
+    blocked = jnp.broadcast_to(blocked[:, None], (owners, size["zc"]) + blocked.shape[1:])
     blocked = blocked.reshape((groups,) + blocked.shape[2:])
-    own = lax.all_to_all(blocked, ("x", "zlo"), split_axis=0, concat_axis=0, tiled=True)
+    own = lax.all_to_all(blocked, ("x", "zb", "zc"), split_axis=0, concat_axis=0, tiled=True)
     length = size["yhi"] * size["ylo"]
     move = functools.partial(ring_move, size["yhi"], size["ylo"])
     ring = {0: rows.reshape(stripe, quarter)}
@@ -170,9 +173,9 @@
     place = lax.axis_index("yhi") * size["ylo"] + lax.axis_index("ylo")
     partial_value = multiply(lhs, near, far, order, length, place, lax.axis_index("core"), pairs_local)
     pieces = lax.all_to_all(
-        partial_value, ("x", "zlo", "core"), split_axis=0, concat_axis=0, tiled=True
+        partial_value, ("x", "zb", "zc", "core"), split_axis=0, concat_axis=0, tiled=True
     )
-    ladder = jnp.sum(pieces.reshape((size["x"], parts) + pieces.shape[1:]), axis=0)
+    ladder = jnp.sum(pieces.reshape((owners, parts) + pieces.shape[1:]), axis=0)
     ladder = ladder.reshape(parts, 2, pairs_local, quarter // 2)
     ladder = ladder.transpose(2, 0, 1, 3).reshape(pairs_local, out_width)
 
@@ -188,7 +191,7 @@
 
 
 def solution(mesh):
-    fine = Mesh(mesh.devices.reshape(4, 8, 2, 4, 2, 2), AXES)
+    fine = Mesh(mesh.devices.reshape(4, 8, 2, 2, 2, 2, 2), AXES)
     split = P(AXES, None)
     return jax.shard_map(
         local,

time: 154 us -> 148 us (0.961)
  waiting for transfers between devices: 65.3 us -> 55 us
  starting transfers between devices: 65.3 us -> 68.3 us
  Pallas kernels: 8.07 us -> 6.14 us
    ppermute x8, waiting for transfers between devices: 32.6 us -> 9.96 us  [ring_move(): return lax.ppermute(value, ('ylo', 'yhi'), pairs)]
    all_to_all x3, waiting for transfers between devices: 32.7 us -> 45 us  [the longest x1 37.3 us: local(): lax.all_to_all(partial_value, ('x', 'zb', 'zc', 'core'), split_axis=0, co...]
    all_to_all x3, starting transfers between devices: 33.6 us -> 35.7 us  [the longest x1 17.5 us: local(): lax.all_to_all(quarters, ('za', 'zc', 'core'), split_axis=0, concat_axis=...]
    pallas_call x1, Pallas kernels: 2.58 us -> 0.61 us  [assemble(): pl.pallas_call(functools.partial(assemble_kernel, pairs), grid=(groups //...]
  transfers between devices with their start and end apart: 12 -> 12, of which waited for: 8 -> 9; matrix products, arithmetic and copies ran while one was open for 6% -> 7% of each run, Pallas kernels for 2% -> 0%
where the time goes in v9:
time: 148 us; the launch traced here: 145 us
  starting transfers between devices  68.3 us (46%)
  waiting for transfers between devices  55 us (37%)
  local copies, waits for them, and re-layouts  9.98 us (7%)
  Pallas kernels  6.14 us (4%)
  other arithmetic  5.69 us (4%)
    all_to_all x1, waiting for transfers between devices, local(): lax.all_to_all(partial_value, ('x', 'zb', 'zc', 'core'), split_axis=0, co...  37.3 us
    ppermute x8, starting transfers between devices, ring_move(): return lax.ppermute(value, ('ylo', 'yhi'), pairs)  28.6 us
    all_to_all x1, starting transfers between devices, local(): lax.all_to_all(quarters, ('za', 'zc', 'core'), split_axis=0, concat_axis=...  17.5 us
    all_to_all x1, starting transfers between devices, local(): lax.all_to_all(blocked, ('x', 'zb', 'zc'), split_axis=0, concat_axis=0, t...  10.4 us
    ppermute x8, waiting for transfers between devices, ring_move(): return lax.ppermute(value, ('ylo', 'yhi'), pairs)  9.96 us
    all_to_all x1, starting transfers between devices, local(): lax.all_to_all(partial_value, ('x', 'zb', 'zc', 'core'), split_axis=0, co...  7.85 us
    all_to_all x1, waiting for transfers between devices, local(): lax.all_to_all(blocked, ('x', 'zb', 'zc'), split_axis=0, concat_axis=0, t...  5.38 us
    ppermute x1, starting transfers between devices, local(): other = lax.ppermute(own, 'core', SWAP)  4.06 us
  transfers between devices with their start and end apart: 12, of which 9 were waited for; matrix products, arithmetic and copies ran while one was open for 7% of the time, Pallas kernels for 0%

profile of v9, /device:TPU:1, one launch (start us, length us, event | category | flops | bytes accessed | tf_op | source)
XLA Modules:
  0.0 145.5 jit_solution(8001398056056777378)
XLA Ops:
  0.0 1.6 %spread_quarters.1 = bf16[8,32,512]{2,1,0:T(8,128)(2,1)} custom-call(bf16[32,2048]{1,0:T(8,128)(2,1)} %x_ref.1), custom_call_target="tpu_custom_call" | custom-call | bytes 393216 | tf_op jit(solution)/shard_map/spread_quarters/pallas_call | solution.py:31
  1.6 17.5 %all-to-all-start = ((bf16[8,32,512]{2,1,0:T(8,128)(2,1)}), bf16[8,32,512]{2,1,0:T(8,128)(2,1)S(1)}, u32[]{:S(2)}, u32[]{:S(2)}) async-start(bf16[8,32,512]{2,1,0:T(8,128)(2,1)} %spread_quarters.1), calls=%async_computation | async-start | bytes 524288 | tf_op jit(solution)/shard_map/all_to_all | solution.py:143
  19.1 1.4 fusion.15
  21.7 1.4 broadcast_select_fusion
  23.1 1.6 %reshape.106 = bf16[12,4,8,2,2,2,128]{6,5,4,3,2,1,0:T(2,128)(2,1)S(1)} reshape(bf16[12,32768]{1,0:T(8,128)(2,1)S(1)} %broadcast_select_fusion) | data formatting | bytes 1572864 | tf_op jit(solution)/shard_map/reshape | solution.py:149
  25.9 2.4 %all-to-all-done = bf16[8,32,512]{2,1,0:T(8,128)(2,1)S(1)} async-done(((bf16[8,32,512]{2,1,0:T(8,128)(2,1)}), bf16[8,32,512]{2,1,0:T(8,128)(2,1)S(1)}, u32[]{:S(2)}, u32[]{:S(2)}) %all-to-all-start) | async-done | bytes 262176 | tf_op jit(solution)/shard_map/all_to_all | solution.py:143
  28.3 1.3 broadcast_in_dim.72
  29.6 10.4 %all-to-all-start.1 = ((bf16[32,24,1024]{2,1,0:T(8,128)(2,1)}), bf16[32,24,1024]{2,1,0:T(8,128)(2,1)S(1)}, u32[]{:S(2)}, u32[]{:S(2)}) async-start(bf16[32,24,1024]{2,1,0:T(8,128)(2,1)} %bitcast.6), calls=%async_computation.1 | async-start | bytes 3145728 | tf_op jit(solution)/shard_map/all_to_all | solution.py:158
  40.0 3.3 %collective-permute-start = (bf16[256,512]{1,0:T(8,128)(2,1)S(1)}, bf16[256,512]{1,0:T(8,128)(2,1)S(1)}, u32[]{:S(2)}, u32[]{:S(2)}) collective-permute-start(bf16[256,512]{1,0:T(8,128)(2,1)S(1)} %bitcast.16), channel_id=1, source_target_pairs={{0,256},{256,512},{512,768},{768,16},{16,272},{272,528},{528,784},... | collective-permute-start | bytes 786440 | tf_op jit(solution)/shard_map/ppermute | solution.py:80
  43.3 4.5 %collective-permute-start.3 = (bf16[256,512]{1,0:T(8,128)(2,1)S(1)}, bf16[256,512]{1,0:T(8,128)(2,1)S(1)}, u32[]{:S(2)}, u32[]{:S(2)}) collective-permute-start(bf16[256,512]{1,0:T(8,128)(2,1)S(1)} %bitcast.17), channel_id=1, source_target_pairs={{0,784},{256,0},{512,256},{768,512},{16,768},{272,16},{528,272},{7... | collective-permute-start | bytes 786440 | tf_op jit(solution)/shard_map/ppermute | solution.py:80
  47.8 3.9 %collective-permute-done.refs_1_ = bf16[256,512]{1,0:T(8,128)(2,1)S(1)} collective-permute-done((bf16[256,512]{1,0:T(8,128)(2,1)S(1)}, bf16[256,512]{1,0:T(8,128)(2,1)S(1)}, u32[]{:S(2)}, u32[]{:S(2)}) %collective-permute-start) | collective-permute-done | bytes 262176 | tf_op jit(solution)/shard_map/ppermute | solution.py:80
  51.8 1.9 %collective-permute-start.1 = (bf16[256,512]{1,0:T(8,128)(2,1)S(1)}, bf16[256,512]{1,0:T(8,128)(2,1)S(1)}, u32[]{:S(2)}, u32[]{:S(2)}) collective-permute-start(bf16[256,512]{1,0:T(8,128)(2,1)S(1)} %collective-permute-done.refs_1_), channel_id=1, source_target_pairs={{0,256},{256,512},{512,768},{768,16},{16,272},{272,528},{528,784},... | collective-permute-start | bytes 786440 | tf_op jit(solution)/shard_map/ppermute | solution.py:80
  54.4 4.6 %collective-permute-start.4 = (bf16[256,512]{1,0:T(8,128)(2,1)S(1)}, bf16[256,512]{1,0:T(8,128)(2,1)S(1)}, u32[]{:S(2)}, u32[]{:S(2)}) collective-permute-start(bf16[256,512]{1,0:T(8,128)(2,1)S(1)} %collective-permute-done.3.refs_2_), channel_id=1, source_target_pairs={{0,784},{256,0},{512,256},{768,512},{16,768},{272,16},{528,272},{7... | collective-permute-start | bytes 786440 | tf_op jit(solution)/shard_map/ppermute | solution.py:80
  59.7 1.6 %collective-permute-done.1.refs_3_ = bf16[256,512]{1,0:T(8,128)(2,1)S(1)} collective-permute-done((bf16[256,512]{1,0:T(8,128)(2,1)S(1)}, bf16[256,512]{1,0:T(8,128)(2,1)S(1)}, u32[]{:S(2)}, u32[]{:S(2)}) %collective-permute-start.1) | collective-permute-done | bytes 262176 | tf_op jit(solution)/shard_map/ppermute | solution.py:80
  61.3 1.9 %collective-permute-start.2 = (bf16[256,512]{1,0:T(8,128)(2,1)S(1)}, bf16[256,512]{1,0:T(8,128)(2,1)S(1)}, u32[]{:S(2)}, u32[]{:S(2)}) collective-permute-start(bf16[256,512]{1,0:T(8,128)(2,1)S(1)} %collective-permute-done.1.refs_3_), channel_id=1, source_target_pairs={{0,256},{256,512},{512,768},{768,16},{16,272},{272,528},{528,784},... | collective-permute-start | bytes 786440 | tf_op jit(solution)/shard_map/ppermute | solution.py:80
  63.9 4.6 %collective-permute-start.5 = (bf16[256,512]{1,0:T(8,128)(2,1)S(1)}, bf16[256,512]{1,0:T(8,128)(2,1)S(1)}, u32[]{:S(2)}, u32[]{:S(2)}) collective-permute-start(bf16[256,512]{1,0:T(8,128)(2,1)S(1)} %collective-permute-done.4.refs_4_), channel_id=1, source_target_pairs={{0,784},{256,0},{512,256},{768,512},{16,768},{272,16},{528,272},{7... | collective-permute-start | bytes 786440 | tf_op jit(solution)/shard_map/ppermute | solution.py:80
  72.5 5.4 %all-to-all-done.1.own_ref = bf16[32,24,1024]{2,1,0:T(8,128)(2,1)S(1)} async-done(((bf16[32,24,1024]{2,1,0:T(8,128)(2,1)}), bf16[32,24,1024]{2,1,0:T(8,128)(2,1)S(1)}, u32[]{:S(2)}, u32[]{:S(2)}) %all-to-all-start.1) | async-done | bytes 1572896 | tf_op jit(solution)/shard_map/all_to_all | solution.py:158
  77.9 4.1 %collective-permute-start.6 = (bf16[32,24,1024]{2,1,0:T(8,128)(2,1)S(1)}, bf16[32,24,1024]{2,1,0:T(8,128)(2,1)S(1)}, u32[]{:S(2)}, u32[]{:S(2)}) collective-permute-start(bf16[32,24,1024]{2,1,0:T(8,128)(2,1)S(1)} %all-to-all-done.1.own_ref), channel_id=1, source_target_pairs={{0,1},{1,0},{2,3},{3,2},{4,5},{5,4},{6,7},{7,6},{8,9},{9,8},{10,11... | collective-permute-start | bytes 4718600 | tf_op jit(solution)/shard_map/ppermute | solution.py:170
  82.0 3.3 %collective-permute-start.7 = (bf16[256,256]{1,0:T(8,128)(2,1)}, bf16[256,256]{1,0:T(8,128)(2,1)S(1)}, u32[]{:S(2)}, u32[]{:S(2)}) collective-permute-start(bf16[256,256]{1,0:T(8,128)(2,1)} %slice.20), channel_id=1, source_target_pairs={{0,256},{256,512},{512,768},{768,16},{16,272},{272,528},{528,784},... | collective-permute-start | bytes 393224 | tf_op jit(solution)/shard_map/ppermute | solution.py:80
  85.3 4.5 %collective-permute-start.8 = (bf16[256,256]{1,0:T(8,128)(2,1)}, bf16[256,256]{1,0:T(8,128)(2,1)}, u32[]{:S(2)}, u32[]{:S(2)}) collective-permute-start(bf16[256,256]{1,0:T(8,128)(2,1)} %slice.21), channel_id=1, source_target_pairs={{0,784},{256,0},{512,256},{768,512},{16,768},{272,16},{528,272},{7... | collective-permute-start | bytes 393224 | tf_op jit(solution)/shard_map/ppermute | solution.py:80
  90.5 1.4 collective-permute-done.7.refs_7_
  93.0 3.9 %multiply.1 = f32[64,24,256]{2,1,0:T(8,128)} custom-call(s32[1]{0:T(128)} %bitcast.1.place_ref, s32[1]{0:T(128)} %bitcast.2.core_ref, bf16[768,2048]{1,0:T(8,128)(2,1)S(1)} %bitcast.15, bf16[256,512]{1,0:T(8,128)(2,1)S(1)} %bitcast.18, bf16[256,512]{1,0:T(8,128)(2,1)S(1)} %copy-done.5, bf16[256,512]{1,0:T(8,128)(2,1)S(1)} %copy-done.7, ...), custom_call_target="tpu_custom_call" | custom-call | flops 1610612736 | bytes 6815744 | tf_op jit(solution)/shard_map/multiply/pallas_call | solution.py:116
  97.0 7.8 %all-to-all-start.2 = ((f32[64,24,256]{2,1,0:T(8,128)}), f32[64,24,256]{2,1,0:T(8,128)S(1)}, u32[]{:S(2)}, u32[]{:S(2)}) async-start(f32[64,24,256]{2,1,0:T(8,128)} %multiply.1), calls=%async_computation.2 | async-start | bytes 3145728 | tf_op jit(solution)/shard_map/all_to_all | solution.py:175
  107.1 37.3 %all-to-all-done.2 = f32[64,24,256]{2,1,0:T(8,128)S(1)} async-done(((f32[64,24,256]{2,1,0:T(8,128)}), f32[64,24,256]{2,1,0:T(8,128)S(1)}, u32[]{:S(2)}, u32[]{:S(2)}) %all-to-all-start.2) | async-done | bytes 1572896 | tf_op jit(solution)/shard_map/all_to_all | solution.py:175
  (52 shorter events, 13.6 us)
Async XLA Ops:
  1.6 26.6 %all-to-all-start = ((bf16[8,32,512]{2,1,0:T(8,128)(2,1)}), bf16[8,32,512]{2,1,0:T(8,128)(2,1)S(1)}, u32[]{:S(2)}, u32[]{:S(2)}) async-start(bf16[8,32,512]{2,1,0:T(8,128)(2,1)} %spread_quarters.1), calls=%async_computation | async-start | bytes 524288 | tf_op jit(solution)/shard_map/all_to_all | solution.py:143
  29.6 48.3 %all-to-all-start.1 = ((bf16[32,24,1024]{2,1,0:T(8,128)(2,1)}), bf16[32,24,1024]{2,1,0:T(8,128)(2,1)S(1)}, u32[]{:S(2)}, u32[]{:S(2)}) async-start(bf16[32,24,1024]{2,1,0:T(8,128)(2,1)} %bitcast.6), calls=%async_computation.1 | async-start | bytes 3145728 | tf_op jit(solution)/shard_map/all_to_all | solution.py:158
  40.0 11.8 %collective-permute-start = (bf16[256,512]{1,0:T(8,128)(2,1)S(1)}, bf16[256,512]{1,0:T(8,128)(2,1)S(1)}, u32[]{:S(2)}, u32[]{:S(2)}) collective-permute-start(bf16[256,512]{1,0:T(8,128)(2,1)S(1)} %bitcast.16), channel_id=1, source_target_pairs={{0,256},{256,512},{512,768},{768,16},{16,272},{272,528},{528,784},... | collective-permute-start | bytes 786440 | tf_op jit(solution)/shard_map/ppermute | solution.py:80
  43.3 11.1 %collective-permute-start.3 = (bf16[256,512]{1,0:T(8,128)(2,1)S(1)}, bf16[256,512]{1,0:T(8,128)(2,1)S(1)}, u32[]{:S(2)}, u32[]{:S(2)}) collective-permute-start(bf16[256,512]{1,0:T(8,128)(2,1)S(1)} %bitcast.17), channel_id=1, source_target_pairs={{0,784},{256,0},{512,256},{768,512},{16,768},{272,16},{528,272},{7... | collective-permute-start | bytes 786440 | tf_op jit(solution)/shard_map/ppermute | solution.py:80
  51.8 9.5 %collective-permute-start.1 = (bf16[256,512]{1,0:T(8,128)(2,1)S(1)}, bf16[256,512]{1,0:T(8,128)(2,1)S(1)}, u32[]{:S(2)}, u32[]{:S(2)}) collective-permute-start(bf16[256,512]{1,0:T(8,128)(2,1)S(1)} %collective-permute-done.refs_1_), channel_id=1, source_target_pairs={{0,256},{256,512},{512,768},{768,16},{16,272},{272,528},{528,784},... | collective-permute-start | bytes 786440 | tf_op jit(solution)/shard_map/ppermute | solution.py:80
  54.4 9.5 %collective-permute-start.4 = (bf16[256,512]{1,0:T(8,128)(2,1)S(1)}, bf16[256,512]{1,0:T(8,128)(2,1)S(1)}, u32[]{:S(2)}, u32[]{:S(2)}) collective-permute-start(bf16[256,512]{1,0:T(8,128)(2,1)S(1)} %collective-permute-done.3.refs_2_), channel_id=1, source_target_pairs={{0,784},{256,0},{512,256},{768,512},{16,768},{272,16},{528,272},{7... | collective-permute-start | bytes 786440 | tf_op jit(solution)/shard_map/ppermute | solution.py:80
  61.3 8.6 %collective-permute-start.2 = (bf16[256,512]{1,0:T(8,128)(2,1)S(1)}, bf16[256,512]{1,0:T(8,128)(2,1)S(1)}, u32[]{:S(2)}, u32[]{:S(2)}) collective-permute-start(bf16[256,512]{1,0:T(8,128)(2,1)S(1)} %collective-permute-done.1.refs_3_), channel_id=1, source_target_pairs={{0,256},{256,512},{512,768},{768,16},{16,272},{272,528},{528,784},... | collective-permute-start | bytes 786440 | tf_op jit(solution)/shard_map/ppermute | solution.py:80
  63.9 7.9 %collective-permute-start.5 = (bf16[256,512]{1,0:T(8,128)(2,1)S(1)}, bf16[256,512]{1,0:T(8,128)(2,1)S(1)}, u32[]{:S(2)}, u32[]{:S(2)}) collective-permute-start(bf16[256,512]{1,0:T(8,128)(2,1)S(1)} %collective-permute-done.4.refs_4_), channel_id=1, source_target_pairs={{0,784},{256,0},{512,256},{768,512},{16,768},{272,16},{528,272},{7... | collective-permute-start | bytes 786440 | tf_op jit(solution)/shard_map/ppermute | solution.py:80
  68.5 0.7 copy-start.10
  69.9 2.6 %copy-start = (bf16[256,512]{1,0:T(8,128)(2,1)}, bf16[256,512]{1,0:T(8,128)(2,1)S(1)}, u32[]{:S(2)}) copy-start(bf16[256,512]{1,0:T(8,128)(2,1)S(1)} %collective-permute-done.2.refs_5_) | copy-start | bytes 786436
  71.8 0.7 copy-start.2
  77.9 12.0 %collective-permute-start.6 = (bf16[32,24,1024]{2,1,0:T(8,128)(2,1)S(1)}, bf16[32,24,1024]{2,1,0:T(8,128)(2,1)S(1)}, u32[]{:S(2)}, u32[]{:S(2)}) collective-permute-start(bf16[32,24,1024]{2,1,0:T(8,128)(2,1)S(1)} %all-to-all-done.1.own_ref), channel_id=1, source_target_pairs={{0,1},{1,0},{2,3},{3,2},{4,5},{5,4},{6,7},{7,6},{8,9},{9,8},{10,11... | collective-permute-start | bytes 4718600 | tf_op jit(solution)/shard_map/ppermute | solution.py:170
  82.0 10.0 %collective-permute-start.7 = (bf16[256,256]{1,0:T(8,128)(2,1)}, bf16[256,256]{1,0:T(8,128)(2,1)S(1)}, u32[]{:S(2)}, u32[]{:S(2)}) collective-permute-start(bf16[256,256]{1,0:T(8,128)(2,1)} %slice.20), channel_id=1, source_target_pairs={{0,256},{256,512},{512,768},{768,16},{16,272},{272,528},{528,784},... | collective-permute-start | bytes 393224 | tf_op jit(solution)/shard_map/ppermute | solution.py:80
  85.3 7.7 %collective-permute-start.8 = (bf16[256,256]{1,0:T(8,128)(2,1)}, bf16[256,256]{1,0:T(8,128)(2,1)}, u32[]{:S(2)}, u32[]{:S(2)}) collective-permute-start(bf16[256,256]{1,0:T(8,128)(2,1)} %slice.21), channel_id=1, source_target_pairs={{0,784},{256,0},{512,256},{768,512},{16,768},{272,16},{528,272},{7... | collective-permute-start | bytes 393224 | tf_op jit(solution)/shard_map/ppermute | solution.py:80
  89.8 3.2 %copy-start.1 = (bf16[256,512]{1,0:T(8,128)(2,1)S(1)}, bf16[256,512]{1,0:T(8,128)(2,1)}, u32[]{:S(2)}) copy-start(bf16[256,512]{1,0:T(8,128)(2,1)} %copy-done) | copy-start | bytes 786436
  89.8 3.2 %copy-start.3 = (bf16[256,512]{1,0:T(8,128)(2,1)S(1)}, bf16[256,512]{1,0:T(8,128)(2,1)}, u32[]{:S(2)}) copy-start(bf16[256,512]{1,0:T(8,128)(2,1)} %copy-done.2) | copy-start | bytes 786436
  89.8 3.2 %copy-start.5 = (bf16[256,512]{1,0:T(8,128)(2,1)S(1)}, bf16[256,512]{1,0:T(8,128)(2,1)}, u32[]{:S(2)}) copy-start(bf16[256,512]{1,0:T(8,128)(2,1)} %copy-done.4) | copy-start | bytes 786436
  89.8 3.2 %copy-start.7 = (bf16[256,512]{1,0:T(8,128)(2,1)S(1)}, bf16[256,512]{1,0:T(8,128)(2,1)}, u32[]{:S(2)}) copy-start(bf16[256,512]{1,0:T(8,128)(2,1)} %copy-done.6) | copy-start | bytes 786436
  89.8 3.2 %copy-start.9 = (bf16[256,512]{1,0:T(8,128)(2,1)S(1)}, bf16[256,512]{1,0:T(8,128)(2,1)}, u32[]{:S(2)}) copy-start(bf16[256,512]{1,0:T(8,128)(2,1)} %copy-done.8) | copy-start | bytes 786436
  89.9 3.2 %copy-start.11 = (bf16[256,512]{1,0:T(8,128)(2,1)S(1)}, bf16[256,512]{1,0:T(8,128)(2,1)}, u32[]{:S(2)}) copy-start(bf16[256,512]{1,0:T(8,128)(2,1)} %copy-done.10) | copy-start | bytes 786436
  97.0 7.9 %copy-start.12 = (s32[12,2]{0,1:T(2,128)S(1)}, s32[12,2]{0,1:T(2,128)}, u32[]{:S(2)}) copy-start(s32[12,2]{0,1:T(2,128)} %param.8) | copy-start | bytes 292
  97.0 8.6 %copy-start.13 = (f32[200]{0:T(256)S(1)}, f32[200]{0:T(256)}, u32[]{:S(2)}) copy-start(f32[200]{0:T(256)} %param.10) | copy-start | bytes 2404
  97.0 8.9 %copy-start.14 = (f32[128]{0:T(128)S(1)}, f32[128]{0:T(128)}, u32[]{:S(2)}) copy-start(f32[128]{0:T(128)} %param.11) | copy-start | bytes 1540
  97.0 47.4 %all-to-all-start.2 = ((f32[64,24,256]{2,1,0:T(8,128)}), f32[64,24,256]{2,1,0:T(8,128)S(1)}, u32[]{:S(2)}, u32[]{:S(2)}) async-start(f32[64,24,256]{2,1,0:T(8,128)} %multiply.1), calls=%async_computation.2 | async-start | bytes 3145728 | tf_op jit(solution)/shard_map/all_to_all | solution.py:175
  (3 other events, 2.1 us)
